TPU v7x, 256 devices: a whole 4x4x8 slice. The times are simulated.
256 devices in a mesh: vp: 64 (over x, z, core), red: 4 (over y).
Axes of the slice: x: 4, y: 4, z: 8, core: 2. Of those that a mesh axis runs over, the one named last changes fastest.
Arguments:
- virt_sizes: int32 [8], replicated, may hold values from 1 to 320, as said below
- occ_sizes: int32 [8], replicated, may hold values from 1 to 40, as said below
- pair_ids: int32 [1536], replicated, may hold values from 0 to 39999
- amplitudes: bfloat16 [1536, 6400], P('vp', 'red'), may hold values from -6 to 6
- integrals: bfloat16 [102400, 6400], P('vp', 'red'), may hold values from -0.21875 to 0.21875
Outputs:
- ladder: bfloat16 [1536, 102400], P('red', 'vp')
Inputs may be any that keep to these rules, and one draw needn't show every extreme that they name: `virt_sizes`: each entry lies in 1..320, the entries sum to 1600, and one entry equals 320. `occ_sizes`: each entry lies in 1..40, the entries sum to 200, and one entry equals 40.
All inputs are finite; a program needn't handle non-finite values.
Results may differ from a plain program's by a relative error of at most 0.013.
Values may be sent and summed in bfloat16 or wider, within the bound.
No kernel may reach another device: no remote copies, remote signals or barrier semaphores. Data moves between devices by JAX's collectives and lax.ppermute only.
A program may use at most 64 MiB of HBM per device.

v0:
```python
import jax
import jax.numpy as jnp
from jax import lax
from jax.sharding import PartitionSpec as P

NOCC = 200


def irrep_of(positions, sizes):
    bounds = jnp.cumsum(sizes)[:7]
    return jnp.sum((positions[:, None] >= bounds[None, :]).astype(jnp.int32), axis=1)


def pair_irreps(ids, occ_sizes):
    return jnp.bitwise_xor(irrep_of(ids // NOCC, occ_sizes), irrep_of(ids % NOCC, occ_sizes))


def shards(virt_sizes, occ_sizes, pair_ids, amplitudes, integrals):
    width = integrals.shape[0]
    orbital = irrep_of(jnp.arange(width, dtype=jnp.int32), virt_sizes)
    row_orbital = jnp.reshape(lax.axis_index("vp") * (width // lax.axis_size("vp")), (1,))
    col_orbital = jnp.reshape(lax.axis_index("red") * (width // lax.axis_size("red")), (1,))
    row_irrep = irrep_of(row_orbital, virt_sizes)[0]
    col_irrep = irrep_of(col_orbital, virt_sizes)[0]
    row_pair = jnp.bitwise_xor(row_irrep, orbital)
    col_pair = jnp.bitwise_xor(col_irrep, orbital)
    masked = jnp.where(row_pair[:, None] == col_pair[None, :], integrals, jnp.zeros_like(integrals))
    partial_terms = lax.dot_general(
        lax.all_gather(amplitudes, "vp", axis=0, tiled=True),
        masked,
        (((1,), (1,)), ((), ())),
        preferred_element_type=jnp.float32,
    )
    summed = lax.psum_scatter(
        partial_terms.astype(jnp.bfloat16), "red", scatter_dimension=0, tiled=True
    ).astype(jnp.float32)
    portion_rows = summed.shape[0]
    local_ids = lax.dynamic_slice_in_dim(
        pair_ids, lax.axis_index("red") * portion_rows, portion_rows, 0
    )
    occ_pair = pair_irreps(local_ids, occ_sizes)
    keep = jnp.bitwise_xor(occ_pair[:, None], row_pair[None, :]) == 0
    return jnp.where(keep, summed, jnp.zeros_like(summed)).astype(jnp.bfloat16)


def solution(mesh):
    in_specs = (P(), P(), P(), P("vp", "red"), P("vp", "red"))
    out_specs = P("red", "vp")
    return jax.shard_map(shards, mesh=mesh, in_specs=in_specs, out_specs=out_specs, check_vma=False)
```

profile of v0, /device:TPU:1, one launch (start us, length us, event | category | flops | bytes accessed | tf_op | source)
XLA Modules:
  0.0 180.6 jit_solution(10942649333459290175)
XLA Ops:
  6.5 0.0 all-gather.2.cloned.1.call-start
  6.5 0.7 all-gather.2.cloned.1.call-update
  7.3 0.0 reduce-scatter.4.cloned.1.call-start
  7.3 0.8 reduce-window.9
  8.1 0.7 fusion.5
  8.8 0.1 convert_reduce_fusion
  8.9 1.3 broadcast_xor_fusion.1
  10.2 83.9 %all-gather.2.cloned.1.call-done = bf16[1536,1600]{1,0:T(8,128)(2,1)} async-done(((bf16[24,1600]{1,0:T(8,128)(2,1)}), bf16[1536,1600]{1,0:T(8,128)(2,1)}) %all-gather.2.cloned.1.call-update) | async-done | bytes 4915216 | tf_op jit(solution)/shard_map/all_gather | solution.py:29
  94.1 14.3 %fusion = bf16[1536,1600]{0,1:T(8,128)(2,1)} fusion(bf16[1536,1600]{1,0:T(8,128)(2,1)} %all-gather.2.cloned.1.call-done, bf16[1600,1600]{1,0:T(8,128)(2,1)} %param.9, s32[1600]{0:T(1024)S(1)} %get-tuple-element.12, s32[1600]{0:T(1024)S(1)} %get-tuple-element.11), kind=kOutput, calls=%fused_computation.2 | convolution fusion | flops 7871897600 | bytes 14963200 | tf_op jit(solution)/shard_map/dot_general | solution.py:28
  108.4 7.4 %copy.6 = bf16[1536,1600]{1,0:T(8,128)(2,1)} copy(bf16[1536,1600]{0,1:T(8,128)(2,1)} %fusion) | data formatting | bytes 9830400
  115.8 0.0 copy-start
  115.8 0.0 reduce-scatter.4.cloned.1.call-update
  115.9 0.6 copy-done
  116.5 0.2 reduce-window.6
  116.7 0.8 add_select_fusion.1
  117.5 0.1 convert_reduce_fusion.1
  117.6 52.2 %reduce-scatter.4.cloned.1.call-done = bf16[384,1600]{1,0:T(8,128)(2,1)} async-done(((bf16[1536,1600]{1,0:T(8,128)(2,1)}), bf16[384,1600]{1,0:T(8,128)(2,1)}) %reduce-scatter.4.cloned.1.call-update) | async-done | bytes 1228816
  169.7 2.5 %copy.7 = bf16[384,1600]{0,1:T(8,128)(2,1)S(1)} copy(bf16[384,1600]{1,0:T(8,128)(2,1)} %reduce-scatter.4.cloned.1.call-done) | data formatting | bytes 2457600
  172.3 1.5 select_convert_fusion
  (2 shorter events, 0.0 us)
Async XLA Ops:
  6.5 87.6 %all-gather.2.cloned.1.call-start = ((), (), s32[]{:S(2)}) async-start(), calls=%async_computation.1 | async-start | bytes 5191680 | tf_op jit(solution)/shard_map/all_gather | solution.py:29
  7.3 162.5 %reduce-scatter.4.cloned.1.call-start = ((), (), s32[]{:S(2)}) async-start(), calls=%async_computation.2 | async-start | bytes 6389760
  115.8 0.7 copy-start
Sparse Core Ops, SparseCore 0:
  10.1 83.9 all-gather.1
  116.0 53.7 reduce-scatter.3
where the time goes:
time: 181 us
  waiting for transfers between devices  137 us (76%)
  matrix products  14.3 us (8%)
  between operations  13.4 us (7%)
  local copies, waits for them, and re-layouts  10.6 us (6%)
  other arithmetic  5.39 us (3%)
    all_gather x1, waiting for transfers between devices, shards(): lax.all_gather(amplitudes, 'vp', axis=0, tiled=True)  83.9 us
    unnamed x3, waiting for transfers between devices  52.9 us
    dot_general x1, matrix products, shards(): lax.dot_general(lax.all_gather(amplitudes, 'vp', axis=0, tiled=True), mas...  14.3 us
    unnamed x4, local copies, waits for them, and re-layouts  10.6 us
  transfers between devices with their start and end apart: 2, of which 2 were waited for; matrix products, arithmetic and copies ran while one was open for 2% of the time, Pallas kernels for 0%

commit v1 on v0

v1 whole, which is shorter than its diff:
```python
import functools

import jax
import jax.numpy as jnp
from jax import lax
from jax.experimental import pallas as pl
from jax.experimental.pallas import tpu as pltpu
from jax.sharding import Mesh, PartitionSpec as P

VIRT = 1600
NOCC = 200
PAIRS = 1536
BMAX = 320
NX, NZ, NC, NY = 4, 8, 2, 4
AWIDTH = VIRT // (NX * NZ * NC)
CWIDTH = VIRT // NY
ROWS = PAIRS // (NX * NZ * NC)
HALF = NZ * ROWS
PORTION = NC * HALF
LANES = 384
MAIN = 256
WINDOW = 336
SPAN = 512
LAST = 1152
F32, BF16, I32 = jnp.float32, jnp.bfloat16, jnp.int32
SMEM = pl.BlockSpec(memory_space=pltpu.SMEM)
VMEM = pl.BlockSpec(memory_space=pltpu.VMEM)


def offset_of(sizes_ref, group):
    total = jnp.int32(0)
    for g in range(7):
        total += jnp.where(group > g, sizes_ref[g], 0)
    return total


def irrep_of(position, sizes_ref):
    bound, irrep = jnp.int32(0), jnp.zeros_like(position)
    for g in range(7):
        bound += sizes_ref[g]
        irrep += (position >= bound).astype(I32)
    return irrep


def pair_sym(ids, sizes_ref):
    first = lax.shift_right_logical(ids * 5243, 20)
    second = ids - first * NOCC
    return jnp.bitwise_xor(irrep_of(first, sizes_ref), irrep_of(second, sizes_ref))


def vp_index():
    return (lax.axis_index("x") * NZ + lax.axis_index("z")) * NC + lax.axis_index("c")


def row_irrep(virt_ref):
    return irrep_of(vp_index() * AWIDTH, virt_ref)


def col_irrep(virt_ref):
    return irrep_of(lax.axis_index("y") * CWIDTH, virt_ref)


def block_start(offset):
    return jnp.minimum(lax.div(offset, 16) * 16, VIRT - WINDOW)


def load_span(source_ref, span_ref, rows, offset):
    @pl.when(offset < LAST)
    def _():
        start = pl.multiple_of(lax.div(offset, 128) * 128, 128)
        span_ref[...] = source_ref[rows, pl.ds(start, SPAN)]

    @pl.when(offset >= LAST)
    def _():
        span_ref[:, :384] = source_ref[rows, LAST:1536]
        span_ref[:, 384:448] = source_ref[rows, 1536:1600]
        span_ref[:, 448:] = jnp.zeros((span_ref.shape[0], 64), span_ref.dtype)

    shift = jnp.where(offset < LAST, lax.rem(offset, 128), offset - LAST)
    return lax.rem(SPAN - shift, SPAN)


def pack_kernel(virt_ref, occ_ref, ids_ref, t_ref, out_ref, wide, span):
    wide[...] = t_ref[...].astype(F32)
    hc = col_irrep(virt_ref)
    base = vp_index() * ROWS
    row = lax.broadcasted_iota(I32, (ROWS, LANES), 0)
    lane = lax.broadcasted_iota(I32, (ROWS, LANES), 1)
    sym = jnp.zeros((ROWS, LANES), I32)
    for r in range(ROWS):
        sym = jnp.where(row == r, pair_sym(ids_ref[base + r], occ_ref), sym)
    packed = jnp.where(lane >= BMAX, sym.astype(F32), 0.0)
    for s in range(8):
        group = jnp.bitwise_xor(hc, s)
        turn = load_span(wide, span, slice(None), offset_of(virt_ref, group))
        block = pltpu.roll(span[...], turn, 1)[:, :LANES]
        packed = jnp.where((sym == s) & (lane < virt_ref[group]), block, packed)
    out_ref[...] = jnp.concatenate([packed] * NZ, axis=0).astype(BF16)


def blocks_kernel(virt_ref, occ_ref, ids_ref, v_ref, after_ref, out_ref, order_ref, sym_ref, span):
    del after_ref
    ra, hc = row_irrep(virt_ref), col_irrep(virt_ref)
    lane = lax.broadcasted_iota(I32, (WINDOW, LANES), 1)
    for s in range(8):
        group = jnp.bitwise_xor(hc, s)
        start = block_start(offset_of(virt_ref, jnp.bitwise_xor(ra, s)))
        rows = pl.ds(pl.multiple_of(start, 16), WINDOW)
        turn = load_span(v_ref, span, rows, offset_of(virt_ref, group))
        block = pltpu.roll(span[...].astype(F32), turn, 1)[:, :LANES]
        block = jnp.where(lane < virt_ref[group], block, 0.0).astype(BF16)
        out_ref[:, s * MAIN:(s + 1) * MAIN] = block[:, :MAIN]
        out_ref[:, 8 * MAIN + s * 128:8 * MAIN + (s + 1) * 128] = block[:, MAIN:]
    column = lax.broadcasted_iota(I32, (PORTION, PORTION), 0)
    target = lax.broadcasted_iota(I32, (PORTION, PORTION), 1)
    other = (column >= HALF).astype(I32)
    within = column - other * HALF
    z = lax.shift_right_logical(within * 2731, 16)
    core = jnp.bitwise_xor(lax.axis_index("c"), other)
    order_ref[...] = ((z * NC + core) * ROWS + (within - z * ROWS) == target).astype(F32).astype(BF16)
    ids = ids_ref[pl.ds(lax.axis_index("y"), 1), :]
    sym_ref[...] = jnp.broadcast_to(pair_sym(ids, occ_ref), (8, PORTION))


def terms_kernel(virt_ref, own_ref, other_ref, v_ref, o0, o1, o2, o3, stack, total):
    hc = col_irrep(virt_ref)
    x, y = lax.axis_index("x"), lax.axis_index("y")
    for r, out_ref in ((2, o2), (1, o1), (3, o3), (0, o0)):
        portion = lax.rem(y + r, NY)
        rows = pl.ds(pl.multiple_of(lax.rem(x - portion + NX, NX) * HALF, HALF), HALF)
        t = jnp.concatenate([own_ref[rows, :], other_ref[rows, :]], axis=0)
        sym = jnp.broadcast_to(t[:, BMAX:BMAX + 1].astype(F32), (PORTION, MAIN))
        for s in range(8):
            keep = (sym == s).astype(F32).astype(BF16)
            stack[:, s * MAIN:(s + 1) * MAIN] = t[:, :MAIN] * keep
        nt = (((1,), (1,)), ((), ()))
        total[...] = lax.dot_general(v_ref[:, :8 * MAIN], stack[...], nt, preferred_element_type=F32)
        for s in range(8):

            @pl.when(virt_ref[jnp.bitwise_xor(hc, s)] > MAIN)
            def _():
                keep = (sym[:, :128] == s).astype(F32).astype(BF16)
                total[...] += lax.dot_general(
                    v_ref[:, 8 * MAIN + s * 128:8 * MAIN + (s + 1) * 128], t[:, MAIN:] * keep, nt,
                    preferred_element_type=F32)

        out_ref[...] = total[...].astype(BF16)


def place_kernel(virt_ref, a_ref, b_ref, c_ref, d_ref, order_ref, sym_ref, out_ref):
    ra = row_irrep(virt_ref)
    total = a_ref[...].astype(F32) + b_ref[...].astype(F32) + c_ref[...].astype(F32) + d_ref[...].astype(F32)
    total = jnp.dot(total.astype(BF16), order_ref[...], preferred_element_type=F32)
    out_ref[...] = jnp.zeros_like(out_ref)
    row = lax.broadcasted_iota(I32, (WINDOW, PORTION), 0)
    sym = jnp.broadcast_to(sym_ref[:1, :], (WINDOW, PORTION))
    for s in range(8):
        group = jnp.bitwise_xor(ra, s)
        offset = offset_of(virt_ref, group)
        start = block_start(offset)
        rows = pl.ds(pl.multiple_of(start, 16), WINDOW)
        first = offset - start
        keep = (row >= first) & (row < first + virt_ref[group])
        value = jnp.where(sym == s, total, 0.0)
        out_ref[rows, :] = jnp.where(keep, value, out_ref[rows, :].astype(F32)).astype(BF16)


def shift(value, axis, size, by):
    return lax.ppermute(value, axis, [(i, (i + by) % size) for i in range(size)])


def call(kernel, specs, out, scratch=(), flops=0, moved=0):
    return pl.pallas_call(
        kernel,
        in_specs=specs,
        out_specs=jax.tree.map(lambda _: VMEM, out),
        out_shape=out,
        scratch_shapes=list(scratch),
        compiler_params=pltpu.CompilerParams(vmem_limit_bytes=48 * 2**20),
        cost_estimate=pl.CostEstimate(flops=flops, bytes_accessed=moved, transcendentals=0),
    )


def shards(virt_sizes, occ_sizes, pair_ids, amplitudes, integrals):
    shape = jax.ShapeDtypeStruct
    packed = call(
        pack_kernel, [SMEM, SMEM, SMEM, VMEM], shape((HALF, LANES), BF16),
        [pltpu.VMEM((ROWS, VIRT), F32), pltpu.VMEM((ROWS, SPAN), F32)], moved=300000,
    )(virt_sizes, occ_sizes, pair_ids, amplitudes)
    mine = lax.all_to_all(packed, "z", 0, 0, tiled=True)
    across = [shift(mine, "x", NX, k) for k in (2, 1, 3)]
    blocks, order, sym = call(
        blocks_kernel, [SMEM, SMEM, VMEM, VMEM, VMEM],
        (shape((WINDOW, 8 * LANES), BF16), shape((PORTION, PORTION), BF16), shape((8, PORTION), I32)),
        [pltpu.VMEM((WINDOW, SPAN), BF16)], moved=12000000,
    )(virt_sizes, occ_sizes, pair_ids.reshape(NY, PORTION), integrals, mine[:16, :128])
    own = jnp.concatenate([mine, across[1], across[0], across[2]], axis=0)
    other = shift(own, "c", NC, 1)
    tile = shape((WINDOW, PORTION), BF16)
    terms = call(
        terms_kernel, [SMEM, VMEM, VMEM, VMEM], (tile,) * NY,
        [pltpu.VMEM((PORTION, 8 * MAIN), BF16), pltpu.VMEM((WINDOW, PORTION), F32)],
        flops=2 * PAIRS * WINDOW * 8 * MAIN, moved=4500000,
    )(virt_sizes, own, other, blocks)
    far = [shift(terms[r], "y", NY, r) for r in (2, 1, 3)]
    out = call(
        place_kernel, [SMEM] + [VMEM] * 6, shape((VIRT, PORTION), BF16), moved=2600000,
    )(virt_sizes, terms[0], *far, order, sym)
    return out.T


def solution(mesh):
    grid = Mesh(mesh.devices.reshape(NX, NZ, NC, NY), ("x", "z", "c", "y"))
    vp = ("x", "z", "c")
    in_specs = (P(), P(), P(), P(vp, "y"), P(vp, "y"))
    return jax.shard_map(shards, mesh=grid, in_specs=in_specs, out_specs=P("y", vp), check_vma=False)
```

time: 181 us -> 65 us (0.36)
  waiting for transfers between devices: 137 us -> 15.6 us
  blocking collectives: 0 us -> 16.7 us
  Pallas kernels: 0 us -> 16.1 us
  matrix products: 14.3 us -> 0 us
  between operations: 13.4 us -> 0.06 us
  starting transfers between devices: 0.04 us -> 13.2 us
  local copies, waits for them, and re-layouts: 10.6 us -> 2.91 us
  other arithmetic: 5.39 us -> 0.06 us
    all_gather x1 -> x0, waiting for transfers between devices: 83.9 us -> none  [shards(): lax.all_gather(amplitudes, 'vp', axis=0, tiled=True)]
    unnamed x3 -> x0, waiting for transfers between devices: 52.9 us -> none
    all_to_all x0 -> x1, blocking collectives: none -> 16.7 us  [shards(): mine = lax.all_to_all(packed, 'z', 0, 0, tiled=True)]
    pallas_call x0 -> x4, Pallas kernels: none -> 16.1 us  [the longest x1 6.3 us: shards(): call(terms_kernel, [SMEM, VMEM, VMEM, VMEM], (tile,) * NY, [pltpu.VMEM((P...]
    ppermute x0 -> x7, waiting for transfers between devices: none -> 15.6 us  [shift(): lax.ppermute(value, axis, [(i, (i + by) % size) for i in range(size)])]
    dot_general x1 -> x0, matrix products: 14.3 us -> none  [shards(): lax.dot_general(lax.all_gather(amplitudes, 'vp', axis=0, tiled=True), mas...]
    ppermute x0 -> x7, starting transfers between devices: none -> 13.2 us  [shift(): lax.ppermute(value, axis, [(i, (i + by) % size) for i in range(size)])]
    unnamed x4 -> x14, local copies, waits for them, and re-layouts: 10.6 us -> 2.9 us
  transfers between devices with their start and end apart: 2 -> 7, of which waited for: 2 -> 5; matrix products, arithmetic and copies ran while one was open for 2% -> 0% of each run, Pallas kernels for 0% -> 8%
where the time goes in v1:
time: 65 us; the launch traced here: 64.7 us
  blocking collectives  16.7 us (26%)
  Pallas kernels  16.1 us (25%)
  waiting for transfers between devices  15.6 us (24%)
  starting transfers between devices  13.2 us (20%)
  local copies, waits for them, and re-layouts  2.91 us (4%)
    all_to_all x1, blocking collectives, shards(): mine = lax.all_to_all(packed, 'z', 0, 0, tiled=True)  16.7 us
    ppermute x7, waiting for transfers between devices, shift(): lax.ppermute(value, axis, [(i, (i + by) % size) for i in range(size)])  15.6 us
    ppermute x7, starting transfers between devices, shift(): lax.ppermute(value, axis, [(i, (i + by) % size) for i in range(size)])  13.2 us
    pallas_call x1, Pallas kernels, shards(): call(terms_kernel, [SMEM, VMEM, VMEM, VMEM], (tile,) * NY, [pltpu.VMEM((P...  6.3 us
    pallas_call x1, Pallas kernels, shards(): call(blocks_kernel, [SMEM, SMEM, VMEM, VMEM, VMEM], (shape((WINDOW, 8 * L...  4.94 us
    pallas_call x1, Pallas kernels, shards(): call(place_kernel, [SMEM] + [VMEM] * 6, shape((VIRT, PORTION), BF16), mov...  3.03 us
    unnamed x14, local copies, waits for them, and re-layouts  2.9 us
    pallas_call x1, Pallas kernels, shards(): call(pack_kernel, [SMEM, SMEM, SMEM, VMEM], shape((HALF, LANES), BF16), [...  1.85 us
  transfers between devices with their start and end apart: 7, of which 5 were waited for; matrix products, arithmetic and copies ran while one was open for 0% of the time, Pallas kernels for 8%

profile of v1, /device:TPU:1, one launch (start us, length us, event | category | flops | bytes accessed | tf_op | source)
XLA Modules:
  0.0 64.7 jit_solution(15120588168412953525)
XLA Ops:
  0.0 0.0 copy-start
  0.0 0.9 %copy-done = bf16[24,1600]{1,0:T(8,128)(2,1)S(1)} copy-done((bf16[24,1600]{1,0:T(8,128)(2,1)S(1)}, bf16[24,1600]{1,0:T(8,128)(2,1)}, u32[]{:S(2)}) %copy-start) | copy-done | bytes 76824
  0.9 0.0 copy-start.1
  0.9 0.7 %copy-done.1 = s32[1536]{0:T(1024)S(1)} copy-done((s32[1536]{0:T(1024)S(1)}, s32[1536]{0:T(1024)}, u32[]{:S(2)}) %copy-start.1) | copy-done | bytes 6168
  1.6 0.0 copy-start.3
  1.6 0.7 %copy-done.3 = s32[8]{0:T(128)S(1)} copy-done((s32[8]{0:T(128)S(1)}, s32[8]{0:T(128)}, u32[]{:S(2)}) %copy-start.3) | copy-done | bytes 56
  2.2 0.0 copy-start.5
  2.2 0.7 %copy-done.5 = s32[8]{0:T(128)S(1)} copy-done((s32[8]{0:T(128)S(1)}, s32[8]{0:T(128)}, u32[]{:S(2)}) %copy-start.5) | copy-done | bytes 56
  2.9 0.0 copy-start.2
  2.9 0.0 copy-start.4
  2.9 0.0 copy-start.6
  2.9 1.9 %shard_map.55 = bf16[192,384]{1,0:T(8,128)(2,1)S(1)} custom-call(s32[8]{0:T(128)S(1)} %copy-done.3, s32[8]{0:T(128)S(1)} %copy-done.5, s32[1536]{0:T(1024)S(1)} %copy-done.1, bf16[24,1600]{1,0:T(8,128)(2,1)S(1)} %copy-done), custom_call_target="tpu_custom_call" | custom-call | bytes 300000 | tf_op jit(solution)/shard_map/pallas_call | solution.py:186
  4.8 16.7 %all_to_all.12 = bf16[8,24,384]{2,1,0:T(8,128)(2,1)S(1)} all-to-all(bf16[8,24,384]{2,1,0:T(8,128)(2,1)S(1)} %bitcast.3), channel_id=1, replica_groups=mesh['x'=4,'z'=8,'c'=2,'y'=4] {'z'}, dimensions={0} | all-to-all | bytes 294912 | tf_op jit(solution)/shard_map/all_to_all | solution.py:190
  21.5 2.5 %collective-permute-start.2 = (bf16[192,384]{1,0:T(8,128)(2,1)S(1)}, bf16[192,384]{1,0:T(8,128)(2,1)S(1)}, u32[]{:S(2)}, u32[]{:S(2)}) collective-permute-start(bf16[192,384]{1,0:T(8,128)(2,1)S(1)} %bitcast.4), channel_id=1, source_target_pairs={{0,192},{64,0},{128,64},{192,128},{1,193},{65,1},{129,65},{193,129... | collective-permute-start | bytes 442376 | tf_op jit(solution)/shard_map/ppermute | solution.py:169
  24.0 0.5 collective-permute-start.1
  24.5 0.6 collective-permute-start
  25.1 2.3 %collective-permute-done.2 = bf16[192,384]{1,0:T(8,128)(2,1)S(1)} collective-permute-done((bf16[192,384]{1,0:T(8,128)(2,1)S(1)}, bf16[192,384]{1,0:T(8,128)(2,1)S(1)}, u32[]{:S(2)}, u32[]{:S(2)}) %collective-permute-start.2) | collective-permute-done | bytes 147488 | tf_op jit(solution)/shard_map/ppermute | solution.py:169
  27.4 2.2 %collective-permute-done.1 = bf16[192,384]{1,0:T(8,128)(2,1)S(1)} collective-permute-done((bf16[192,384]{1,0:T(8,128)(2,1)S(1)}, bf16[192,384]{1,0:T(8,128)(2,1)S(1)}, u32[]{:S(2)}, u32[]{:S(2)}) %collective-permute-start.1) | collective-permute-done | bytes 147488 | tf_op jit(solution)/shard_map/ppermute | solution.py:169
  29.6 1.5 %collective-permute-done = bf16[192,384]{1,0:T(8,128)(2,1)S(1)} collective-permute-done((bf16[192,384]{1,0:T(8,128)(2,1)S(1)}, bf16[192,384]{1,0:T(8,128)(2,1)S(1)}, u32[]{:S(2)}, u32[]{:S(2)}) %collective-permute-start) | collective-permute-done | bytes 147488 | tf_op jit(solution)/shard_map/ppermute | solution.py:169
  31.1 0.1 pad_maximum_fusion.own_ref
  31.1 4.0 %collective-permute-start.3 = (bf16[768,384]{1,0:T(8,128)(2,1)S(1)}, bf16[768,384]{1,0:T(8,128)(2,1)S(1)}, u32[]{:S(2)}, u32[]{:S(2)}) collective-permute-start(bf16[768,384]{1,0:T(8,128)(2,1)S(1)} %pad_maximum_fusion.own_ref), channel_id=1, source_target_pairs={{0,4},{4,0},{1,5},{5,1},{2,6},{6,2},{3,7},{7,3},{8,12},{12,8},{9,1... | collective-permute-start | bytes 1769480 | tf_op jit(solution)/shard_map/ppermute | solution.py:169
  35.1 0.0 copy-done.2
  35.1 0.0 copy-done.4
  35.1 0.0 copy-done.6
  35.1 4.9 %shard_map.56 = (bf16[336,3072]{1,0:T(8,128)(2,1)S(1)}, bf16[384,384]{1,0:T(8,128)(2,1)S(1)}, s32[8,384]{1,0:T(8,128)S(1)}) custom-call(s32[8]{0:T(128)S(1)} %copy-done.4, s32[8]{0:T(128)S(1)} %copy-done.6, s32[4,384]{1,0:T(4,128)S(1)} %reshape.5.ids_ref, bf16[1600,1600]{1,0:T(8,128)(2,1)} %v_ref.1, bf16[16,128]{1,0:T(8,128)(2,1)S(1)} %slice.4.after_ref), custom_call_target="tpu_custom_call" | custom-call | bytes 12000000 | tf_op jit(solution)/shard_map/pallas_call | solution.py:192
  40.1 0.0 collective-permute-done.3.other_ref
  40.1 6.3 %shard_map.57 = (bf16[336,384]{1,0:T(8,128)(2,1)S(1)}, bf16[336,384]{1,0:T(8,128)(2,1)S(1)}, bf16[336,384]{1,0:T(8,128)(2,1)S(1)}, bf16[336,384]{1,0:T(8,128)(2,1)S(1)}) custom-call(s32[8]{0:T(128)S(1)} %copy-done.4, bf16[768,384]{1,0:T(8,128)(2,1)S(1)} %pad_maximum_fusion.own_ref, bf16[768,384]{1,0:T(8,128)(2,1)S(1)} %collective-permute-done.3.other_ref, ...), custom_call_target="tpu_custom_call" | custom-call | flops 2113929216 | bytes 4500000 | tf_op jit(solution)/shard_map/pallas_call | solution.py:200
  46.4 3.0 %collective-permute-start.4 = (bf16[336,384]{1,0:T(8,128)(2,1)S(1)}, bf16[336,384]{1,0:T(8,128)(2,1)S(1)}, u32[]{:S(2)}, u32[]{:S(2)}) collective-permute-start(bf16[336,384]{1,0:T(8,128)(2,1)S(1)} %get-tuple-element.14), channel_id=1, source_target_pairs={{0,2},{1,3},{2,0},{3,1},{4,6},{5,7},{6,4},{7,5},{8,10},{9,11},{10,... | collective-permute-start | bytes 774152 | tf_op jit(solution)/shard_map/ppermute | solution.py:169
  49.4 0.4 collective-permute-start.5
  49.8 2.3 %collective-permute-start.6 = (bf16[336,384]{1,0:T(8,128)(2,1)S(1)}, bf16[336,384]{1,0:T(8,128)(2,1)S(1)}, u32[]{:S(2)}, u32[]{:S(2)}) collective-permute-start(bf16[336,384]{1,0:T(8,128)(2,1)S(1)} %get-tuple-element.16), channel_id=1, source_target_pairs={{0,3},{1,0},{2,1},{3,2},{4,7},{5,4},{6,5},{7,6},{8,11},{9,8},{10,9... | collective-permute-start | bytes 774152 | tf_op jit(solution)/shard_map/ppermute | solution.py:169
  52.0 3.8 %collective-permute-done.4.b_ref = bf16[336,384]{1,0:T(8,128)(2,1)S(1)} collective-permute-done((bf16[336,384]{1,0:T(8,128)(2,1)S(1)}, bf16[336,384]{1,0:T(8,128)(2,1)S(1)}, u32[]{:S(2)}, u32[]{:S(2)}) %collective-permute-start.4) | collective-permute-done | bytes 258080 | tf_op jit(solution)/shard_map/ppermute | solution.py:169
  55.8 5.8 %collective-permute-done.5.c_ref = bf16[336,384]{1,0:T(8,128)(2,1)S(1)} collective-permute-done((bf16[336,384]{1,0:T(8,128)(2,1)S(1)}, bf16[336,384]{1,0:T(8,128)(2,1)S(1)}, u32[]{:S(2)}, u32[]{:S(2)}) %collective-permute-start.5) | collective-permute-done | bytes 258080 | tf_op jit(solution)/shard_map/ppermute | solution.py:169
  61.7 0.0 collective-permute-done.6.d_ref
  61.7 3.0 %shard_map.58 = bf16[1600,384]{1,0:T(8,128)(2,1)} custom-call(s32[8]{0:T(128)S(1)} %copy-done.4, bf16[336,384]{1,0:T(8,128)(2,1)S(1)} %get-tuple-element.13.a_ref, bf16[336,384]{1,0:T(8,128)(2,1)S(1)} %collective-permute-done.4.b_ref, bf16[336,384]{1,0:T(8,128)(2,1)S(1)} %collective-permute-done.5.c_ref, bf16[336,384]{1,0:T(8,128)(2,1)S(1)} %collective-permute-done.6.d_ref, ...), custom_call_target="tpu_custom_call" | custom-call | bytes 2600000 | tf_op jit(solution)/shard_map/pallas_call | solution.py:206
  (2 shorter events, 0.0 us)
Async XLA Ops:
  0.0 0.9 %copy-start = (bf16[24,1600]{1,0:T(8,128)(2,1)S(1)}, bf16[24,1600]{1,0:T(8,128)(2,1)}, u32[]{:S(2)}) copy-start(bf16[24,1600]{1,0:T(8,128)(2,1)} %t_ref.1) | copy-start | bytes 230404
  0.9 0.7 %copy-start.1 = (s32[1536]{0:T(1024)S(1)}, s32[1536]{0:T(1024)}, u32[]{:S(2)}) copy-start(s32[1536]{0:T(1024)} %ids_ref.1) | copy-start | bytes 18436
  1.6 0.7 %copy-start.3 = (s32[8]{0:T(128)S(1)}, s32[8]{0:T(128)}, u32[]{:S(2)}) copy-start(s32[8]{0:T(128)} %virt_ref.7) | copy-start | bytes 100
  2.2 0.7 %copy-start.5 = (s32[8]{0:T(128)S(1)}, s32[8]{0:T(128)}, u32[]{:S(2)}) copy-start(s32[8]{0:T(128)} %occ_ref.3) | copy-start | bytes 100
  2.9 32.2 %copy-start.2 = (s32[1536]{0:T(1024)S(1)}, s32[1536]{0:T(1024)}, u32[]{:S(2)}) copy-start(s32[1536]{0:T(1024)} %ids_ref.1) | copy-start | bytes 18436
  2.9 32.2 %copy-start.4 = (s32[8]{0:T(128)S(1)}, s32[8]{0:T(128)}, u32[]{:S(2)}) copy-start(s32[8]{0:T(128)} %virt_ref.7) | copy-start | bytes 100
  2.9 32.2 %copy-start.6 = (s32[8]{0:T(128)S(1)}, s32[8]{0:T(128)}, u32[]{:S(2)}) copy-start(s32[8]{0:T(128)} %occ_ref.3) | copy-start | bytes 100
  21.5 5.9 %collective-permute-start.2 = (bf16[192,384]{1,0:T(8,128)(2,1)S(1)}, bf16[192,384]{1,0:T(8,128)(2,1)S(1)}, u32[]{:S(2)}, u32[]{:S(2)}) collective-permute-start(bf16[192,384]{1,0:T(8,128)(2,1)S(1)} %bitcast.4), channel_id=1, source_target_pairs={{0,192},{64,0},{128,64},{192,128},{1,193},{65,1},{129,65},{193,129... | collective-permute-start | bytes 442376 | tf_op jit(solution)/shard_map/ppermute | solution.py:169
  24.0 5.6 %collective-permute-start.1 = (bf16[192,384]{1,0:T(8,128)(2,1)S(1)}, bf16[192,384]{1,0:T(8,128)(2,1)S(1)}, u32[]{:S(2)}, u32[]{:S(2)}) collective-permute-start(bf16[192,384]{1,0:T(8,128)(2,1)S(1)} %bitcast.5), channel_id=1, source_target_pairs={{0,128},{64,192},{128,0},{192,64},{1,129},{65,193},{129,1},{193,65... | collective-permute-start | bytes 442376 | tf_op jit(solution)/shard_map/ppermute | solution.py:169
  24.5 6.6 %collective-permute-start = (bf16[192,384]{1,0:T(8,128)(2,1)S(1)}, bf16[192,384]{1,0:T(8,128)(2,1)S(1)}, u32[]{:S(2)}, u32[]{:S(2)}) collective-permute-start(bf16[192,384]{1,0:T(8,128)(2,1)S(1)} %bitcast.6), channel_id=1, source_target_pairs={{0,64},{64,128},{128,192},{192,0},{1,65},{65,129},{129,193},{193,1... | collective-permute-start | bytes 442376 | tf_op jit(solution)/shard_map/ppermute | solution.py:169
  31.1 9.0 %collective-permute-start.3 = (bf16[768,384]{1,0:T(8,128)(2,1)S(1)}, bf16[768,384]{1,0:T(8,128)(2,1)S(1)}, u32[]{:S(2)}, u32[]{:S(2)}) collective-permute-start(bf16[768,384]{1,0:T(8,128)(2,1)S(1)} %pad_maximum_fusion.own_ref), channel_id=1, source_target_pairs={{0,4},{4,0},{1,5},{5,1},{2,6},{6,2},{3,7},{7,3},{8,12},{12,8},{9,1... | collective-permute-start | bytes 1769480 | tf_op jit(solution)/shard_map/ppermute | solution.py:169
  46.4 9.4 %collective-permute-start.4 = (bf16[336,384]{1,0:T(8,128)(2,1)S(1)}, bf16[336,384]{1,0:T(8,128)(2,1)S(1)}, u32[]{:S(2)}, u32[]{:S(2)}) collective-permute-start(bf16[336,384]{1,0:T(8,128)(2,1)S(1)} %get-tuple-element.14), channel_id=1, source_target_pairs={{0,2},{1,3},{2,0},{3,1},{4,6},{5,7},{6,4},{7,5},{8,10},{9,11},{10,... | collective-permute-start | bytes 774152 | tf_op jit(solution)/shard_map/ppermute | solution.py:169
  49.4 12.3 %collective-permute-start.5 = (bf16[336,384]{1,0:T(8,128)(2,1)S(1)}, bf16[336,384]{1,0:T(8,128)(2,1)S(1)}, u32[]{:S(2)}, u32[]{:S(2)}) collective-permute-start(bf16[336,384]{1,0:T(8,128)(2,1)S(1)} %get-tuple-element.15), channel_id=1, source_target_pairs={{0,1},{1,2},{2,3},{3,0},{4,5},{5,6},{6,7},{7,4},{8,9},{9,10},{10,1... | collective-permute-start | bytes 774152 | tf_op jit(solution)/shard_map/ppermute | solution.py:169
  49.8 11.9 %collective-permute-start.6 = (bf16[336,384]{1,0:T(8,128)(2,1)S(1)}, bf16[336,384]{1,0:T(8,128)(2,1)S(1)}, u32[]{:S(2)}, u32[]{:S(2)}) collective-permute-start(bf16[336,384]{1,0:T(8,128)(2,1)S(1)} %get-tuple-element.16), channel_id=1, source_target_pairs={{0,3},{1,0},{2,1},{3,2},{4,7},{5,4},{6,5},{7,6},{8,11},{9,8},{10,9... | collective-permute-start | bytes 774152 | tf_op jit(solution)/shard_map/ppermute | solution.py:169

commit v2 on v1

v2 whole, which is shorter than its diff:
```python
import functools

import jax
import jax.numpy as jnp
from jax import lax
from jax.experimental import pallas as pl
from jax.experimental.pallas import tpu as pltpu
from jax.sharding import Mesh, PartitionSpec as P

VIRT = 1600
NOCC = 200
PAIRS = 1536
BMAX = 320
NX, NZ, NC, NY = 4, 8, 2, 4
AWIDTH = VIRT // (NX * NZ * NC)
CWIDTH = VIRT // NY
ROWS = PAIRS // (NX * NZ * NC)
HALF = NZ * ROWS
PORTION = NC * HALF
LANES = 384
MAIN = 256
WINDOW = 352
FOLD = WINDOW // 2
MESSAGE = WINDOW + FOLD
SPAN = 512
LAST = 1152
F32, BF16, I32 = jnp.float32, jnp.bfloat16, jnp.int32
SMEM = pl.BlockSpec(memory_space=pltpu.SMEM)
VMEM = pl.BlockSpec(memory_space=pltpu.VMEM)
HBM = pl.BlockSpec(memory_space=pltpu.HBM)
NT = (((1,), (1,)), ((), ()))


def offset_of(sizes_ref, group):
    total = jnp.int32(0)
    for g in range(7):
        total += jnp.where(group > g, sizes_ref[g], 0)
    return total


def irrep_of(position, sizes_ref):
    bound, irrep = jnp.int32(0), jnp.zeros_like(position)
    for g in range(7):
        bound += sizes_ref[g]
        irrep += (position >= bound).astype(I32)
    return irrep


def pair_sym(ids, sizes_ref):
    first = lax.shift_right_logical(ids * 5243, 20)
    second = ids - first * NOCC
    return jnp.bitwise_xor(irrep_of(first, sizes_ref), irrep_of(second, sizes_ref))


def vp_index():
    return (lax.axis_index("x") * NZ + lax.axis_index("z")) * NC + lax.axis_index("c")


def row_irrep(virt_ref):
    return irrep_of(vp_index() * AWIDTH, virt_ref)


def col_irrep(virt_ref):
    return irrep_of(lax.axis_index("y") * CWIDTH, virt_ref)


def block_start(offset):
    return pl.multiple_of(lax.div(offset, 16) * 16, 16)


def load_span(source_ref, span_ref, offset):
    @pl.when(offset < LAST)
    def _():
        start = pl.multiple_of(lax.div(offset, 128) * 128, 128)
        span_ref[...] = source_ref[:, pl.ds(start, SPAN)]

    @pl.when(offset >= LAST)
    def _():
        span_ref[:, :384] = source_ref[:, LAST:1536]
        span_ref[:, 384:448] = source_ref[:, 1536:1600]
        span_ref[:, 448:] = jnp.zeros((span_ref.shape[0], 64), span_ref.dtype)

    shift = jnp.where(offset < LAST, lax.rem(offset, 128), offset - LAST)
    return lax.rem(SPAN - shift, SPAN)


def pack_kernel(virt_hbm, occ_hbm, ids_hbm, t_hbm, out_ref, virt_out, occ_out,
                virt_ref, occ_ref, ids_ref, t_ref, wide, span, sems):
    pairs = ((virt_hbm, virt_ref), (occ_hbm, occ_ref), (ids_hbm, ids_ref), (t_hbm, t_ref))
    copies = [pltpu.make_async_copy(a, b, sems.at[i]) for i, (a, b) in enumerate(pairs)]
    for copy in copies:
        copy.start()
    for copy in copies:
        copy.wait()
    for g in range(8):
        virt_out[g] = virt_ref[g]
        occ_out[g] = occ_ref[g]
    wide[...] = t_ref[...].astype(F32)
    hc = col_irrep(virt_ref)
    base = vp_index() * ROWS
    row = lax.broadcasted_iota(I32, (ROWS, LANES), 0)
    lane = lax.broadcasted_iota(I32, (ROWS, LANES), 1)
    sym = jnp.zeros((ROWS, LANES), I32)
    for r in range(ROWS):
        sym = jnp.where(row == r, pair_sym(ids_ref[base + r], occ_ref), sym)
    packed = jnp.where(lane >= BMAX, sym.astype(F32), 0.0)
    for s in range(8):
        group = jnp.bitwise_xor(hc, s)
        turn = load_span(wide, span, offset_of(virt_ref, group))
        block = pltpu.roll(span[...], turn, 1)[:, :LANES]
        packed = jnp.where((sym == s) & (lane < virt_ref[group]), block, packed)
    out_ref[...] = jnp.concatenate([packed] * NZ, axis=0).astype(BF16)


def blocks_kernel(virt_ref, occ_ref, ids_ref, v_hbm, mine_ref, out_ref, order_ref, sym_ref, copy_ref,
                  windows, span, rolled, sems):
    ra, hc = row_irrep(virt_ref), col_irrep(virt_ref)
    starts = [block_start(offset_of(virt_ref, jnp.bitwise_xor(ra, s))) for s in range(8)]
    firsts = [pl.multiple_of(jnp.minimum(start, VIRT - WINDOW), 16) for start in starts]
    copies = [
        pltpu.make_async_copy(v_hbm.at[pl.ds(firsts[s], WINDOW), :], windows.at[s], sems.at[s]) for s in range(8)
    ]
    for copy in copies:
        copy.start()
    copy_ref[...] = mine_ref[...]
    rolled[WINDOW:, :] = jnp.zeros((WINDOW, LANES), BF16)
    odd = jnp.bitwise_and(lax.axis_index("x") + lax.axis_index("y"), 1) == 1
    column = lax.broadcasted_iota(I32, (128, PORTION), 0)
    target = lax.broadcasted_iota(I32, (128, PORTION), 1)
    for half in range(2):
        core = jnp.bitwise_xor(lax.axis_index("c"), half)

        def hits(position):
            z = lax.shift_right_logical(position * 2731, 16)
            return (z * NC + core) * ROWS + (position - z * ROWS) == target

        full = hits(column + jnp.where(odd, 64, 0))
        part = hits(jnp.bitwise_and(column, 63) + jnp.where(odd, 0, 128))
        order_ref[half * 128:half * 128 + 128, :] = full.astype(F32).astype(BF16)
        order_ref[256 + half * 128:384 + half * 128, :] = (part & (column < 64)).astype(F32).astype(BF16)
        order_ref[512 + half * 128:640 + half * 128, :] = (part & (column >= 64)).astype(F32).astype(BF16)
    ids = ids_ref[pl.ds(lax.axis_index("y"), 1), :]
    sym_ref[...] = jnp.broadcast_to(pair_sym(ids, occ_ref), (16, PORTION)).astype(F32).astype(BF16)
    lane = lax.broadcasted_iota(I32, (WINDOW, LANES), 1)
    for s in range(8):
        group = jnp.bitwise_xor(hc, s)
        copies[s].wait()
        turn = load_span(windows.at[s], span, offset_of(virt_ref, group))
        block = pltpu.roll(span[...].astype(F32), turn, 1)[:, :LANES]
        rolled[:WINDOW, :] = jnp.where(lane < virt_ref[group], block, 0.0).astype(BF16)
        block = rolled[pl.ds(pl.multiple_of(starts[s] - firsts[s], 16), WINDOW), :]
        out_ref[:, s * MAIN:(s + 1) * MAIN] = block[:, :MAIN]
        out_ref[:, 8 * MAIN + s * 128:8 * MAIN + (s + 1) * 128] = block[:, MAIN:]


def terms_kernel(virt_ref, t_ref, v_ref, o0, o1, o2, o3, stack, total):
    hc = col_irrep(virt_ref)
    x, y = lax.axis_index("x"), lax.axis_index("y")
    t = t_ref[...]
    sym = jnp.broadcast_to(t[:, BMAX:BMAX + 1].astype(F32), (NX * HALF, MAIN)).astype(BF16)
    for s in range(8):
        stack[:, s * MAIN:(s + 1) * MAIN] = jnp.where(sym == jnp.asarray(s, BF16), t[:, :MAIN], jnp.zeros((), BF16))
    total[...] = lax.dot_general(v_ref[:, :8 * MAIN], stack[...], NT, preferred_element_type=F32)
    for s in range(8):

        @pl.when(virt_ref[jnp.bitwise_xor(hc, s)] > MAIN)
        def _():
            rest = jnp.where(sym[:, :128] == jnp.asarray(s, BF16), t[:, MAIN:], jnp.zeros((), BF16))
            block = v_ref[:, 8 * MAIN + s * 128:8 * MAIN + (s + 1) * 128]
            total[...] += lax.dot_general(block, rest, NT, preferred_element_type=F32)

    lane = lax.broadcasted_iota(I32, (FOLD, 128), 1)
    for k in range(NX):
        whole = k * HALF + (k % 2) * 64
        part = k * HALF + (1 - k % 2) * 128 - (k % 2) * 64
        upper, lower = total[:FOLD, part:part + 128], total[FOLD:, part:part + 128]
        if k % 2:
            upper = pltpu.roll(upper, 64, 1)
        else:
            lower = pltpu.roll(lower, 64, 1)
        folded = jnp.where(lane < 64, upper, lower).astype(BF16)
        full = total[:, whole:whole + 128].astype(BF16)
        step = lax.rem(x - k - y + 2 * NX, NY)
        for r, out_ref in enumerate((o0, o1, o2, o3)):

            @pl.when(step == r)
            def _():
                out_ref[:WINDOW, :] = full
                out_ref[WINDOW:, :] = folded


def place_kernel(virt_ref, a0, a1, a2, a3, b0, b1, b2, b3, order_ref, sym_ref, out_ref, total, wide, sem):
    ra = row_irrep(virt_ref)
    for half, refs in enumerate(((a0, a1, a2, a3), (b0, b1, b2, b3))):
        value = refs[0][...].astype(F32)
        for ref in refs[1:]:
            value += ref[...].astype(F32)
        total[:, half * 128:(half + 1) * 128] = value.astype(BF16)
    value = jnp.dot(total[:WINDOW, :], order_ref[:256, :], preferred_element_type=F32)
    upper = jnp.dot(total[WINDOW:, :], order_ref[256:512, :], preferred_element_type=F32)
    lower = jnp.dot(total[WINDOW:, :], order_ref[512:, :], preferred_element_type=F32)
    value = (value + jnp.concatenate([upper, lower], axis=0)).astype(BF16)
    sym = sym_ref[...]
    row = lax.broadcasted_iota(I32, (16, PORTION), 0)
    for group in range(8):
        offset = offset_of(virt_ref, group)
        start = block_start(offset)
        mask = sym == jnp.bitwise_xor(ra, group).astype(F32).astype(BF16)
        kept = jnp.where(jnp.concatenate([mask] * (WINDOW // 16), axis=0), value, jnp.zeros((), BF16))
        head = wide[pl.ds(start, 16), :].astype(F32)
        wide[pl.ds(start, 16), :] = jnp.where(row < offset - start, head, kept[:16].astype(F32)).astype(BF16)
        wide[pl.ds(start + 16, WINDOW - 16), :] = kept[16:]
    copy = pltpu.make_async_copy(wide.at[pl.ds(0, VIRT), :], out_ref, sem)
    copy.start()
    copy.wait()


def shift(value, axis, size, by):
    return lax.ppermute(value, axis, [(i, (i + by) % size) for i in range(size)])


def call(kernel, specs, out, scratch=(), out_specs=None, flops=0, moved=0, limit=40):
    return pl.pallas_call(
        kernel,
        in_specs=specs,
        out_specs=out_specs or jax.tree.map(lambda _: VMEM, out),
        out_shape=out,
        scratch_shapes=list(scratch),
        compiler_params=pltpu.CompilerParams(vmem_limit_bytes=limit * 2**20),
        cost_estimate=pl.CostEstimate(flops=flops, bytes_accessed=moved, transcendentals=0),
    )


def shards(virt_sizes, occ_sizes, pair_ids, amplitudes, integrals):
    shape = jax.ShapeDtypeStruct
    packed, virt, occ = call(
        pack_kernel, [HBM] * 4, (shape((HALF, LANES), BF16), shape((8,), I32), shape((8,), I32)),
        [pltpu.SMEM((8,), I32), pltpu.SMEM((8,), I32), pltpu.SMEM((PAIRS,), I32), pltpu.VMEM((ROWS, VIRT), BF16),
         pltpu.VMEM((ROWS, VIRT), F32), pltpu.VMEM((ROWS, SPAN), F32), pltpu.SemaphoreType.DMA((4,))],
        (VMEM, SMEM, SMEM), moved=300000, limit=64,
    )(virt_sizes, occ_sizes, pair_ids, amplitudes)
    mine = lax.all_to_all(packed, "z", 0, 0, tiled=True)
    across = [shift(mine, "x", NX, k) for k in (2, 1, 3)]
    blocks, order, sym, mine = call(
        blocks_kernel, [SMEM, SMEM, VMEM, HBM, VMEM],
        (shape((WINDOW, 8 * LANES), BF16), shape((6 * 128, PORTION), BF16), shape((16, PORTION), BF16),
         shape((HALF, LANES), BF16)),
        [pltpu.VMEM((8, WINDOW, VIRT), BF16), pltpu.VMEM((WINDOW, SPAN), BF16),
         pltpu.VMEM((2 * WINDOW, LANES), BF16), pltpu.SemaphoreType.DMA((8,))], moved=16000000, limit=48,
    )(virt, occ, pair_ids.reshape(NY, PORTION), integrals, mine)
    own = jnp.concatenate([mine, across[1], across[0], across[2]], axis=0)
    other = shift(own, "c", NC, 1)
    tile = shape((MESSAGE, 128), BF16)
    near, far = [], []
    for half in (own, other):
        terms = call(
            terms_kernel, [SMEM, VMEM, VMEM], (tile,) * NY,
            [pltpu.VMEM((NX * HALF, 8 * MAIN), BF16), pltpu.VMEM((WINDOW, NX * HALF), F32)],
            flops=PAIRS * WINDOW * 8 * MAIN, moved=4500000,
        )(virt, half, blocks)
        near.append(terms[0])
        far.append([shift(terms[r], "y", NY, r) for r in (2, 1, 3)])
    out = call(
        place_kernel, [SMEM] + [VMEM] * 10, shape((VIRT, PORTION), BF16),
        [pltpu.VMEM((MESSAGE, 2 * 128), BF16), pltpu.VMEM((VIRT + WINDOW, PORTION), BF16), pltpu.SemaphoreType.DMA],
        HBM, moved=2600000,
    )(virt, near[0], *far[0], near[1], *far[1], order, sym)
    return out.T


def solution(mesh):
    grid = Mesh(mesh.devices.reshape(NX, NZ, NC, NY), ("x", "z", "c", "y"))
    vp = ("x", "z", "c")
    in_specs = (P(), P(), P(), P(vp, "y"), P(vp, "y"))
    return jax.shard_map(shards, mesh=grid, in_specs=in_specs, out_specs=P("y", vp), check_vma=False)
```

time: 65 us -> 58.2 us (0.90)
  waiting for transfers between devices: 15.6 us -> 6.74 us
  starting transfers between devices: 13.2 us -> 16.7 us
  Pallas kernels: 16.1 us -> 15.2 us
  local copies, waits for them, and re-layouts: 2.91 us -> 2.08 us
    ppermute x7 -> x10, waiting for transfers between devices: 15.6 us -> 6.74 us  [shift(): lax.ppermute(value, axis, [(i, (i + by) % size) for i in range(size)])]
    ppermute x7 -> x10, starting transfers between devices: 13.2 us -> 16.7 us  [shift(): lax.ppermute(value, axis, [(i, (i + by) % size) for i in range(size)])]
    unnamed x14 -> x7, local copies, waits for them, and re-layouts: 2.9 us -> 1.35 us
    pallas_call x4 -> x5, Pallas kernels: 16.1 us -> 15.2 us  [the longest x2 5.36 us: shards(): call(terms_kernel, [SMEM, VMEM, VMEM], (tile,) * NY, [pltpu.VMEM((NX * HA...]
    reshape x1, local copies, waits for them, and re-layouts: 0.01 us -> 0.7 us  [shards(): pair_ids.reshape(NY, PORTION)]
  transfers between devices with their start and end apart: 7 -> 10, of which waited for: 5 -> 2; matrix products, arithmetic and copies ran while one was open for 0% -> 1% of each run, Pallas kernels for 8% -> 18%
where the time goes in v2:
time: 58.2 us; the launch traced here: 57.9 us
  blocking collectives  16.9 us (29%)
  starting transfers between devices  16.7 us (29%)
  Pallas kernels  15.2 us (26%)
  waiting for transfers between devices  6.74 us (12%)
  local copies, waits for them, and re-layouts  2.08 us (4%)
    all_to_all x1, blocking collectives, shards(): mine = lax.all_to_all(packed, 'z', 0, 0, tiled=True)  16.9 us
    ppermute x10, starting transfers between devices, shift(): lax.ppermute(value, axis, [(i, (i + by) % size) for i in range(size)])  16.7 us
    ppermute x10, waiting for transfers between devices, shift(): lax.ppermute(value, axis, [(i, (i + by) % size) for i in range(size)])  6.74 us
    pallas_call x2, Pallas kernels, shards(): call(terms_kernel, [SMEM, VMEM, VMEM], (tile,) * NY, [pltpu.VMEM((NX * HA...  5.36 us
    pallas_call x1, Pallas kernels, shards(): call(blocks_kernel, [SMEM, SMEM, VMEM, HBM, VMEM], (shape((WINDOW, 8 * LA...  4.91 us
    pallas_call x1, Pallas kernels, shards(): call(pack_kernel, [HBM] * 4, (shape((HALF, LANES), BF16), shape((8,), I32...  2.72 us
    pallas_call x1, Pallas kernels, shards(): call(place_kernel, [SMEM] + [VMEM] * 10, shape((VIRT, PORTION), BF16), [p...  2.2 us
    unnamed x7, local copies, waits for them, and re-layouts  1.35 us
  transfers between devices with their start and end apart: 10, of which 2 were waited for; matrix products, arithmetic and copies ran while one was open for 1% of the time, Pallas kernels for 18%

profile of v2, /device:TPU:1, one launch (start us, length us, event | category | flops | bytes accessed | tf_op | source)
XLA Modules:
  0.0 57.9 jit_solution(7081752393275635088)
XLA Ops:
  0.0 2.7 %shard_map.55 = (bf16[192,384]{1,0:T(8,128)(2,1)}, s32[8]{0:T(128)}, s32[8]{0:T(128)}) custom-call(s32[8]{0:T(128)} %virt_hbm.1, s32[8]{0:T(128)} %occ_hbm.1, s32[1536]{0:T(1024)} %ids_hbm.1, bf16[24,1600]{1,0:T(8,128)(2,1)} %t_hbm.1), custom_call_target="tpu_custom_call" | custom-call | bytes 300000 | tf_op jit(solution)/shard_map/pallas_call | solution.py:236
  2.7 16.9 %all_to_all.11 = bf16[8,24,384]{2,1,0:T(8,128)(2,1)S(1)} all-to-all(bf16[8,24,384]{2,1,0:T(8,128)(2,1)} %bitcast.7), channel_id=1, replica_groups=mesh['x'=4,'z'=8,'c'=2,'y'=4] {'z'}, dimensions={0} | all-to-all | bytes 294912 | tf_op jit(solution)/shard_map/all_to_all | solution.py:242
  19.7 1.2 %collective-permute-start = (bf16[192,384]{1,0:T(8,128)(2,1)S(1)}, bf16[192,384]{1,0:T(8,128)(2,1)S(1)}, u32[]{:S(2)}, u32[]{:S(2)}) collective-permute-start(bf16[192,384]{1,0:T(8,128)(2,1)S(1)} %bitcast.3), channel_id=1, source_target_pairs={{0,64},{64,128},{128,192},{192,0},{1,65},{65,129},{129,193},{193,1... | collective-permute-start | bytes 442376 | tf_op jit(solution)/shard_map/ppermute | solution.py:219
  20.9 0.7 %reshape.5.ids_ref = s32[4,384]{1,0:T(4,128)S(1)} reshape(s32[1536]{0:T(1024)} %ids_hbm.1) | data formatting | bytes 12288 | tf_op jit(solution)/shard_map/reshape | solution.py:250
  21.6 2.5 %collective-permute-start.1 = (bf16[192,384]{1,0:T(8,128)(2,1)S(1)}, bf16[192,384]{1,0:T(8,128)(2,1)S(1)}, u32[]{:S(2)}, u32[]{:S(2)}) collective-permute-start(bf16[192,384]{1,0:T(8,128)(2,1)S(1)} %bitcast.4), channel_id=1, source_target_pairs={{0,128},{64,192},{128,0},{192,64},{1,129},{65,193},{129,1},{193,65... | collective-permute-start | bytes 442376 | tf_op jit(solution)/shard_map/ppermute | solution.py:219
  24.0 1.2 %collective-permute-start.2 = (bf16[192,384]{1,0:T(8,128)(2,1)S(1)}, bf16[192,384]{1,0:T(8,128)(2,1)S(1)}, u32[]{:S(2)}, u32[]{:S(2)}) collective-permute-start(bf16[192,384]{1,0:T(8,128)(2,1)S(1)} %bitcast.5), channel_id=1, source_target_pairs={{0,192},{64,0},{128,64},{192,128},{1,193},{65,1},{129,65},{193,129... | collective-permute-start | bytes 442376 | tf_op jit(solution)/shard_map/ppermute | solution.py:219
  25.2 0.0 copy-start
  25.2 0.7 %copy-done = s32[8]{0:T(128)S(1)} copy-done((s32[8]{0:T(128)S(1)}, s32[8]{0:T(128)}, u32[]{:S(2)}) %copy-start) | copy-done | bytes 56
  25.9 0.0 copy-start.1
  25.9 0.6 %copy-done.1 = s32[8]{0:T(128)S(1)} copy-done((s32[8]{0:T(128)S(1)}, s32[8]{0:T(128)}, u32[]{:S(2)}) %copy-start.1) | copy-done | bytes 56
  26.5 4.9 %shard_map.56 = (bf16[352,3072]{1,0:T(8,128)(2,1)S(1)}, bf16[768,384]{1,0:T(8,128)(2,1)S(1)}, bf16[16,384]{1,0:T(8,128)(2,1)S(1)}, bf16[192,384]{1,0:T(8,128)(2,1)S(1)}) custom-call(s32[8]{0:T(128)S(1)} %copy-done, s32[8]{0:T(128)S(1)} %copy-done.1, s32[4,384]{1,0:T(4,128)S(1)} %reshape.5.ids_ref, bf16[1600,1600]{1,0:T(8,128)(2,1)} %v_hbm.1, ...), custom_call_target="tpu_custom_call" | custom-call | bytes 16000000 | tf_op jit(solution)/shard_map/pallas_call | solution.py:244
  31.4 0.0 collective-permute-done
  31.5 0.0 collective-permute-done.1
  31.5 0.0 collective-permute-done.2
  31.6 3.4 %collective-permute-start.6 = (bf16[768,384]{1,0:T(8,128)(2,1)S(1)}, bf16[768,384]{1,0:T(8,128)(2,1)S(1)}, u32[]{:S(2)}, u32[]{:S(2)}) collective-permute-start(bf16[768,384]{1,0:T(8,128)(2,1)S(1)} %constant_dynamic-update-slice_fusion.t_ref), channel_id=1, source_target_pairs={{0,4},{4,0},{1,5},{5,1},{2,6},{6,2},{3,7},{7,3},{8,12},{12,8},{9,1... | collective-permute-start | bytes 1769480 | tf_op jit(solution)/shard_map/ppermute | solution.py:219
  34.9 2.7 %shard_map.57 = (bf16[528,128]{1,0:T(8,128)(2,1)S(1)}, bf16[528,128]{1,0:T(8,128)(2,1)S(1)}, bf16[528,128]{1,0:T(8,128)(2,1)S(1)}, bf16[528,128]{1,0:T(8,128)(2,1)S(1)}) custom-call(s32[8]{0:T(128)S(1)} %copy-done, bf16[768,384]{1,0:T(8,128)(2,1)S(1)} %constant_dynamic-update-slice_fusion.t_ref, bf16[352,3072]{1,0:T(8,128)(2,1)S(1)} %get-tuple-element.24.v_ref), custom_call_target="tpu_custom_call" | custom-call | flops 1107296256 | bytes 4500000 | tf_op jit(solution)/shard_map/pallas_call | solution.py:256
  37.6 3.0 %collective-permute-start.3 = (bf16[528,128]{1,0:T(8,128)(2,1)S(1)}, bf16[528,128]{1,0:T(8,128)(2,1)S(1)}, u32[]{:S(2)}, u32[]{:S(2)}) collective-permute-start(bf16[528,128]{1,0:T(8,128)(2,1)S(1)} %get-tuple-element.26), channel_id=1, source_target_pairs={{0,2},{1,3},{2,0},{3,1},{4,6},{5,7},{6,4},{7,5},{8,10},{9,11},{10,... | collective-permute-start | bytes 405512 | tf_op jit(solution)/shard_map/ppermute | solution.py:219
  40.6 0.4 collective-permute-start.4
  41.0 2.3 %collective-permute-start.5 = (bf16[528,128]{1,0:T(8,128)(2,1)S(1)}, bf16[528,128]{1,0:T(8,128)(2,1)S(1)}, u32[]{:S(2)}, u32[]{:S(2)}) collective-permute-start(bf16[528,128]{1,0:T(8,128)(2,1)S(1)} %get-tuple-element.28), channel_id=1, source_target_pairs={{0,3},{1,0},{2,1},{3,2},{4,7},{5,4},{6,5},{7,6},{8,11},{9,8},{10,9... | collective-permute-start | bytes 405512 | tf_op jit(solution)/shard_map/ppermute | solution.py:219
  43.3 0.0 collective-permute-done.6.t_ref
  43.3 2.7 %shard_map.58 = (bf16[528,128]{1,0:T(8,128)(2,1)S(1)}, bf16[528,128]{1,0:T(8,128)(2,1)S(1)}, bf16[528,128]{1,0:T(8,128)(2,1)S(1)}, bf16[528,128]{1,0:T(8,128)(2,1)S(1)}) custom-call(s32[8]{0:T(128)S(1)} %copy-done, bf16[768,384]{1,0:T(8,128)(2,1)S(1)} %collective-permute-done.6.t_ref, bf16[352,3072]{1,0:T(8,128)(2,1)S(1)} %get-tuple-element.24.v_ref), custom_call_target="tpu_custom_call" | custom-call | flops 1107296256 | bytes 4500000 | tf_op jit(solution)/shard_map/pallas_call | solution.py:256
  45.9 0.1 collective-permute-start.7
  46.0 0.6 collective-permute-start.8
  46.6 0.0 collective-permute-done.3.a1
  46.6 2.2 %collective-permute-start.9 = (bf16[528,128]{1,0:T(8,128)(2,1)S(1)}, bf16[528,128]{1,0:T(8,128)(2,1)S(1)}, u32[]{:S(2)}, u32[]{:S(2)}) collective-permute-start(bf16[528,128]{1,0:T(8,128)(2,1)S(1)} %get-tuple-element.32), channel_id=1, source_target_pairs={{0,3},{1,0},{2,1},{3,2},{4,7},{5,4},{6,5},{7,6},{8,11},{9,8},{10,9... | collective-permute-start | bytes 405512 | tf_op jit(solution)/shard_map/ppermute | solution.py:219
  48.8 0.0 collective-permute-done.4.a2
  48.8 0.0 collective-permute-done.5.a3
  48.8 3.1 %collective-permute-done.7.b1 = bf16[528,128]{1,0:T(8,128)(2,1)S(1)} collective-permute-done((bf16[528,128]{1,0:T(8,128)(2,1)S(1)}, bf16[528,128]{1,0:T(8,128)(2,1)S(1)}, u32[]{:S(2)}, u32[]{:S(2)}) %collective-permute-start.7) | collective-permute-done | bytes 135200 | tf_op jit(solution)/shard_map/ppermute | solution.py:219
  51.9 3.7 %collective-permute-done.8.b2 = bf16[528,128]{1,0:T(8,128)(2,1)S(1)} collective-permute-done((bf16[528,128]{1,0:T(8,128)(2,1)S(1)}, bf16[528,128]{1,0:T(8,128)(2,1)S(1)}, u32[]{:S(2)}, u32[]{:S(2)}) %collective-permute-start.8) | collective-permute-done | bytes 135200 | tf_op jit(solution)/shard_map/ppermute | solution.py:219
  55.5 0.0 collective-permute-done.9.b3
  55.5 2.2 %shard_map.59 = bf16[1600,384]{1,0:T(8,128)(2,1)} custom-call(s32[8]{0:T(128)S(1)} %copy-done, bf16[528,128]{1,0:T(8,128)(2,1)S(1)} %get-tuple-element.25.a0, bf16[528,128]{1,0:T(8,128)(2,1)S(1)} %collective-permute-done.3.a1, bf16[528,128]{1,0:T(8,128)(2,1)S(1)} %collective-permute-done.4.a2, bf16[528,128]{1,0:T(8,128)(2,1)S(1)} %collective-permute-done.5.a3, ...), custom_call_target="tpu_custom_call" | custom-call | bytes 2600000 | tf_op jit(solution)/shard_map/pallas_call | solution.py:263
  (4 shorter events, 0.1 us)
Async XLA Ops:
  19.7 11.8 %collective-permute-start = (bf16[192,384]{1,0:T(8,128)(2,1)S(1)}, bf16[192,384]{1,0:T(8,128)(2,1)S(1)}, u32[]{:S(2)}, u32[]{:S(2)}) collective-permute-start(bf16[192,384]{1,0:T(8,128)(2,1)S(1)} %bitcast.3), channel_id=1, source_target_pairs={{0,64},{64,128},{128,192},{192,0},{1,65},{65,129},{129,193},{193,1... | collective-permute-start | bytes 442376 | tf_op jit(solution)/shard_map/ppermute | solution.py:219
  21.6 9.9 %collective-permute-start.1 = (bf16[192,384]{1,0:T(8,128)(2,1)S(1)}, bf16[192,384]{1,0:T(8,128)(2,1)S(1)}, u32[]{:S(2)}, u32[]{:S(2)}) collective-permute-start(bf16[192,384]{1,0:T(8,128)(2,1)S(1)} %bitcast.4), channel_id=1, source_target_pairs={{0,128},{64,192},{128,0},{192,64},{1,129},{65,193},{129,1},{193,65... | collective-permute-start | bytes 442376 | tf_op jit(solution)/shard_map/ppermute | solution.py:219
  24.0 7.5 %collective-permute-start.2 = (bf16[192,384]{1,0:T(8,128)(2,1)S(1)}, bf16[192,384]{1,0:T(8,128)(2,1)S(1)}, u32[]{:S(2)}, u32[]{:S(2)}) collective-permute-start(bf16[192,384]{1,0:T(8,128)(2,1)S(1)} %bitcast.5), channel_id=1, source_target_pairs={{0,192},{64,0},{128,64},{192,128},{1,193},{65,1},{129,65},{193,129... | collective-permute-start | bytes 442376 | tf_op jit(solution)/shard_map/ppermute | solution.py:219
  25.2 0.7 %copy-start = (s32[8]{0:T(128)S(1)}, s32[8]{0:T(128)}, u32[]{:S(2)}) copy-start(s32[8]{0:T(128)} %get-tuple-element.20.virt_ref) | copy-start | bytes 100
  25.9 0.6 %copy-start.1 = (s32[8]{0:T(128)S(1)}, s32[8]{0:T(128)}, u32[]{:S(2)}) copy-start(s32[8]{0:T(128)} %get-tuple-element.21.occ_ref) | copy-start | bytes 100
  31.6 11.7 %collective-permute-start.6 = (bf16[768,384]{1,0:T(8,128)(2,1)S(1)}, bf16[768,384]{1,0:T(8,128)(2,1)S(1)}, u32[]{:S(2)}, u32[]{:S(2)}) collective-permute-start(bf16[768,384]{1,0:T(8,128)(2,1)S(1)} %constant_dynamic-update-slice_fusion.t_ref), channel_id=1, source_target_pairs={{0,4},{4,0},{1,5},{5,1},{2,6},{6,2},{3,7},{7,3},{8,12},{12,8},{9,1... | collective-permute-start | bytes 1769480 | tf_op jit(solution)/shard_map/ppermute | solution.py:219
  37.6 9.0 %collective-permute-start.3 = (bf16[528,128]{1,0:T(8,128)(2,1)S(1)}, bf16[528,128]{1,0:T(8,128)(2,1)S(1)}, u32[]{:S(2)}, u32[]{:S(2)}) collective-permute-start(bf16[528,128]{1,0:T(8,128)(2,1)S(1)} %get-tuple-element.26), channel_id=1, source_target_pairs={{0,2},{1,3},{2,0},{3,1},{4,6},{5,7},{6,4},{7,5},{8,10},{9,11},{10,... | collective-permute-start | bytes 405512 | tf_op jit(solution)/shard_map/ppermute | solution.py:219
  40.6 8.2 %collective-permute-start.4 = (bf16[528,128]{1,0:T(8,128)(2,1)S(1)}, bf16[528,128]{1,0:T(8,128)(2,1)S(1)}, u32[]{:S(2)}, u32[]{:S(2)}) collective-permute-start(bf16[528,128]{1,0:T(8,128)(2,1)S(1)} %get-tuple-element.27), channel_id=1, source_target_pairs={{0,1},{1,2},{2,3},{3,0},{4,5},{5,6},{6,7},{7,4},{8,9},{9,10},{10,1... | collective-permute-start | bytes 405512 | tf_op jit(solution)/shard_map/ppermute | solution.py:219
  41.0 7.8 %collective-permute-start.5 = (bf16[528,128]{1,0:T(8,128)(2,1)S(1)}, bf16[528,128]{1,0:T(8,128)(2,1)S(1)}, u32[]{:S(2)}, u32[]{:S(2)}) collective-permute-start(bf16[528,128]{1,0:T(8,128)(2,1)S(1)} %get-tuple-element.28), channel_id=1, source_target_pairs={{0,3},{1,0},{2,1},{3,2},{4,7},{5,4},{6,5},{7,6},{8,11},{9,8},{10,9... | collective-permute-start | bytes 405512 | tf_op jit(solution)/shard_map/ppermute | solution.py:219
  45.9 5.9 %collective-permute-start.7 = (bf16[528,128]{1,0:T(8,128)(2,1)S(1)}, bf16[528,128]{1,0:T(8,128)(2,1)S(1)}, u32[]{:S(2)}, u32[]{:S(2)}) collective-permute-start(bf16[528,128]{1,0:T(8,128)(2,1)S(1)} %get-tuple-element.30), channel_id=1, source_target_pairs={{0,2},{1,3},{2,0},{3,1},{4,6},{5,7},{6,4},{7,5},{8,10},{9,11},{10,... | collective-permute-start | bytes 405512 | tf_op jit(solution)/shard_map/ppermute | solution.py:219
  46.0 9.5 %collective-permute-start.8 = (bf16[528,128]{1,0:T(8,128)(2,1)S(1)}, bf16[528,128]{1,0:T(8,128)(2,1)S(1)}, u32[]{:S(2)}, u32[]{:S(2)}) collective-permute-start(bf16[528,128]{1,0:T(8,128)(2,1)S(1)} %get-tuple-element.31), channel_id=1, source_target_pairs={{0,1},{1,2},{2,3},{3,0},{4,5},{5,6},{6,7},{7,4},{8,9},{9,10},{10,1... | collective-permute-start | bytes 405512 | tf_op jit(solution)/shard_map/ppermute | solution.py:219
  46.6 8.9 %collective-permute-start.9 = (bf16[528,128]{1,0:T(8,128)(2,1)S(1)}, bf16[528,128]{1,0:T(8,128)(2,1)S(1)}, u32[]{:S(2)}, u32[]{:S(2)}) collective-permute-start(bf16[528,128]{1,0:T(8,128)(2,1)S(1)} %get-tuple-element.32), channel_id=1, source_target_pairs={{0,3},{1,0},{2,1},{3,2},{4,7},{5,4},{6,5},{7,6},{8,11},{9,8},{10,9... | collective-permute-start | bytes 405512 | tf_op jit(solution)/shard_map/ppermute | solution.py:219

commit v3 on v2

v3 whole, which is shorter than its diff:
```python
import functools

import jax
import jax.numpy as jnp
from jax import lax
from jax.experimental import pallas as pl
from jax.experimental.pallas import tpu as pltpu
from jax.sharding import Mesh, PartitionSpec as P

VIRT = 1600
NOCC = 200
PAIRS = 1536
BMAX = 320
NX, NZ, NC, NY = 4, 8, 2, 4
AWIDTH = VIRT // (NX * NZ * NC)
CWIDTH = VIRT // NY
ROWS = PAIRS // (NX * NZ * NC)
HALF = NZ * ROWS
PORTION = NC * HALF
LANES = 384
MAIN = 256
WINDOW = 336
FOLD = WINDOW // 2
MESSAGE = WINDOW + FOLD
SPAN = 512
LAST = 1152
META = BMAX - MAIN + 8
F32, BF16, I32 = jnp.float32, jnp.bfloat16, jnp.int32
SMEM = pl.BlockSpec(memory_space=pltpu.SMEM)
VMEM = pl.BlockSpec(memory_space=pltpu.VMEM)
HBM = pl.BlockSpec(memory_space=pltpu.HBM)
NT = (((1,), (1,)), ((), ()))


def offset_of(sizes, group):
    total = jnp.int32(0)
    for g in range(7):
        total += jnp.where(group > g, sizes[g], 0)
    return total


def size_of(sizes, group):
    total = jnp.int32(0)
    for g in range(8):
        total += jnp.where(group == g, sizes[g], 0)
    return total


def irrep_of(position, sizes):
    bound, irrep = jnp.int32(0), jnp.zeros_like(position)
    for g in range(7):
        bound += sizes[g]
        irrep += (position >= bound).astype(I32)
    return irrep


def pair_sym(ids, sizes):
    first = lax.shift_right_logical(ids * 5243, 20)
    second = ids - first * NOCC
    return jnp.bitwise_xor(irrep_of(first, sizes), irrep_of(second, sizes))


def vp_index():
    return (lax.axis_index("x") * NZ + lax.axis_index("z")) * NC + lax.axis_index("c")


def row_irrep(virt):
    return irrep_of(vp_index() * AWIDTH, virt)


def col_irrep(virt):
    return irrep_of(lax.axis_index("y") * CWIDTH, virt)


def block_start(offset):
    return pl.multiple_of(lax.div(offset, 16) * 16, 16)


def pack_kernel(virt_hbm, occ_hbm, ids_hbm, t_hbm, out_ref, virt_ref, occ_ref, ids_ref, t_ref, wide, sems):
    pairs = ((virt_hbm, virt_ref), (occ_hbm, occ_ref), (ids_hbm, ids_ref), (t_hbm, t_ref))
    copies = [pltpu.make_async_copy(a, b, sems.at[i]) for i, (a, b) in enumerate(pairs)]
    for copy in copies:
        copy.start()
    wide[:, 1536:] = jnp.zeros((ROWS, SPAN + 128), F32)
    for copy in copies[:3]:
        copy.wait()
    virt, occ = [virt_ref[g] for g in range(8)], [occ_ref[g] for g in range(8)]
    hc = col_irrep(virt)
    base = vp_index() * ROWS
    row = lax.broadcasted_iota(I32, (ROWS, 128), 0)
    lane = lax.broadcasted_iota(I32, (ROWS, 128), 1)
    ids = jnp.zeros((ROWS, 128), I32)
    for r in range(ROWS):
        ids = jnp.where(row == r, ids_ref[base + r], ids)
    sym = pair_sym(ids, occ)
    meta = jnp.where(lane < META, sym, 0)
    for g in range(8):
        meta = jnp.where(lane == META + g, lax.shift_right_logical(virt[g], 4), meta)
        meta = jnp.where(lane == META + 8 + g, jnp.bitwise_and(virt[g], 15), meta)
    parts = [jnp.zeros((ROWS, 128), F32)] * 2 + [jnp.where(lane >= BMAX - MAIN, meta, 0).astype(F32)]
    copies[3].wait()
    wide[:, :VIRT] = t_ref[...].astype(F32)
    for s in range(8):
        group = jnp.bitwise_xor(hc, s)
        offset, size = offset_of(virt, group), size_of(virt, group)
        span = wide[:, pl.ds(pl.multiple_of(lax.div(offset, 128) * 128, 128), SPAN)]
        span = pltpu.roll(span, lax.rem(SPAN - lax.rem(offset, 128), SPAN), 1)
        for i in range(3):
            keep = (sym == s) & (lane < size - i * 128)
            parts[i] = jnp.where(keep, span[:, i * 128:(i + 1) * 128], parts[i])
    packed = jnp.concatenate(parts, axis=1)
    out_ref[...] = jnp.concatenate([packed] * NZ, axis=0).astype(BF16)


def blocks_kernel(mine_ref, v_hbm, out_ref, order_ref, meta_ref, copy_ref, windows, span, sizes, sems):
    sizes[...] = mine_ref[:16, MAIN:].astype(F32).astype(I32)
    virt = [sizes[0, META + g] * 16 + sizes[0, META + 8 + g] for g in range(8)]
    ra, hc = row_irrep(virt), col_irrep(virt)
    starts = [block_start(offset_of(virt, jnp.bitwise_xor(ra, s))) for s in range(8)]
    firsts = [pl.multiple_of(jnp.minimum(start, VIRT - WINDOW), 16) for start in starts]
    copies = [
        pltpu.make_async_copy(v_hbm.at[pl.ds(firsts[s], WINDOW), :], windows.at[s, pl.ds(0, WINDOW), :], sems.at[s])
        for s in range(8)
    ]
    for copy in copies:
        copy.start()
    copy_ref[...] = mine_ref[...]
    row = lax.broadcasted_iota(I32, (8, 128), 0)
    meta = jnp.zeros((8, 128), I32)
    for g in range(8):
        meta = jnp.where(row == g, virt[g], meta)
    meta_ref[...] = meta
    column = lax.broadcasted_iota(I32, (128, PORTION), 0)
    target = lax.broadcasted_iota(I32, (128, PORTION), 1)
    for half in range(2):
        core = jnp.bitwise_xor(lax.axis_index("c"), half)

        def hits(position):
            z = lax.shift_right_logical(position * 2731, 16)
            return (z * NC + core) * ROWS + (position - z * ROWS) == target

        part = hits(jnp.bitwise_and(column, 63) + 128)
        order_ref[half * 128:half * 128 + 128, :] = hits(column).astype(F32).astype(BF16)
        order_ref[256 + half * 128:384 + half * 128, :] = (part & (column < 64)).astype(F32).astype(BF16)
        order_ref[512 + half * 128:640 + half * 128, :] = (part & (column >= 64)).astype(F32).astype(BF16)
    lane = lax.broadcasted_iota(I32, (WINDOW, LANES), 1)
    row = lax.broadcasted_iota(I32, (WINDOW, LANES), 0)
    for s in range(8):
        group = jnp.bitwise_xor(hc, s)
        offset, size = offset_of(virt, group), size_of(virt, group)
        rows = pl.ds(pl.multiple_of(starts[s] - firsts[s], 16), WINDOW)
        keep = (lane < size) & (row < VIRT - starts[s])

        def emit(value, turn):
            block = pltpu.roll(value.astype(F32), turn, 1)[:, :LANES]
            block = jnp.where(keep, block, 0.0).astype(BF16)
            out_ref[:, s * MAIN:(s + 1) * MAIN] = block[:, :MAIN]
            out_ref[:, 8 * MAIN + s * 128:8 * MAIN + (s + 1) * 128] = block[:, MAIN:]

        copies[s].wait()

        @pl.when(offset < LAST)
        def _():
            start = pl.multiple_of(lax.div(offset, 128) * 128, 128)
            emit(windows[s, rows, pl.ds(start, SPAN)], lax.rem(SPAN - lax.rem(offset, 128), SPAN))

        @pl.when(offset >= LAST)
        def _():
            span[:, :384] = windows[s, rows, LAST:1536]
            span[:, 384:448] = windows[s, rows, 1536:1600]
            span[:, 448:] = jnp.zeros((WINDOW, 64), BF16)
            emit(span[...], lax.rem(SPAN - (offset - LAST), SPAN))


def terms_kernel(steps, meta_ref, t_ref, v_ref, *refs):
    outs, (stack, tails, syms, total) = refs[:-4], refs[-4:]
    virt = [meta_ref[g, 0] for g in range(8)]
    hc = col_irrep(virt)
    x, y = lax.axis_index("x"), lax.axis_index("y")
    for i, r in enumerate(steps):
        slot = lax.rem(x - y - r + 2 * NX, NX)
        part = t_ref[pl.ds(pl.multiple_of(slot * HALF, HALF), HALF), :]
        rows = slice(i * MAIN, i * MAIN + HALF)
        sym = jnp.broadcast_to(part[:, BMAX:BMAX + 1].astype(F32), (HALF, MAIN)).astype(BF16)
        for s in range(8):
            keep = sym == jnp.asarray(s, BF16)
            stack[rows, s * MAIN:(s + 1) * MAIN] = jnp.where(keep, part[:, :MAIN], jnp.zeros((), BF16))
        tails[rows, :] = part[:, MAIN:]
        syms[rows, :] = sym[:, :128]
    total[...] = lax.dot_general(v_ref[:, :8 * MAIN], stack[...], NT, preferred_element_type=F32)
    for s in range(8):

        @pl.when(size_of(virt, jnp.bitwise_xor(hc, s)) > MAIN)
        def _():
            rest = jnp.where(syms[...] == jnp.asarray(s, BF16), tails[...], jnp.zeros((), BF16))
            block = v_ref[:, 8 * MAIN + s * 128:8 * MAIN + (s + 1) * 128]
            total[...] += lax.dot_general(block, rest, NT, preferred_element_type=F32)

    lane = lax.broadcasted_iota(I32, (FOLD, 128), 1)
    for i in range(len(steps)):
        outs[i][:WINDOW, :] = total[:, i * MAIN:i * MAIN + 128].astype(BF16)
        part = total[:, i * MAIN + 128:(i + 1) * MAIN]
        outs[i][WINDOW:, :] = jnp.where(lane < 64, part[:FOLD], pltpu.roll(part[FOLD:], 64, 1)).astype(BF16)
    if 0 in steps:
        i = steps.index(0)
        one = (lax.broadcasted_iota(I32, (16, 128), 1) == 0).astype(F32).astype(BF16)
        sym = lax.dot_general(one, syms[i * MAIN:(i + 1) * MAIN, :], NT, preferred_element_type=F32)
        outs[-1][:16, :] = sym[:, :128].astype(BF16)
        outs[-1][16:, :] = jnp.where(lane[:16] < 64, sym[:, 128:], 0.0).astype(BF16)


def place_kernel(meta_ref, a0, a1, a2, a3, b0, b1, b2, b3, sym_a, sym_b, order_ref, out_ref, total, wide, sem):
    virt = [meta_ref[g, 0] for g in range(8)]
    ra = row_irrep(virt)
    syms = jnp.concatenate([sym_a[...], sym_b[...]], axis=1)
    sym = jnp.dot(syms[:16], order_ref[:256, :], preferred_element_type=F32)
    sym += jnp.dot(syms[16:], order_ref[256:512, :], preferred_element_type=F32)
    sym = sym.astype(BF16)
    for half, refs in enumerate(((a0, a1, a2, a3), (b0, b1, b2, b3))):
        value = refs[0][...].astype(F32)
        for ref in refs[1:]:
            value += ref[...].astype(F32)
        total[:, half * 128:(half + 1) * 128] = value.astype(BF16)
    value = jnp.dot(total[:WINDOW, :], order_ref[:256, :], preferred_element_type=F32)
    upper = jnp.dot(total[WINDOW:, :], order_ref[256:512, :], preferred_element_type=F32)
    lower = jnp.dot(total[WINDOW:, :], order_ref[512:, :], preferred_element_type=F32)
    value = (value + jnp.concatenate([upper, lower], axis=0)).astype(BF16)
    row = lax.broadcasted_iota(I32, (16, PORTION), 0)
    for group in range(8):
        offset = offset_of(virt, group)
        start = block_start(offset)
        mask = sym == jnp.bitwise_xor(ra, group).astype(F32).astype(BF16)
        kept = jnp.where(jnp.concatenate([mask] * (WINDOW // 16), axis=0), value, jnp.zeros((), BF16))
        head = wide[pl.ds(start, 16), :].astype(F32)
        wide[pl.ds(start, 16), :] = jnp.where(row < offset - start, head, kept[:16].astype(F32)).astype(BF16)
        wide[pl.ds(start + 16, WINDOW - 16), :] = kept[16:]
    copy = pltpu.make_async_copy(wide.at[pl.ds(0, VIRT), :], out_ref, sem)
    copy.start()
    copy.wait()


def shift(value, axis, size, by):
    return lax.ppermute(value, axis, [(i, (i + by) % size) for i in range(size)])


def call(kernel, specs, out, scratch=(), out_specs=None, flops=0, moved=0, limit=40):
    return pl.pallas_call(
        kernel,
        in_specs=specs,
        out_specs=out_specs or jax.tree.map(lambda _: VMEM, out),
        out_shape=out,
        scratch_shapes=list(scratch),
        compiler_params=pltpu.CompilerParams(vmem_limit_bytes=limit * 2**20),
        cost_estimate=pl.CostEstimate(flops=flops, bytes_accessed=moved, transcendentals=0),
    )


def shards(virt_sizes, occ_sizes, pair_ids, amplitudes, integrals):
    shape = jax.ShapeDtypeStruct
    packed = call(
        pack_kernel, [HBM] * 4, shape((HALF, LANES), BF16),
        [pltpu.SMEM((8,), I32), pltpu.SMEM((8,), I32), pltpu.SMEM((PAIRS,), I32), pltpu.VMEM((ROWS, VIRT), BF16),
         pltpu.VMEM((ROWS, 1536 + SPAN + 128), F32), pltpu.SemaphoreType.DMA((4,))],
        moved=300000, limit=64,
    )(virt_sizes, occ_sizes, pair_ids, amplitudes)
    mine = lax.all_to_all(packed, "z", 0, 0, tiled=True)
    across = [shift(mine, "x", NX, k) for k in (2, 1, 3)]
    blocks, order, meta, mine = call(
        blocks_kernel, [VMEM, HBM],
        (shape((WINDOW, 8 * LANES), BF16), shape((6 * 128, PORTION), BF16), shape((8, 128), I32),
         shape((HALF, LANES), BF16)),
        [pltpu.VMEM((8, 2 * WINDOW, VIRT), BF16), pltpu.VMEM((WINDOW, SPAN), BF16),
         pltpu.VMEM((16, 128), I32), pltpu.SemaphoreType.DMA((8,))], moved=16000000, limit=48,
    )(mine, integrals)
    own = jnp.concatenate([mine, across[1], across[0], across[2]], axis=0)
    other = shift(own, "c", NC, 1)
    tile, sym = shape((MESSAGE, 128), BF16), shape((32, 128), BF16)
    near, far = [], []
    for half in (own, other):
        sent = {}
        for steps, out in (((2,), (tile,)), ((1, 3, 0), (tile, tile, tile, sym))):
            columns = len(steps) * MAIN
            terms = call(
                functools.partial(terms_kernel, steps), [VMEM] * 3, out,
                [pltpu.VMEM((columns, 8 * MAIN), BF16), pltpu.VMEM((columns, 128), BF16),
                 pltpu.VMEM((columns, 128), BF16), pltpu.VMEM((WINDOW, columns), F32)],
                flops=2 * columns * WINDOW * 8 * MAIN, moved=4500000,
            )(meta, half, blocks)
            for r, term in zip(steps, terms):
                sent[r] = shift(term, "y", NY, r) if r else term
        near.append(terms[-1])
        far.append([sent[r] for r in range(NY)])
    out = call(
        place_kernel, [VMEM] * 12, shape((VIRT, PORTION), BF16),
        [pltpu.VMEM((MESSAGE, 2 * 128), BF16), pltpu.VMEM((VIRT + WINDOW, PORTION), BF16), pltpu.SemaphoreType.DMA],
        HBM, moved=2600000,
    )(meta, *far[0], *far[1], *near, order)
    return out.T


def solution(mesh):
    grid = Mesh(mesh.devices.reshape(NX, NZ, NC, NY), ("x", "z", "c", "y"))
    vp = ("x", "z", "c")
    in_specs = (P(), P(), P(), P(vp, "y"), P(vp, "y"))
    return jax.shard_map(shards, mesh=grid, in_specs=in_specs, out_specs=P("y", vp), check_vma=False)
```

time: 58.2 us -> 53.2 us (0.914)
  local copies, waits for them, and re-layouts: 2.08 us -> 0.09 us
  Pallas kernels: 15.2 us -> 13.9 us
  waiting for transfers between devices: 6.74 us -> 5.5 us
    pallas_call x5 -> x7, Pallas kernels: 15.2 us -> 13.9 us  [the longest x4 6.08 us: shards(): call(functools.partial(terms_kernel, steps), [VMEM] * 3, out, [pltpu.VMEM...]
    unnamed x7 -> x3, local copies, waits for them, and re-layouts: 1.35 us -> 0.07 us
    ppermute x10, waiting for transfers between devices: 6.74 us -> 5.5 us  [shift(): lax.ppermute(value, axis, [(i, (i + by) % size) for i in range(size)])]
    reshape x1 -> x0, local copies, waits for them, and re-layouts: 0.7 us -> none  [shards(): pair_ids.reshape(NY, PORTION)]
  transfers between devices with their start and end apart: 10 -> 10, of which waited for: 2 -> 3; matrix products, arithmetic and copies ran while one was open for 1% -> 0% of each run, Pallas kernels for 18% -> 20%
where the time goes in v3:
time: 53.2 us; the launch traced here: 53 us
  blocking collectives  16.9 us (32%)
  starting transfers between devices  16.3 us (31%)
  Pallas kernels  13.9 us (26%)
  waiting for transfers between devices  5.5 us (10%)
    all_to_all x1, blocking collectives, shards(): mine = lax.all_to_all(packed, 'z', 0, 0, tiled=True)  16.9 us
    ppermute x10, starting transfers between devices, shift(): lax.ppermute(value, axis, [(i, (i + by) % size) for i in range(size)])  16.3 us
    pallas_call x4, Pallas kernels, shards(): call(functools.partial(terms_kernel, steps), [VMEM] * 3, out, [pltpu.VMEM...  6.08 us
    ppermute x10, waiting for transfers between devices, shift(): lax.ppermute(value, axis, [(i, (i + by) % size) for i in range(size)])  5.5 us
    pallas_call x1, Pallas kernels, shards(): call(blocks_kernel, [VMEM, HBM], (shape((WINDOW, 8 * LANES), BF16), shape...  4.33 us
    pallas_call x1, Pallas kernels, shards(): call(pack_kernel, [HBM] * 4, shape((HALF, LANES), BF16), [pltpu.SMEM((8,)...  1.78 us
    pallas_call x1, Pallas kernels, shards(): call(place_kernel, [VMEM] * 12, shape((VIRT, PORTION), BF16), [pltpu.VMEM...  1.69 us
  transfers between devices with their start and end apart: 10, of which 3 were waited for; matrix products, arithmetic and copies ran while one was open for 0% of the time, Pallas kernels for 20%

profile of v3, /device:TPU:1, one launch (start us, length us, event | category | flops | bytes accessed | tf_op | source)
XLA Modules:
  0.0 53.0 jit_solution(8456035993718287437)
XLA Ops:
  0.0 1.8 %shard_map.55 = bf16[192,384]{1,0:T(8,128)(2,1)} custom-call(s32[8]{0:T(128)} %virt_hbm.1, s32[8]{0:T(128)} %occ_hbm.1, s32[1536]{0:T(1024)} %ids_hbm.1, bf16[24,1600]{1,0:T(8,128)(2,1)} %t_hbm.1), custom_call_target="tpu_custom_call" | custom-call | bytes 300000 | tf_op jit(solution)/shard_map/pallas_call | solution.py:260
  1.8 16.9 %all_to_all.11 = bf16[8,24,384]{2,1,0:T(8,128)(2,1)S(1)} all-to-all(bf16[8,24,384]{2,1,0:T(8,128)(2,1)} %bitcast.7), channel_id=1, replica_groups=mesh['x'=4,'z'=8,'c'=2,'y'=4] {'z'}, dimensions={0} | all-to-all | bytes 294912 | tf_op jit(solution)/shard_map/all_to_all | solution.py:266
  18.7 1.2 %collective-permute-start = (bf16[192,384]{1,0:T(8,128)(2,1)S(1)}, bf16[192,384]{1,0:T(8,128)(2,1)S(1)}, u32[]{:S(2)}, u32[]{:S(2)}) collective-permute-start(bf16[192,384]{1,0:T(8,128)(2,1)S(1)} %bitcast.3), channel_id=1, source_target_pairs={{0,64},{64,128},{128,192},{192,0},{1,65},{65,129},{129,193},{193,1... | collective-permute-start | bytes 442376 | tf_op jit(solution)/shard_map/ppermute | solution.py:243
  20.0 1.5 %collective-permute-start.2 = (bf16[192,384]{1,0:T(8,128)(2,1)S(1)}, bf16[192,384]{1,0:T(8,128)(2,1)S(1)}, u32[]{:S(2)}, u32[]{:S(2)}) collective-permute-start(bf16[192,384]{1,0:T(8,128)(2,1)S(1)} %bitcast.4), channel_id=1, source_target_pairs={{0,192},{64,0},{128,64},{192,128},{1,193},{65,1},{129,65},{193,129... | collective-permute-start | bytes 442376 | tf_op jit(solution)/shard_map/ppermute | solution.py:243
  21.4 1.5 %collective-permute-start.1 = (bf16[192,384]{1,0:T(8,128)(2,1)S(1)}, bf16[192,384]{1,0:T(8,128)(2,1)S(1)}, u32[]{:S(2)}, u32[]{:S(2)}) collective-permute-start(bf16[192,384]{1,0:T(8,128)(2,1)S(1)} %bitcast.5), channel_id=1, source_target_pairs={{0,128},{64,192},{128,0},{192,64},{1,129},{65,193},{129,1},{193,65... | collective-permute-start | bytes 442376 | tf_op jit(solution)/shard_map/ppermute | solution.py:243
  22.9 4.3 %shard_map.56 = (bf16[336,3072]{1,0:T(8,128)(2,1)S(1)}, bf16[768,384]{1,0:T(8,128)(2,1)S(1)}, s32[8,128]{1,0:T(8,128)S(1)}, bf16[192,384]{1,0:T(8,128)(2,1)S(1)}) custom-call(bf16[192,384]{1,0:T(8,128)(2,1)S(1)} %bitcast.6, bf16[1600,1600]{1,0:T(8,128)(2,1)} %v_hbm.1), custom_call_target="tpu_custom_call" | custom-call | bytes 16000000 | tf_op jit(solution)/shard_map/pallas_call | solution.py:268
  27.3 0.0 collective-permute-done
  27.4 0.2 collective-permute-done.1
  27.6 0.0 collective-permute-done.2
  27.7 3.6 %collective-permute-start.6 = (bf16[768,384]{1,0:T(8,128)(2,1)S(1)}, bf16[768,384]{1,0:T(8,128)(2,1)S(1)}, u32[]{:S(2)}, u32[]{:S(2)}) collective-permute-start(bf16[768,384]{1,0:T(8,128)(2,1)S(1)} %constant_dynamic-update-slice_fusion.t_ref), channel_id=1, source_target_pairs={{0,4},{4,0},{1,5},{5,1},{2,6},{6,2},{3,7},{7,3},{8,12},{12,8},{9,1... | collective-permute-start | bytes 1769480 | tf_op jit(solution)/shard_map/ppermute | solution.py:243
  31.2 1.0 %shard_map.58 = bf16[504,128]{1,0:T(8,128)(2,1)S(1)} custom-call(s32[8,128]{1,0:T(8,128)S(1)} %get-tuple-element.17.meta_ref, bf16[768,384]{1,0:T(8,128)(2,1)S(1)} %constant_dynamic-update-slice_fusion.t_ref, bf16[336,3072]{1,0:T(8,128)(2,1)S(1)} %get-tuple-element.19.v_ref), custom_call_target="tpu_custom_call" | custom-call | flops 352321536 | bytes 4500000 | tf_op jit(solution)/shard_map/pallas_call | solution.py:283
  32.3 3.0 %collective-permute-start.4 = (bf16[504,128]{1,0:T(8,128)(2,1)S(1)}, bf16[504,128]{1,0:T(8,128)(2,1)S(1)}, u32[]{:S(2)}, u32[]{:S(2)}) collective-permute-start(bf16[504,128]{1,0:T(8,128)(2,1)S(1)} %shard_map.58), channel_id=1, source_target_pairs={{0,2},{1,3},{2,0},{3,1},{4,6},{5,7},{6,4},{7,5},{8,10},{9,11},{10,... | collective-permute-start | bytes 387080 | tf_op jit(solution)/shard_map/ppermute | solution.py:243
  35.3 2.1 %shard_map.57 = (bf16[504,128]{1,0:T(8,128)(2,1)S(1)}, bf16[504,128]{1,0:T(8,128)(2,1)S(1)}, bf16[504,128]{1,0:T(8,128)(2,1)S(1)}, bf16[32,128]{1,0:T(8,128)(2,1)S(1)}) custom-call(s32[8,128]{1,0:T(8,128)S(1)} %get-tuple-element.17.meta_ref, bf16[768,384]{1,0:T(8,128)(2,1)S(1)} %constant_dynamic-update-slice_fusion.t_ref, ...), custom_call_target="tpu_custom_call" | custom-call | flops 1056964608 | bytes 4500000 | tf_op jit(solution)/shard_map/pallas_call | solution.py:283
  37.4 0.4 collective-permute-start.3
  37.8 2.3 %collective-permute-start.5 = (bf16[504,128]{1,0:T(8,128)(2,1)S(1)}, bf16[504,128]{1,0:T(8,128)(2,1)S(1)}, u32[]{:S(2)}, u32[]{:S(2)}) collective-permute-start(bf16[504,128]{1,0:T(8,128)(2,1)S(1)} %get-tuple-element.22), channel_id=1, source_target_pairs={{0,3},{1,0},{2,1},{3,2},{4,7},{5,4},{6,5},{7,6},{8,11},{9,8},{10,9... | collective-permute-start | bytes 387080 | tf_op jit(solution)/shard_map/ppermute | solution.py:243
  40.1 0.0 collective-permute-done.6.t_ref
  40.1 1.9 %shard_map.59 = (bf16[504,128]{1,0:T(8,128)(2,1)S(1)}, bf16[504,128]{1,0:T(8,128)(2,1)S(1)}, bf16[504,128]{1,0:T(8,128)(2,1)S(1)}, bf16[32,128]{1,0:T(8,128)(2,1)S(1)}) custom-call(s32[8,128]{1,0:T(8,128)S(1)} %get-tuple-element.17.meta_ref, bf16[768,384]{1,0:T(8,128)(2,1)S(1)} %collective-permute-done.6.t_ref, bf16[336,3072]{1,0:T(8,128)(2,1)S(1)} %get-tuple-element.19.v_ref), custom_call_target="tpu_custom_call" | custom-call | flops 1056964608 | bytes 4500000 | tf_op jit(solution)/shard_map/pallas_call | solution.py:283
  42.0 0.0 collective-permute-start.7
  42.1 2.7 %collective-permute-start.9 = (bf16[504,128]{1,0:T(8,128)(2,1)S(1)}, bf16[504,128]{1,0:T(8,128)(2,1)S(1)}, u32[]{:S(2)}, u32[]{:S(2)}) collective-permute-start(bf16[504,128]{1,0:T(8,128)(2,1)S(1)} %get-tuple-element.25), channel_id=1, source_target_pairs={{0,3},{1,0},{2,1},{3,2},{4,7},{5,4},{6,5},{7,6},{8,11},{9,8},{10,9... | collective-permute-start | bytes 387080 | tf_op jit(solution)/shard_map/ppermute | solution.py:243
  44.7 1.0 %shard_map.60 = bf16[504,128]{1,0:T(8,128)(2,1)S(1)} custom-call(s32[8,128]{1,0:T(8,128)S(1)} %get-tuple-element.17.meta_ref, bf16[768,384]{1,0:T(8,128)(2,1)S(1)} %collective-permute-done.6.t_ref, bf16[336,3072]{1,0:T(8,128)(2,1)S(1)} %get-tuple-element.19.v_ref), custom_call_target="tpu_custom_call" | custom-call | flops 352321536 | bytes 4500000 | tf_op jit(solution)/shard_map/pallas_call | solution.py:283
  45.8 0.0 collective-permute-done.4.a2
  45.8 0.1 collective-permute-start.8
  45.9 0.0 collective-permute-done.3.a1
  45.9 0.0 collective-permute-done.5.a3
  45.9 1.2 %collective-permute-done.7.b1 = bf16[504,128]{1,0:T(8,128)(2,1)S(1)} collective-permute-done((bf16[504,128]{1,0:T(8,128)(2,1)S(1)}, bf16[504,128]{1,0:T(8,128)(2,1)S(1)}, u32[]{:S(2)}, u32[]{:S(2)}) %collective-permute-start.7) | collective-permute-done | bytes 129056 | tf_op jit(solution)/shard_map/ppermute | solution.py:243
  47.1 0.0 collective-permute-done.9.b3
  47.1 4.1 %collective-permute-done.8.b2 = bf16[504,128]{1,0:T(8,128)(2,1)S(1)} collective-permute-done((bf16[504,128]{1,0:T(8,128)(2,1)S(1)}, bf16[504,128]{1,0:T(8,128)(2,1)S(1)}, u32[]{:S(2)}, u32[]{:S(2)}) %collective-permute-start.8) | collective-permute-done | bytes 129056 | tf_op jit(solution)/shard_map/ppermute | solution.py:243
  51.1 1.7 %shard_map.61 = bf16[1600,384]{1,0:T(8,128)(2,1)} custom-call(s32[8,128]{1,0:T(8,128)S(1)} %get-tuple-element.17.meta_ref, bf16[504,128]{1,0:T(8,128)(2,1)S(1)} %get-tuple-element.20.a0, bf16[504,128]{1,0:T(8,128)(2,1)S(1)} %collective-permute-done.3.a1, bf16[504,128]{1,0:T(8,128)(2,1)S(1)} %collective-permute-done.4.a2, ...), custom_call_target="tpu_custom_call" | custom-call | bytes 2600000 | tf_op jit(solution)/shard_map/pallas_call | solution.py:293
  (4 shorter events, 0.1 us)
Async XLA Ops:
  18.7 8.6 %collective-permute-start = (bf16[192,384]{1,0:T(8,128)(2,1)S(1)}, bf16[192,384]{1,0:T(8,128)(2,1)S(1)}, u32[]{:S(2)}, u32[]{:S(2)}) collective-permute-start(bf16[192,384]{1,0:T(8,128)(2,1)S(1)} %bitcast.3), channel_id=1, source_target_pairs={{0,64},{64,128},{128,192},{192,0},{1,65},{65,129},{129,193},{193,1... | collective-permute-start | bytes 442376 | tf_op jit(solution)/shard_map/ppermute | solution.py:243
  20.0 7.7 %collective-permute-start.2 = (bf16[192,384]{1,0:T(8,128)(2,1)S(1)}, bf16[192,384]{1,0:T(8,128)(2,1)S(1)}, u32[]{:S(2)}, u32[]{:S(2)}) collective-permute-start(bf16[192,384]{1,0:T(8,128)(2,1)S(1)} %bitcast.4), channel_id=1, source_target_pairs={{0,192},{64,0},{128,64},{192,128},{1,193},{65,1},{129,65},{193,129... | collective-permute-start | bytes 442376 | tf_op jit(solution)/shard_map/ppermute | solution.py:243
  21.4 6.2 %collective-permute-start.1 = (bf16[192,384]{1,0:T(8,128)(2,1)S(1)}, bf16[192,384]{1,0:T(8,128)(2,1)S(1)}, u32[]{:S(2)}, u32[]{:S(2)}) collective-permute-start(bf16[192,384]{1,0:T(8,128)(2,1)S(1)} %bitcast.5), channel_id=1, source_target_pairs={{0,128},{64,192},{128,0},{192,64},{1,129},{65,193},{129,1},{193,65... | collective-permute-start | bytes 442376 | tf_op jit(solution)/shard_map/ppermute | solution.py:243
  27.7 12.4 %collective-permute-start.6 = (bf16[768,384]{1,0:T(8,128)(2,1)S(1)}, bf16[768,384]{1,0:T(8,128)(2,1)S(1)}, u32[]{:S(2)}, u32[]{:S(2)}) collective-permute-start(bf16[768,384]{1,0:T(8,128)(2,1)S(1)} %constant_dynamic-update-slice_fusion.t_ref), channel_id=1, source_target_pairs={{0,4},{4,0},{1,5},{5,1},{2,6},{6,2},{3,7},{7,3},{8,12},{12,8},{9,1... | collective-permute-start | bytes 1769480 | tf_op jit(solution)/shard_map/ppermute | solution.py:243
  32.3 13.5 %collective-permute-start.4 = (bf16[504,128]{1,0:T(8,128)(2,1)S(1)}, bf16[504,128]{1,0:T(8,128)(2,1)S(1)}, u32[]{:S(2)}, u32[]{:S(2)}) collective-permute-start(bf16[504,128]{1,0:T(8,128)(2,1)S(1)} %shard_map.58), channel_id=1, source_target_pairs={{0,2},{1,3},{2,0},{3,1},{4,6},{5,7},{6,4},{7,5},{8,10},{9,11},{10,... | collective-permute-start | bytes 387080 | tf_op jit(solution)/shard_map/ppermute | solution.py:243
  37.4 8.5 %collective-permute-start.3 = (bf16[504,128]{1,0:T(8,128)(2,1)S(1)}, bf16[504,128]{1,0:T(8,128)(2,1)S(1)}, u32[]{:S(2)}, u32[]{:S(2)}) collective-permute-start(bf16[504,128]{1,0:T(8,128)(2,1)S(1)} %get-tuple-element.21), channel_id=1, source_target_pairs={{0,1},{1,2},{2,3},{3,0},{4,5},{5,6},{6,7},{7,4},{8,9},{9,10},{10,1... | collective-permute-start | bytes 387080 | tf_op jit(solution)/shard_map/ppermute | solution.py:243
  37.8 8.1 %collective-permute-start.5 = (bf16[504,128]{1,0:T(8,128)(2,1)S(1)}, bf16[504,128]{1,0:T(8,128)(2,1)S(1)}, u32[]{:S(2)}, u32[]{:S(2)}) collective-permute-start(bf16[504,128]{1,0:T(8,128)(2,1)S(1)} %get-tuple-element.22), channel_id=1, source_target_pairs={{0,3},{1,0},{2,1},{3,2},{4,7},{5,4},{6,5},{7,6},{8,11},{9,8},{10,9... | collective-permute-start | bytes 387080 | tf_op jit(solution)/shard_map/ppermute | solution.py:243
  42.0 5.0 %collective-permute-start.7 = (bf16[504,128]{1,0:T(8,128)(2,1)S(1)}, bf16[504,128]{1,0:T(8,128)(2,1)S(1)}, u32[]{:S(2)}, u32[]{:S(2)}) collective-permute-start(bf16[504,128]{1,0:T(8,128)(2,1)S(1)} %get-tuple-element.24), channel_id=1, source_target_pairs={{0,1},{1,2},{2,3},{3,0},{4,5},{5,6},{6,7},{7,4},{8,9},{9,10},{10,1... | collective-permute-start | bytes 387080 | tf_op jit(solution)/shard_map/ppermute | solution.py:243
  42.1 5.0 %collective-permute-start.9 = (bf16[504,128]{1,0:T(8,128)(2,1)S(1)}, bf16[504,128]{1,0:T(8,128)(2,1)S(1)}, u32[]{:S(2)}, u32[]{:S(2)}) collective-permute-start(bf16[504,128]{1,0:T(8,128)(2,1)S(1)} %get-tuple-element.25), channel_id=1, source_target_pairs={{0,3},{1,0},{2,1},{3,2},{4,7},{5,4},{6,5},{7,6},{8,11},{9,8},{10,9... | collective-permute-start | bytes 387080 | tf_op jit(solution)/shard_map/ppermute | solution.py:243
  45.8 5.4 %collective-permute-start.8 = (bf16[504,128]{1,0:T(8,128)(2,1)S(1)}, bf16[504,128]{1,0:T(8,128)(2,1)S(1)}, u32[]{:S(2)}, u32[]{:S(2)}) collective-permute-start(bf16[504,128]{1,0:T(8,128)(2,1)S(1)} %shard_map.60), channel_id=1, source_target_pairs={{0,2},{1,3},{2,0},{3,1},{4,6},{5,7},{6,4},{7,5},{8,10},{9,11},{10,... | collective-permute-start | bytes 387080 | tf_op jit(solution)/shard_map/ppermute | solution.py:243

commit v4 on v3

--- a/solution.py
+++ b/solution.py
@@ -20,8 +20,7 @@
 LANES = 384
 MAIN = 256
 WINDOW = 336
-FOLD = WINDOW // 2
-MESSAGE = WINDOW + FOLD
+MESSAGE = 3 * WINDOW
 SPAN = 512
 LAST = 1152
 META = BMAX - MAIN + 8
@@ -130,19 +129,14 @@
     for g in range(8):
         meta = jnp.where(row == g, virt[g], meta)
     meta_ref[...] = meta
-    column = lax.broadcasted_iota(I32, (128, PORTION), 0)
-    target = lax.broadcasted_iota(I32, (128, PORTION), 1)
-    for half in range(2):
-        core = jnp.bitwise_xor(lax.axis_index("c"), half)
-
-        def hits(position):
-            z = lax.shift_right_logical(position * 2731, 16)
-            return (z * NC + core) * ROWS + (position - z * ROWS) == target
-
-        part = hits(jnp.bitwise_and(column, 63) + 128)
-        order_ref[half * 128:half * 128 + 128, :] = hits(column).astype(F32).astype(BF16)
-        order_ref[256 + half * 128:384 + half * 128, :] = (part & (column < 64)).astype(F32).astype(BF16)
-        order_ref[512 + half * 128:640 + half * 128, :] = (part & (column >= 64)).astype(F32).astype(BF16)
+    column = lax.broadcasted_iota(I32, (PORTION, PORTION), 0)
+    target = lax.broadcasted_iota(I32, (PORTION, PORTION), 1)
+    tail = column >= 2 * 128
+    other = jnp.bitwise_and(jnp.where(tail, lax.shift_right_logical(column, 6), lax.shift_right_logical(column, 7)), 1)
+    position = jnp.where(tail, 128 + jnp.bitwise_and(column, 63), jnp.bitwise_and(column, 127))
+    core = jnp.bitwise_xor(lax.axis_index("c"), other)
+    z = lax.shift_right_logical(position * 2731, 16)
+    order_ref[...] = ((z * NC + core) * ROWS + (position - z * ROWS) == target).astype(F32).astype(BF16)
     lane = lax.broadcasted_iota(I32, (WINDOW, LANES), 1)
     row = lax.broadcasted_iota(I32, (WINDOW, LANES), 0)
     for s in range(8):
@@ -172,14 +166,15 @@
             emit(span[...], lax.rem(SPAN - (offset - LAST), SPAN))
 
 
-def terms_kernel(steps, meta_ref, t_ref, v_ref, *refs):
-    outs, (stack, tails, syms, total) = refs[:-4], refs[-4:]
+def portion_rows(t_ref, r):
+    slot = lax.rem(lax.axis_index("x") - lax.axis_index("y") - r + 2 * NX, NX)
+    return t_ref[pl.ds(pl.multiple_of(slot * HALF, HALF), HALF), :]
+
+
+def multiply(meta_ref, v_ref, parts, stack, tails, syms, total):
     virt = [meta_ref[g, 0] for g in range(8)]
     hc = col_irrep(virt)
-    x, y = lax.axis_index("x"), lax.axis_index("y")
-    for i, r in enumerate(steps):
-        slot = lax.rem(x - y - r + 2 * NX, NX)
-        part = t_ref[pl.ds(pl.multiple_of(slot * HALF, HALF), HALF), :]
+    for i, part in enumerate(parts):
         rows = slice(i * MAIN, i * MAIN + HALF)
         sym = jnp.broadcast_to(part[:, BMAX:BMAX + 1].astype(F32), (HALF, MAIN)).astype(BF16)
         for s in range(8):
@@ -196,35 +191,55 @@
             block = v_ref[:, 8 * MAIN + s * 128:8 * MAIN + (s + 1) * 128]
             total[...] += lax.dot_general(block, rest, NT, preferred_element_type=F32)
 
-    lane = lax.broadcasted_iota(I32, (FOLD, 128), 1)
-    for i in range(len(steps)):
-        outs[i][:WINDOW, :] = total[:, i * MAIN:i * MAIN + 128].astype(BF16)
-        part = total[:, i * MAIN + 128:(i + 1) * MAIN]
-        outs[i][WINDOW:, :] = jnp.where(lane < 64, part[:FOLD], pltpu.roll(part[FOLD:], 64, 1)).astype(BF16)
-    if 0 in steps:
-        i = steps.index(0)
-        one = (lax.broadcasted_iota(I32, (16, 128), 1) == 0).astype(F32).astype(BF16)
-        sym = lax.dot_general(one, syms[i * MAIN:(i + 1) * MAIN, :], NT, preferred_element_type=F32)
-        outs[-1][:16, :] = sym[:, :128].astype(BF16)
-        outs[-1][16:, :] = jnp.where(lane[:16] < 64, sym[:, 128:], 0.0).astype(BF16)
-
-
-def place_kernel(meta_ref, a0, a1, a2, a3, b0, b1, b2, b3, sym_a, sym_b, order_ref, out_ref, total, wide, sem):
+
+def own_kernel(steps, meta_ref, t_ref, v_ref, *refs):
+    outs, scratch = refs[:-4], refs[-4:]
+    multiply(meta_ref, v_ref, [portion_rows(t_ref, r) for r in steps], *scratch)
+    total = scratch[-1]
+    for i, out_ref in enumerate(outs):
+        out_ref[:WINDOW, :] = total[:, i * MAIN:i * MAIN + 128].astype(BF16)
+        out_ref[WINDOW:, :] = total[:, i * MAIN + 128:(i + 1) * MAIN].astype(BF16)
+
+
+def other_kernel(steps, after, meta_ref, t_ref, v_ref, *refs):
+    refs = refs[after:]
+    n = len(steps)
+    mine, outs, scratch = refs[:n], refs[n:2 * n], refs[2 * n:]
+    multiply(meta_ref, v_ref, [portion_rows(t_ref, r) for r in steps], *scratch)
+    total = scratch[-1]
+    lane = lax.broadcasted_iota(I32, (WINDOW, 128), 1)
+    for i, (mine_ref, out_ref) in enumerate(zip(mine, outs)):
+        out_ref[:WINDOW, :] = mine_ref[:WINDOW, :]
+        out_ref[WINDOW:2 * WINDOW, :] = total[:, i * MAIN:i * MAIN + 128].astype(BF16)
+        tail = pltpu.roll(total[:, i * MAIN + 128:(i + 1) * MAIN], 64, 1)
+        out_ref[2 * WINDOW:, :] = jnp.where(lane < 64, mine_ref[WINDOW:, :].astype(F32), tail).astype(BF16)
+
+
+def stay_kernel(meta_ref, own_ref, other_ref, v_ref, out_ref, sym_ref, *scratch):
+    multiply(meta_ref, v_ref, [portion_rows(own_ref, 0), portion_rows(other_ref, 0)], *scratch)
+    syms, total = scratch[-2:]
+    lane = lax.broadcasted_iota(I32, (WINDOW, 128), 1)
+    out_ref[:WINDOW, :] = total[:, :128].astype(BF16)
+    out_ref[WINDOW:2 * WINDOW, :] = total[:, MAIN:MAIN + 128].astype(BF16)
+    tail = jnp.where(lane < 64, total[:, 128:MAIN], pltpu.roll(total[:, MAIN + 128:], 64, 1))
+    out_ref[2 * WINDOW:, :] = tail.astype(BF16)
+    one = (lane[:16] == 0).astype(F32).astype(BF16)
+    sym = lax.dot_general(one, syms[...], NT, preferred_element_type=F32)
+    sym_ref[:, :128] = sym[:, :128].astype(BF16)
+    sym_ref[:, 128:256] = sym[:, MAIN:MAIN + 128].astype(BF16)
+    tail = jnp.where(lane[:16] < 64, sym[:, 128:MAIN], pltpu.roll(sym[:, MAIN + 128:], 64, 1))
+    sym_ref[:, 256:] = tail.astype(BF16)
+
+
+def place_kernel(meta_ref, a_ref, b_ref, c_ref, d_ref, sym_ref, order_ref, out_ref, total, wide, sem):
     virt = [meta_ref[g, 0] for g in range(8)]
     ra = row_irrep(virt)
-    syms = jnp.concatenate([sym_a[...], sym_b[...]], axis=1)
-    sym = jnp.dot(syms[:16], order_ref[:256, :], preferred_element_type=F32)
-    sym += jnp.dot(syms[16:], order_ref[256:512, :], preferred_element_type=F32)
-    sym = sym.astype(BF16)
-    for half, refs in enumerate(((a0, a1, a2, a3), (b0, b1, b2, b3))):
-        value = refs[0][...].astype(F32)
-        for ref in refs[1:]:
-            value += ref[...].astype(F32)
-        total[:, half * 128:(half + 1) * 128] = value.astype(BF16)
-    value = jnp.dot(total[:WINDOW, :], order_ref[:256, :], preferred_element_type=F32)
-    upper = jnp.dot(total[WINDOW:, :], order_ref[256:512, :], preferred_element_type=F32)
-    lower = jnp.dot(total[WINDOW:, :], order_ref[512:, :], preferred_element_type=F32)
-    value = (value + jnp.concatenate([upper, lower], axis=0)).astype(BF16)
+    sym = jnp.dot(sym_ref[...], order_ref[...], preferred_element_type=F32).astype(BF16)
+    for i in range(3):
+        rows = slice(i * WINDOW, (i + 1) * WINDOW)
+        value = a_ref[rows, :].astype(F32) + b_ref[rows, :].astype(F32) + c_ref[rows, :].astype(F32)
+        total[:, i * 128:(i + 1) * 128] = (value + d_ref[rows, :].astype(F32)).astype(BF16)
+    value = jnp.dot(total[...], order_ref[...], preferred_element_type=F32).astype(BF16)
     row = lax.broadcasted_iota(I32, (16, PORTION), 0)
     for group in range(8):
         offset = offset_of(virt, group)
@@ -267,34 +282,42 @@
     across = [shift(mine, "x", NX, k) for k in (2, 1, 3)]
     blocks, order, meta, mine = call(
         blocks_kernel, [VMEM, HBM],
-        (shape((WINDOW, 8 * LANES), BF16), shape((6 * 128, PORTION), BF16), shape((8, 128), I32),
+        (shape((WINDOW, 8 * LANES), BF16), shape((PORTION, PORTION), BF16), shape((8, 128), I32),
          shape((HALF, LANES), BF16)),
         [pltpu.VMEM((8, 2 * WINDOW, VIRT), BF16), pltpu.VMEM((WINDOW, SPAN), BF16),
          pltpu.VMEM((16, 128), I32), pltpu.SemaphoreType.DMA((8,))], moved=16000000, limit=48,
     )(mine, integrals)
     own = jnp.concatenate([mine, across[1], across[0], across[2]], axis=0)
     other = shift(own, "c", NC, 1)
-    tile, sym = shape((MESSAGE, 128), BF16), shape((32, 128), BF16)
-    near, far = [], []
-    for half in (own, other):
-        sent = {}
-        for steps, out in (((2,), (tile,)), ((1, 3, 0), (tile, tile, tile, sym))):
-            columns = len(steps) * MAIN
-            terms = call(
-                functools.partial(terms_kernel, steps), [VMEM] * 3, out,
-                [pltpu.VMEM((columns, 8 * MAIN), BF16), pltpu.VMEM((columns, 128), BF16),
-                 pltpu.VMEM((columns, 128), BF16), pltpu.VMEM((WINDOW, columns), F32)],
-                flops=2 * columns * WINDOW * 8 * MAIN, moved=4500000,
-            )(meta, half, blocks)
-            for r, term in zip(steps, terms):
-                sent[r] = shift(term, "y", NY, r) if r else term
-        near.append(terms[-1])
-        far.append([sent[r] for r in range(NY)])
+    tile, part = shape((MESSAGE, 128), BF16), shape((2 * WINDOW, 128), BF16)
+
+    def scratch(columns):
+        return [pltpu.VMEM((columns, 8 * MAIN), BF16), pltpu.VMEM((columns, 128), BF16),
+                pltpu.VMEM((columns, 128), BF16), pltpu.VMEM((WINDOW, columns), F32)]
+
+    def cost(columns):
+        return dict(flops=2 * columns * WINDOW * 8 * MAIN, moved=4000000)
+
+    two, plus, minus = call(
+        functools.partial(own_kernel, (2, 1, 3)), [VMEM] * 3, (part,) * 3, scratch(3 * MAIN), **cost(3 * MAIN)
+    )(meta, own, blocks)
+    far, terms = [], ()
+    for steps, mine in (((2,), (two,)), ((1, 3), (plus, minus))):
+        columns = len(steps) * MAIN
+        operands = (meta, other, blocks, *terms, *mine)
+        terms = call(
+            functools.partial(other_kernel, steps, len(terms)), [VMEM] * len(operands), (tile,) * len(steps),
+            scratch(columns), **cost(columns)
+        )(*operands)
+        far += [shift(term, "y", NY, r) for r, term in zip(steps, terms)]
+    stay, sym = call(
+        stay_kernel, [VMEM] * 4, (tile, shape((16, PORTION), BF16)), scratch(2 * MAIN), flops=20*10**9
+    )(meta, own, other, blocks)
     out = call(
-        place_kernel, [VMEM] * 12, shape((VIRT, PORTION), BF16),
-        [pltpu.VMEM((MESSAGE, 2 * 128), BF16), pltpu.VMEM((VIRT + WINDOW, PORTION), BF16), pltpu.SemaphoreType.DMA],
+        place_kernel, [VMEM] * 7, shape((VIRT, PORTION), BF16),
+        [pltpu.VMEM((WINDOW, PORTION), BF16), pltpu.VMEM((VIRT + WINDOW, PORTION), BF16), pltpu.SemaphoreType.DMA],
         HBM, moved=2600000,
-    )(meta, *far[0], *far[1], *near, order)
+    )(meta, stay, *far, sym, order)
     return out.T
 
 

time: 53.2 us -> 51.7 us (0.972)
  starting transfers between devices: 16.3 us -> 13.5 us
  waiting for transfers between devices: 5.5 us -> 6.74 us
    ppermute x10 -> x7, starting transfers between devices: 16.3 us -> 13.5 us  [shift(): lax.ppermute(value, axis, [(i, (i + by) % size) for i in range(size)])]
    ppermute x10 -> x7, waiting for transfers between devices: 5.5 us -> 6.74 us  [shift(): lax.ppermute(value, axis, [(i, (i + by) % size) for i in range(size)])]
  transfers between devices with their start and end apart: 10 -> 7, of which waited for: 3 -> 2; matrix products, arithmetic and copies ran while one was open for 0% -> 0% of each run, Pallas kernels for 20% -> 18%
where the time goes in v4:
time: 51.7 us; the launch traced here: 51.5 us
  blocking collectives  16.9 us (33%)
  Pallas kernels  13.9 us (27%)
  starting transfers between devices  13.5 us (26%)
  waiting for transfers between devices  6.74 us (13%)
    all_to_all x1, blocking collectives, shards(): mine = lax.all_to_all(packed, 'z', 0, 0, tiled=True)  16.9 us
    ppermute x7, starting transfers between devices, shift(): lax.ppermute(value, axis, [(i, (i + by) % size) for i in range(size)])  13.5 us
    ppermute x7, waiting for transfers between devices, shift(): lax.ppermute(value, axis, [(i, (i + by) % size) for i in range(size)])  6.74 us
    pallas_call x1, Pallas kernels, shards(): call(blocks_kernel, [VMEM, HBM], (shape((WINDOW, 8 * LANES), BF16), shape...  4.27 us
    pallas_call x2, Pallas kernels, shards(): call(functools.partial(other_kernel, steps, len(terms)), [VMEM] * len(ope...  2.54 us
    pallas_call x1, Pallas kernels, shards(): call(functools.partial(own_kernel, (2, 1, 3)), [VMEM] * 3, (part,) * 3, s...  2.04 us
    pallas_call x1, Pallas kernels, shards(): call(pack_kernel, [HBM] * 4, shape((HALF, LANES), BF16), [pltpu.SMEM((8,)...  1.78 us
    pallas_call x1, Pallas kernels, shards(): call(place_kernel, [VMEM] * 7, shape((VIRT, PORTION), BF16), [pltpu.VMEM(...  1.68 us
  transfers between devices with their start and end apart: 7, of which 2 were waited for; matrix products, arithmetic and copies ran while one was open for 0% of the time, Pallas kernels for 18%

profile of v4, /device:TPU:1, one launch (start us, length us, event | category | flops | bytes accessed | tf_op | source)
XLA Modules:
  0.0 51.5 jit_solution(1617247591646755811)
XLA Ops:
  0.0 1.8 %shard_map.55 = bf16[192,384]{1,0:T(8,128)(2,1)} custom-call(s32[8]{0:T(128)} %virt_hbm.1, s32[8]{0:T(128)} %occ_hbm.1, s32[1536]{0:T(1024)} %ids_hbm.1, bf16[24,1600]{1,0:T(8,128)(2,1)} %t_hbm.1), custom_call_target="tpu_custom_call" | custom-call | bytes 300000 | tf_op jit(solution)/shard_map/pallas_call | solution.py:275
  1.8 16.9 %all_to_all.11 = bf16[8,24,384]{2,1,0:T(8,128)(2,1)S(1)} all-to-all(bf16[8,24,384]{2,1,0:T(8,128)(2,1)} %bitcast.7), channel_id=1, replica_groups=mesh['x'=4,'z'=8,'c'=2,'y'=4] {'z'}, dimensions={0} | all-to-all | bytes 294912 | tf_op jit(solution)/shard_map/all_to_all | solution.py:281
  18.7 1.2 %collective-permute-start = (bf16[192,384]{1,0:T(8,128)(2,1)S(1)}, bf16[192,384]{1,0:T(8,128)(2,1)S(1)}, u32[]{:S(2)}, u32[]{:S(2)}) collective-permute-start(bf16[192,384]{1,0:T(8,128)(2,1)S(1)} %bitcast.3), channel_id=1, source_target_pairs={{0,64},{64,128},{128,192},{192,0},{1,65},{65,129},{129,193},{193,1... | collective-permute-start | bytes 442376 | tf_op jit(solution)/shard_map/ppermute | solution.py:258
  20.0 1.5 %collective-permute-start.2 = (bf16[192,384]{1,0:T(8,128)(2,1)S(1)}, bf16[192,384]{1,0:T(8,128)(2,1)S(1)}, u32[]{:S(2)}, u32[]{:S(2)}) collective-permute-start(bf16[192,384]{1,0:T(8,128)(2,1)S(1)} %bitcast.4), channel_id=1, source_target_pairs={{0,192},{64,0},{128,64},{192,128},{1,193},{65,1},{129,65},{193,129... | collective-permute-start | bytes 442376 | tf_op jit(solution)/shard_map/ppermute | solution.py:258
  21.4 1.5 %collective-permute-start.1 = (bf16[192,384]{1,0:T(8,128)(2,1)S(1)}, bf16[192,384]{1,0:T(8,128)(2,1)S(1)}, u32[]{:S(2)}, u32[]{:S(2)}) collective-permute-start(bf16[192,384]{1,0:T(8,128)(2,1)S(1)} %bitcast.5), channel_id=1, source_target_pairs={{0,128},{64,192},{128,0},{192,64},{1,129},{65,193},{129,1},{193,65... | collective-permute-start | bytes 442376 | tf_op jit(solution)/shard_map/ppermute | solution.py:258
  22.9 4.3 %shard_map.56 = (bf16[336,3072]{1,0:T(8,128)(2,1)S(1)}, bf16[384,384]{1,0:T(8,128)(2,1)S(1)}, s32[8,128]{1,0:T(8,128)S(1)}, bf16[192,384]{1,0:T(8,128)(2,1)S(1)}) custom-call(bf16[192,384]{1,0:T(8,128)(2,1)S(1)} %bitcast.6, bf16[1600,1600]{1,0:T(8,128)(2,1)} %v_hbm.1), custom_call_target="tpu_custom_call" | custom-call | bytes 16000000 | tf_op jit(solution)/shard_map/pallas_call | solution.py:283
  27.3 0.0 collective-permute-done
  27.3 0.3 collective-permute-done.1
  27.6 0.0 collective-permute-done.2
  27.7 3.6 %collective-permute-start.3 = (bf16[768,384]{1,0:T(8,128)(2,1)S(1)}, bf16[768,384]{1,0:T(8,128)(2,1)S(1)}, u32[]{:S(2)}, u32[]{:S(2)}) collective-permute-start(bf16[768,384]{1,0:T(8,128)(2,1)S(1)} %constant_dynamic-update-slice_fusion.own_ref.t_ref), channel_id=1, source_target_pairs={{0,4},{4,0},{1,5},{5,1},{2,6},{6,2},{3,7},{7,3},{8,12},{12,8},{9,1... | collective-permute-start | bytes 1769480 | tf_op jit(solution)/shard_map/ppermute | solution.py:258
  31.2 2.0 %shard_map.58 = (bf16[672,128]{1,0:T(8,128)(2,1)S(1)}, bf16[672,128]{1,0:T(8,128)(2,1)S(1)}, bf16[672,128]{1,0:T(8,128)(2,1)S(1)}) custom-call(s32[8,128]{1,0:T(8,128)S(1)} %get-tuple-element.16.meta_ref, bf16[768,384]{1,0:T(8,128)(2,1)S(1)} %constant_dynamic-update-slice_fusion.own_ref.t_ref, bf16[336,3072]{1,0:T(8,128)(2,1)S(1)} %get-tuple-element.18.v_ref), custom_call_target="tpu_custom_call" | custom-call | flops 1056964608 | bytes 4000000 | tf_op jit(solution)/shard_map/pallas_call | solution.py:301
  33.3 0.0 collective-permute-done.3.other_ref.t_ref
  33.3 1.1 %shard_map.59.refs_0_ = bf16[1008,128]{1,0:T(8,128)(2,1)S(1)} custom-call(s32[8,128]{1,0:T(8,128)S(1)} %get-tuple-element.16.meta_ref, bf16[768,384]{1,0:T(8,128)(2,1)S(1)} %collective-permute-done.3.other_ref.t_ref, bf16[336,3072]{1,0:T(8,128)(2,1)S(1)} %get-tuple-element.18.v_ref, bf16[672,128]{1,0:T(8,128)(2,1)S(1)} %get-tuple-element.20.refs_0_), custom_call_target="tpu_custom_call" | custom-call | flops 352321536 | bytes 4000000 | tf_op jit(solution)/shard_map/pallas_call | solution.py:308
  34.4 3.0 %collective-permute-start.4 = (bf16[1008,128]{1,0:T(8,128)(2,1)S(1)}, bf16[1008,128]{1,0:T(8,128)(2,1)S(1)}, u32[]{:S(2)}, u32[]{:S(2)}) collective-permute-start(bf16[1008,128]{1,0:T(8,128)(2,1)S(1)} %shard_map.59.refs_0_), channel_id=1, source_target_pairs={{0,2},{1,3},{2,0},{3,1},{4,6},{5,7},{6,4},{7,5},{8,10},{9,11},{10,... | collective-permute-start | bytes 774152 | tf_op jit(solution)/shard_map/ppermute | solution.py:258
  37.3 1.5 %shard_map.60 = (bf16[1008,128]{1,0:T(8,128)(2,1)S(1)}, bf16[1008,128]{1,0:T(8,128)(2,1)S(1)}) custom-call(s32[8,128]{1,0:T(8,128)S(1)} %get-tuple-element.16.meta_ref, bf16[768,384]{1,0:T(8,128)(2,1)S(1)} %collective-permute-done.3.other_ref.t_ref, bf16[336,3072]{1,0:T(8,128)(2,1)S(1)} %get-tuple-element.18.v_ref, bf16[1008,128]{1,0:T(8,128)(2,1)S(1)} %shard_map.59.refs_0_, ...), custom_call_target="tpu_custom_call" | custom-call | flops 704643072 | bytes 4000000 | tf_op jit(solution)/shard_map/pallas_call | solution.py:308
  38.8 0.5 collective-permute-start.5
  39.3 2.3 %collective-permute-start.6 = (bf16[1008,128]{1,0:T(8,128)(2,1)S(1)}, bf16[1008,128]{1,0:T(8,128)(2,1)S(1)}, u32[]{:S(2)}, u32[]{:S(2)}) collective-permute-start(bf16[1008,128]{1,0:T(8,128)(2,1)S(1)} %get-tuple-element.24), channel_id=1, source_target_pairs={{0,3},{1,0},{2,1},{3,2},{4,7},{5,4},{6,5},{7,6},{8,11},{9,8},{10,9... | collective-permute-start | bytes 774152 | tf_op jit(solution)/shard_map/ppermute | solution.py:258
  41.6 1.6 %shard_map.57 = (bf16[1008,128]{1,0:T(8,128)(2,1)S(1)}, bf16[16,384]{1,0:T(8,128)(2,1)S(1)}) custom-call(s32[8,128]{1,0:T(8,128)S(1)} %get-tuple-element.16.meta_ref, bf16[768,384]{1,0:T(8,128)(2,1)S(1)} %constant_dynamic-update-slice_fusion.own_ref.t_ref, bf16[768,384]{1,0:T(8,128)(2,1)S(1)} %collective-permute-done.3.other_ref.t_ref, ...), custom_call_target="tpu_custom_call" | custom-call | flops 20000000000 | tf_op jit(solution)/shard_map/pallas_call | solution.py:313
  43.2 6.4 %collective-permute-done.5.c_ref = bf16[1008,128]{1,0:T(8,128)(2,1)S(1)} collective-permute-done((bf16[1008,128]{1,0:T(8,128)(2,1)S(1)}, bf16[1008,128]{1,0:T(8,128)(2,1)S(1)}, u32[]{:S(2)}, u32[]{:S(2)}) %collective-permute-start.5) | collective-permute-done | bytes 258080 | tf_op jit(solution)/shard_map/ppermute | solution.py:258
  49.6 0.0 collective-permute-done.6.d_ref
  49.6 0.0 collective-permute-done.4.b_ref
  49.6 1.7 %shard_map.61 = bf16[1600,384]{1,0:T(8,128)(2,1)} custom-call(s32[8,128]{1,0:T(8,128)S(1)} %get-tuple-element.16.meta_ref, bf16[1008,128]{1,0:T(8,128)(2,1)S(1)} %get-tuple-element.19.a_ref, bf16[1008,128]{1,0:T(8,128)(2,1)S(1)} %collective-permute-done.4.b_ref, bf16[1008,128]{1,0:T(8,128)(2,1)S(1)} %collective-permute-done.5.c_ref, ...), custom_call_target="tpu_custom_call" | custom-call | bytes 2600000 | tf_op jit(solution)/shard_map/pallas_call | solution.py:316
  (4 shorter events, 0.1 us)
Async XLA Ops:
  18.7 8.5 %collective-permute-start = (bf16[192,384]{1,0:T(8,128)(2,1)S(1)}, bf16[192,384]{1,0:T(8,128)(2,1)S(1)}, u32[]{:S(2)}, u32[]{:S(2)}) collective-permute-start(bf16[192,384]{1,0:T(8,128)(2,1)S(1)} %bitcast.3), channel_id=1, source_target_pairs={{0,64},{64,128},{128,192},{192,0},{1,65},{65,129},{129,193},{193,1... | collective-permute-start | bytes 442376 | tf_op jit(solution)/shard_map/ppermute | solution.py:258
  20.0 7.7 %collective-permute-start.2 = (bf16[192,384]{1,0:T(8,128)(2,1)S(1)}, bf16[192,384]{1,0:T(8,128)(2,1)S(1)}, u32[]{:S(2)}, u32[]{:S(2)}) collective-permute-start(bf16[192,384]{1,0:T(8,128)(2,1)S(1)} %bitcast.4), channel_id=1, source_target_pairs={{0,192},{64,0},{128,64},{192,128},{1,193},{65,1},{129,65},{193,129... | collective-permute-start | bytes 442376 | tf_op jit(solution)/shard_map/ppermute | solution.py:258
  21.4 6.2 %collective-permute-start.1 = (bf16[192,384]{1,0:T(8,128)(2,1)S(1)}, bf16[192,384]{1,0:T(8,128)(2,1)S(1)}, u32[]{:S(2)}, u32[]{:S(2)}) collective-permute-start(bf16[192,384]{1,0:T(8,128)(2,1)S(1)} %bitcast.5), channel_id=1, source_target_pairs={{0,128},{64,192},{128,0},{192,64},{1,129},{65,193},{129,1},{193,65... | collective-permute-start | bytes 442376 | tf_op jit(solution)/shard_map/ppermute | solution.py:258
  27.7 5.6 %collective-permute-start.3 = (bf16[768,384]{1,0:T(8,128)(2,1)S(1)}, bf16[768,384]{1,0:T(8,128)(2,1)S(1)}, u32[]{:S(2)}, u32[]{:S(2)}) collective-permute-start(bf16[768,384]{1,0:T(8,128)(2,1)S(1)} %constant_dynamic-update-slice_fusion.own_ref.t_ref), channel_id=1, source_target_pairs={{0,4},{4,0},{1,5},{5,1},{2,6},{6,2},{3,7},{7,3},{8,12},{12,8},{9,1... | collective-permute-start | bytes 1769480 | tf_op jit(solution)/shard_map/ppermute | solution.py:258
  34.4 15.3 %collective-permute-start.4 = (bf16[1008,128]{1,0:T(8,128)(2,1)S(1)}, bf16[1008,128]{1,0:T(8,128)(2,1)S(1)}, u32[]{:S(2)}, u32[]{:S(2)}) collective-permute-start(bf16[1008,128]{1,0:T(8,128)(2,1)S(1)} %shard_map.59.refs_0_), channel_id=1, source_target_pairs={{0,2},{1,3},{2,0},{3,1},{4,6},{5,7},{6,4},{7,5},{8,10},{9,11},{10,... | collective-permute-start | bytes 774152 | tf_op jit(solution)/shard_map/ppermute | solution.py:258
  38.8 10.8 %collective-permute-start.5 = (bf16[1008,128]{1,0:T(8,128)(2,1)S(1)}, bf16[1008,128]{1,0:T(8,128)(2,1)S(1)}, u32[]{:S(2)}, u32[]{:S(2)}) collective-permute-start(bf16[1008,128]{1,0:T(8,128)(2,1)S(1)} %get-tuple-element.23), channel_id=1, source_target_pairs={{0,1},{1,2},{2,3},{3,0},{4,5},{5,6},{6,7},{7,4},{8,9},{9,10},{10,1... | collective-permute-start | bytes 774152 | tf_op jit(solution)/shard_map/ppermute | solution.py:258
  39.3 10.3 %collective-permute-start.6 = (bf16[1008,128]{1,0:T(8,128)(2,1)S(1)}, bf16[1008,128]{1,0:T(8,128)(2,1)S(1)}, u32[]{:S(2)}, u32[]{:S(2)}) collective-permute-start(bf16[1008,128]{1,0:T(8,128)(2,1)S(1)} %get-tuple-element.24), channel_id=1, source_target_pairs={{0,3},{1,0},{2,1},{3,2},{4,7},{5,4},{6,5},{7,6},{8,11},{9,8},{10,9... | collective-permute-start | bytes 774152 | tf_op jit(solution)/shard_map/ppermute | solution.py:258

commit v5 on v4

--- a/solution.py
+++ b/solution.py
@@ -19,6 +19,8 @@
 PORTION = NC * HALF
 LANES = 384
 MAIN = 256
+TAIL = BMAX - MAIN
+DEPTH = 8 * BMAX
 WINDOW = 336
 MESSAGE = 3 * WINDOW
 SPAN = 512
@@ -124,10 +126,12 @@
     for copy in copies:
         copy.start()
     copy_ref[...] = mine_ref[...]
-    row = lax.broadcasted_iota(I32, (8, 128), 0)
+    row, lane = lax.broadcasted_iota(I32, (8, 128), 0), lax.broadcasted_iota(I32, (8, 128), 1)
     meta = jnp.zeros((8, 128), I32)
     for g in range(8):
-        meta = jnp.where(row == g, virt[g], meta)
+        first = offset_of(virt, g)
+        for i, value in enumerate((first, block_start(first), jnp.bitwise_xor(ra, g))):
+            meta = jnp.where((row == g) & (lane == i), value, meta)
     meta_ref[...] = meta
     column = lax.broadcasted_iota(I32, (PORTION, PORTION), 0)
     target = lax.broadcasted_iota(I32, (PORTION, PORTION), 1)
@@ -147,9 +151,12 @@
 
         def emit(value, turn):
             block = pltpu.roll(value.astype(F32), turn, 1)[:, :LANES]
-            block = jnp.where(keep, block, 0.0).astype(BF16)
-            out_ref[:, s * MAIN:(s + 1) * MAIN] = block[:, :MAIN]
-            out_ref[:, 8 * MAIN + s * 128:8 * MAIN + (s + 1) * 128] = block[:, MAIN:]
+            block = jnp.where(keep, block, 0.0)
+            out_ref[:, s * MAIN:(s + 1) * MAIN] = block[:, :MAIN].astype(BF16)
+            tail, place = block[:, MAIN:], slice(8 * MAIN + s // 2 * 128, 8 * MAIN + s // 2 * 128 + 128)
+            if s % 2:
+                tail = out_ref[:, place].astype(F32) + pltpu.roll(tail, TAIL, 1)
+            out_ref[:, place] = tail.astype(BF16)
 
         copies[s].wait()
 
@@ -171,41 +178,40 @@
     return t_ref[pl.ds(pl.multiple_of(slot * HALF, HALF), HALF), :]
 
 
-def multiply(meta_ref, v_ref, parts, stack, tails, syms, total):
-    virt = [meta_ref[g, 0] for g in range(8)]
-    hc = col_irrep(virt)
+def multiply(v_ref, parts, stack, syms, total):
+    lane = lax.broadcasted_iota(I32, (HALF, 128), 1)
+    zero = jnp.zeros((), BF16)
     for i, part in enumerate(parts):
         rows = slice(i * MAIN, i * MAIN + HALF)
         sym = jnp.broadcast_to(part[:, BMAX:BMAX + 1].astype(F32), (HALF, MAIN)).astype(BF16)
         for s in range(8):
-            keep = sym == jnp.asarray(s, BF16)
-            stack[rows, s * MAIN:(s + 1) * MAIN] = jnp.where(keep, part[:, :MAIN], jnp.zeros((), BF16))
-        tails[rows, :] = part[:, MAIN:]
-        syms[rows, :] = sym[:, :128]
-    total[...] = lax.dot_general(v_ref[:, :8 * MAIN], stack[...], NT, preferred_element_type=F32)
-    for s in range(8):
-
-        @pl.when(size_of(virt, jnp.bitwise_xor(hc, s)) > MAIN)
-        def _():
-            rest = jnp.where(syms[...] == jnp.asarray(s, BF16), tails[...], jnp.zeros((), BF16))
-            block = v_ref[:, 8 * MAIN + s * 128:8 * MAIN + (s + 1) * 128]
-            total[...] += lax.dot_general(block, rest, NT, preferred_element_type=F32)
-
-
-def own_kernel(steps, meta_ref, t_ref, v_ref, *refs):
-    outs, scratch = refs[:-4], refs[-4:]
-    multiply(meta_ref, v_ref, [portion_rows(t_ref, r) for r in steps], *scratch)
+            stack[rows, s * MAIN:(s + 1) * MAIN] = jnp.where(sym == jnp.asarray(s, BF16), part[:, :MAIN], zero)
+        sym = sym[:, :128]
+        tail = jnp.where(lane < TAIL, part[:, MAIN:].astype(F32), 0.0)
+        turned = pltpu.roll(tail, TAIL, 1).astype(BF16)
+        tail = tail.astype(BF16)
+        for s in range(0, 8, 2):
+            both = jnp.where(sym == jnp.asarray(s, BF16), tail, zero)
+            both = jnp.where(sym == jnp.asarray(s + 1, BF16), turned, both)
+            stack[rows, 8 * MAIN + s * TAIL:8 * MAIN + s * TAIL + 128] = both
+        syms[rows, :] = sym
+    total[...] = lax.dot_general(v_ref[...], stack[...], NT, preferred_element_type=F32)
+
+
+def own_kernel(steps, t_ref, v_ref, *refs):
+    outs, scratch = refs[:-3], refs[-3:]
+    multiply(v_ref, [portion_rows(t_ref, r) for r in steps], *scratch)
     total = scratch[-1]
     for i, out_ref in enumerate(outs):
         out_ref[:WINDOW, :] = total[:, i * MAIN:i * MAIN + 128].astype(BF16)
         out_ref[WINDOW:, :] = total[:, i * MAIN + 128:(i + 1) * MAIN].astype(BF16)
 
 
-def other_kernel(steps, after, meta_ref, t_ref, v_ref, *refs):
+def other_kernel(steps, after, t_ref, v_ref, *refs):
     refs = refs[after:]
     n = len(steps)
     mine, outs, scratch = refs[:n], refs[n:2 * n], refs[2 * n:]
-    multiply(meta_ref, v_ref, [portion_rows(t_ref, r) for r in steps], *scratch)
+    multiply(v_ref, [portion_rows(t_ref, r) for r in steps], *scratch)
     total = scratch[-1]
     lane = lax.broadcasted_iota(I32, (WINDOW, 128), 1)
     for i, (mine_ref, out_ref) in enumerate(zip(mine, outs)):
@@ -215,8 +221,8 @@
         out_ref[2 * WINDOW:, :] = jnp.where(lane < 64, mine_ref[WINDOW:, :].astype(F32), tail).astype(BF16)
 
 
-def stay_kernel(meta_ref, own_ref, other_ref, v_ref, out_ref, sym_ref, *scratch):
-    multiply(meta_ref, v_ref, [portion_rows(own_ref, 0), portion_rows(other_ref, 0)], *scratch)
+def stay_kernel(own_ref, other_ref, v_ref, out_ref, sym_ref, *scratch):
+    multiply(v_ref, [portion_rows(own_ref, 0), portion_rows(other_ref, 0)], *scratch)
     syms, total = scratch[-2:]
     lane = lax.broadcasted_iota(I32, (WINDOW, 128), 1)
     out_ref[:WINDOW, :] = total[:, :128].astype(BF16)
@@ -231,27 +237,29 @@
     sym_ref[:, 256:] = tail.astype(BF16)
 
 
-def place_kernel(meta_ref, a_ref, b_ref, c_ref, d_ref, sym_ref, order_ref, out_ref, total, wide, sem):
-    virt = [meta_ref[g, 0] for g in range(8)]
-    ra = row_irrep(virt)
-    sym = jnp.dot(sym_ref[...], order_ref[...], preferred_element_type=F32).astype(BF16)
+def place_kernel(meta_ref, a_ref, b_ref, c_ref, d_ref, sym_ref, order_ref, out_ref, total, wide, sems):
+    meta = [[meta_ref[group, i] for i in range(3)] for group in range(8)]
     for i in range(3):
         rows = slice(i * WINDOW, (i + 1) * WINDOW)
         value = a_ref[rows, :].astype(F32) + b_ref[rows, :].astype(F32) + c_ref[rows, :].astype(F32)
         total[:, i * 128:(i + 1) * 128] = (value + d_ref[rows, :].astype(F32)).astype(BF16)
-    value = jnp.dot(total[...], order_ref[...], preferred_element_type=F32).astype(BF16)
-    row = lax.broadcasted_iota(I32, (16, PORTION), 0)
-    for group in range(8):
-        offset = offset_of(virt, group)
-        start = block_start(offset)
-        mask = sym == jnp.bitwise_xor(ra, group).astype(F32).astype(BF16)
-        kept = jnp.where(jnp.concatenate([mask] * (WINDOW // 16), axis=0), value, jnp.zeros((), BF16))
-        head = wide[pl.ds(start, 16), :].astype(F32)
-        wide[pl.ds(start, 16), :] = jnp.where(row < offset - start, head, kept[:16].astype(F32)).astype(BF16)
-        wide[pl.ds(start + 16, WINDOW - 16), :] = kept[16:]
-    copy = pltpu.make_async_copy(wide.at[pl.ds(0, VIRT), :], out_ref, sem)
-    copy.start()
-    copy.wait()
+    row = lax.broadcasted_iota(I32, (16, 128), 0)
+    copies = []
+    for i in range(3):
+        lanes = slice(i * 128, (i + 1) * 128)
+        sym = jnp.dot(sym_ref[...], order_ref[:, lanes], preferred_element_type=F32).astype(BF16)
+        value = jnp.dot(total[...], order_ref[:, lanes], preferred_element_type=F32).astype(BF16)
+        for first, start, code in meta:
+            start = pl.multiple_of(start, 16)
+            mask = sym == code.astype(F32).astype(BF16)
+            kept = jnp.where(jnp.concatenate([mask] * (WINDOW // 16), axis=0), value, jnp.zeros((), BF16))
+            head = wide[pl.ds(start, 16), lanes].astype(F32)
+            wide[pl.ds(start, 16), lanes] = jnp.where(row < first - start, head, kept[:16].astype(F32)).astype(BF16)
+            wide[pl.ds(start + 16, WINDOW - 16), lanes] = kept[16:]
+        copies.append(pltpu.make_async_copy(wide.at[pl.ds(0, VIRT), lanes], out_ref.at[:, lanes], sems.at[i]))
+        copies[i].start()
+    for copy in copies:
+        copy.wait()
 
 
 def shift(value, axis, size, by):
@@ -282,7 +290,7 @@
     across = [shift(mine, "x", NX, k) for k in (2, 1, 3)]
     blocks, order, meta, mine = call(
         blocks_kernel, [VMEM, HBM],
-        (shape((WINDOW, 8 * LANES), BF16), shape((PORTION, PORTION), BF16), shape((8, 128), I32),
+        (shape((WINDOW, DEPTH), BF16), shape((PORTION, PORTION), BF16), shape((8, 128), I32),
          shape((HALF, LANES), BF16)),
         [pltpu.VMEM((8, 2 * WINDOW, VIRT), BF16), pltpu.VMEM((WINDOW, SPAN), BF16),
          pltpu.VMEM((16, 128), I32), pltpu.SemaphoreType.DMA((8,))], moved=16000000, limit=48,
@@ -292,30 +300,29 @@
     tile, part = shape((MESSAGE, 128), BF16), shape((2 * WINDOW, 128), BF16)
 
     def scratch(columns):
-        return [pltpu.VMEM((columns, 8 * MAIN), BF16), pltpu.VMEM((columns, 128), BF16),
-                pltpu.VMEM((columns, 128), BF16), pltpu.VMEM((WINDOW, columns), F32)]
+        return [pltpu.VMEM((columns, DEPTH), BF16), pltpu.VMEM((columns, 128), BF16), pltpu.VMEM((WINDOW, columns), F32)]
 
     def cost(columns):
-        return dict(flops=2 * columns * WINDOW * 8 * MAIN, moved=4000000)
+        return dict(flops=2 * columns * WINDOW * DEPTH, moved=4000000)
 
     two, plus, minus = call(
-        functools.partial(own_kernel, (2, 1, 3)), [VMEM] * 3, (part,) * 3, scratch(3 * MAIN), **cost(3 * MAIN)
-    )(meta, own, blocks)
+        functools.partial(own_kernel, (2, 1, 3)), [VMEM] * 2, (part,) * 3, scratch(3 * MAIN), **cost(3 * MAIN)
+    )(own, blocks)
     far, terms = [], ()
     for steps, mine in (((2,), (two,)), ((1, 3), (plus, minus))):
         columns = len(steps) * MAIN
-        operands = (meta, other, blocks, *terms, *mine)
+        operands = (other, blocks, *terms, *mine)
         terms = call(
             functools.partial(other_kernel, steps, len(terms)), [VMEM] * len(operands), (tile,) * len(steps),
             scratch(columns), **cost(columns)
         )(*operands)
         far += [shift(term, "y", NY, r) for r, term in zip(steps, terms)]
     stay, sym = call(
-        stay_kernel, [VMEM] * 4, (tile, shape((16, PORTION), BF16)), scratch(2 * MAIN), flops=20*10**9
-    )(meta, own, other, blocks)
+        stay_kernel, [VMEM] * 3, (tile, shape((16, PORTION), BF16)), scratch(2 * MAIN), flops=20*10**9
+    )(own, other, blocks)
     out = call(
         place_kernel, [VMEM] * 7, shape((VIRT, PORTION), BF16),
-        [pltpu.VMEM((WINDOW, PORTION), BF16), pltpu.VMEM((VIRT + WINDOW, PORTION), BF16), pltpu.SemaphoreType.DMA],
+        [pltpu.VMEM((WINDOW, PORTION), BF16), pltpu.VMEM((VIRT + WINDOW, PORTION), BF16), pltpu.SemaphoreType.DMA((3,))],
         HBM, moved=2600000,
     )(meta, stay, *far, sym, order)
     return out.T

time: 51.7 us -> 51.4 us (level)
  Pallas kernels: 13.9 us -> 13.3 us
  transfers between devices with their start and end apart: 7 -> 7, of which waited for: 2 -> 1; matrix products, arithmetic and copies ran while one was open for 0% -> 0% of each run, Pallas kernels for 18% -> 18%
where the time goes in v5:
time: 51.4 us; the launch traced here: 51.2 us
  blocking collectives  16.9 us (33%)
  starting transfers between devices  13.7 us (27%)
  Pallas kernels  13.3 us (26%)
  waiting for transfers between devices  6.82 us (13%)
    all_to_all x1, blocking collectives, shards(): mine = lax.all_to_all(packed, 'z', 0, 0, tiled=True)  16.9 us
    ppermute x7, starting transfers between devices, shift(): lax.ppermute(value, axis, [(i, (i + by) % size) for i in range(size)])  13.7 us
    ppermute x7, waiting for transfers between devices, shift(): lax.ppermute(value, axis, [(i, (i + by) % size) for i in range(size)])  6.82 us
    pallas_call x1, Pallas kernels, shards(): call(blocks_kernel, [VMEM, HBM], (shape((WINDOW, DEPTH), BF16), shape((PO...  4.54 us
    pallas_call x2, Pallas kernels, shards(): call(functools.partial(other_kernel, steps, len(terms)), [VMEM] * len(ope...  2.26 us
    pallas_call x1, Pallas kernels, shards(): call(functools.partial(own_kernel, (2, 1, 3)), [VMEM] * 2, (part,) * 3, s...  1.81 us
    pallas_call x1, Pallas kernels, shards(): call(pack_kernel, [HBM] * 4, shape((HALF, LANES), BF16), [pltpu.SMEM((8,)...  1.78 us
    pallas_call x1, Pallas kernels, shards(): call(place_kernel, [VMEM] * 7, shape((VIRT, PORTION), BF16), [pltpu.VMEM(...  1.62 us
  transfers between devices with their start and end apart: 7, of which 1 were waited for; matrix products, arithmetic and copies ran while one was open for 0% of the time, Pallas kernels for 18%

profile of v5, /device:TPU:1, one launch (start us, length us, event | category | flops | bytes accessed | tf_op | source)
XLA Modules:
  0.0 51.2 jit_solution(9675234168306353796)
XLA Ops:
  0.0 1.8 %shard_map.55 = bf16[192,384]{1,0:T(8,128)(2,1)} custom-call(s32[8]{0:T(128)} %virt_hbm.1, s32[8]{0:T(128)} %occ_hbm.1, s32[1536]{0:T(1024)} %ids_hbm.1, bf16[24,1600]{1,0:T(8,128)(2,1)} %t_hbm.1), custom_call_target="tpu_custom_call" | custom-call | bytes 300000 | tf_op jit(solution)/shard_map/pallas_call | solution.py:283
  1.8 16.9 %all_to_all.11 = bf16[8,24,384]{2,1,0:T(8,128)(2,1)S(1)} all-to-all(bf16[8,24,384]{2,1,0:T(8,128)(2,1)} %bitcast.7), channel_id=1, replica_groups=mesh['x'=4,'z'=8,'c'=2,'y'=4] {'z'}, dimensions={0} | all-to-all | bytes 294912 | tf_op jit(solution)/shard_map/all_to_all | solution.py:289
  18.7 1.2 %collective-permute-start = (bf16[192,384]{1,0:T(8,128)(2,1)S(1)}, bf16[192,384]{1,0:T(8,128)(2,1)S(1)}, u32[]{:S(2)}, u32[]{:S(2)}) collective-permute-start(bf16[192,384]{1,0:T(8,128)(2,1)S(1)} %bitcast.3), channel_id=1, source_target_pairs={{0,64},{64,128},{128,192},{192,0},{1,65},{65,129},{129,193},{193,1... | collective-permute-start | bytes 442376 | tf_op jit(solution)/shard_map/ppermute | solution.py:266
  20.0 1.5 %collective-permute-start.2 = (bf16[192,384]{1,0:T(8,128)(2,1)S(1)}, bf16[192,384]{1,0:T(8,128)(2,1)S(1)}, u32[]{:S(2)}, u32[]{:S(2)}) collective-permute-start(bf16[192,384]{1,0:T(8,128)(2,1)S(1)} %bitcast.4), channel_id=1, source_target_pairs={{0,192},{64,0},{128,64},{192,128},{1,193},{65,1},{129,65},{193,129... | collective-permute-start | bytes 442376 | tf_op jit(solution)/shard_map/ppermute | solution.py:266
  21.4 1.5 %collective-permute-start.1 = (bf16[192,384]{1,0:T(8,128)(2,1)S(1)}, bf16[192,384]{1,0:T(8,128)(2,1)S(1)}, u32[]{:S(2)}, u32[]{:S(2)}) collective-permute-start(bf16[192,384]{1,0:T(8,128)(2,1)S(1)} %bitcast.5), channel_id=1, source_target_pairs={{0,128},{64,192},{128,0},{192,64},{1,129},{65,193},{129,1},{193,65... | collective-permute-start | bytes 442376 | tf_op jit(solution)/shard_map/ppermute | solution.py:266
  22.9 4.5 %shard_map.56 = (bf16[336,2560]{1,0:T(8,128)(2,1)S(1)}, bf16[384,384]{1,0:T(8,128)(2,1)S(1)}, s32[8,128]{1,0:T(8,128)S(1)}, bf16[192,384]{1,0:T(8,128)(2,1)S(1)}) custom-call(bf16[192,384]{1,0:T(8,128)(2,1)S(1)} %bitcast.6, bf16[1600,1600]{1,0:T(8,128)(2,1)} %v_hbm.1), custom_call_target="tpu_custom_call" | custom-call | bytes 16000000 | tf_op jit(solution)/shard_map/pallas_call | solution.py:291
  27.5 0.0 collective-permute-done
  27.6 0.0 collective-permute-done.1
  27.6 0.0 collective-permute-done.2
  27.7 3.6 %collective-permute-start.3 = (bf16[768,384]{1,0:T(8,128)(2,1)S(1)}, bf16[768,384]{1,0:T(8,128)(2,1)S(1)}, u32[]{:S(2)}, u32[]{:S(2)}) collective-permute-start(bf16[768,384]{1,0:T(8,128)(2,1)S(1)} %constant_dynamic-update-slice_fusion.own_ref.t_ref), channel_id=1, source_target_pairs={{0,4},{4,0},{1,5},{5,1},{2,6},{6,2},{3,7},{7,3},{8,12},{12,8},{9,1... | collective-permute-start | bytes 1769480 | tf_op jit(solution)/shard_map/ppermute | solution.py:266
  31.2 1.8 %shard_map.58 = (bf16[672,128]{1,0:T(8,128)(2,1)S(1)}, bf16[672,128]{1,0:T(8,128)(2,1)S(1)}, bf16[672,128]{1,0:T(8,128)(2,1)S(1)}) custom-call(bf16[768,384]{1,0:T(8,128)(2,1)S(1)} %constant_dynamic-update-slice_fusion.own_ref.t_ref, bf16[336,2560]{1,0:T(8,128)(2,1)S(1)} %get-tuple-element.18.v_ref), custom_call_target="tpu_custom_call" | custom-call | flops 1321205760 | bytes 4000000 | tf_op jit(solution)/shard_map/pallas_call | solution.py:308
  33.1 0.0 collective-permute-done.3.other_ref.t_ref
  33.1 0.9 %shard_map.59.refs_0_ = bf16[1008,128]{1,0:T(8,128)(2,1)S(1)} custom-call(bf16[768,384]{1,0:T(8,128)(2,1)S(1)} %collective-permute-done.3.other_ref.t_ref, bf16[336,2560]{1,0:T(8,128)(2,1)S(1)} %get-tuple-element.18.v_ref, bf16[672,128]{1,0:T(8,128)(2,1)S(1)} %get-tuple-element.20.refs_0_), custom_call_target="tpu_custom_call" | custom-call | flops 440401920 | bytes 4000000 | tf_op jit(solution)/shard_map/pallas_call | solution.py:315
  33.9 3.2 %collective-permute-start.4 = (bf16[1008,128]{1,0:T(8,128)(2,1)S(1)}, bf16[1008,128]{1,0:T(8,128)(2,1)S(1)}, u32[]{:S(2)}, u32[]{:S(2)}) collective-permute-start(bf16[1008,128]{1,0:T(8,128)(2,1)S(1)} %shard_map.59.refs_0_), channel_id=1, source_target_pairs={{0,2},{1,3},{2,0},{3,1},{4,6},{5,7},{6,4},{7,5},{8,10},{9,11},{10,... | collective-permute-start | bytes 774152 | tf_op jit(solution)/shard_map/ppermute | solution.py:266
  37.1 1.4 %shard_map.60 = (bf16[1008,128]{1,0:T(8,128)(2,1)S(1)}, bf16[1008,128]{1,0:T(8,128)(2,1)S(1)}) custom-call(bf16[768,384]{1,0:T(8,128)(2,1)S(1)} %collective-permute-done.3.other_ref.t_ref, bf16[336,2560]{1,0:T(8,128)(2,1)S(1)} %get-tuple-element.18.v_ref, bf16[1008,128]{1,0:T(8,128)(2,1)S(1)} %shard_map.59.refs_0_, ...), custom_call_target="tpu_custom_call" | custom-call | flops 880803840 | bytes 4000000 | tf_op jit(solution)/shard_map/pallas_call | solution.py:315
  38.5 0.5 collective-permute-start.5
  39.0 2.3 %collective-permute-start.6 = (bf16[1008,128]{1,0:T(8,128)(2,1)S(1)}, bf16[1008,128]{1,0:T(8,128)(2,1)S(1)}, u32[]{:S(2)}, u32[]{:S(2)}) collective-permute-start(bf16[1008,128]{1,0:T(8,128)(2,1)S(1)} %get-tuple-element.24), channel_id=1, source_target_pairs={{0,3},{1,0},{2,1},{3,2},{4,7},{5,4},{6,5},{7,6},{8,11},{9,8},{10,9... | collective-permute-start | bytes 774152 | tf_op jit(solution)/shard_map/ppermute | solution.py:266
  41.3 1.3 %shard_map.57 = (bf16[1008,128]{1,0:T(8,128)(2,1)S(1)}, bf16[16,384]{1,0:T(8,128)(2,1)S(1)}) custom-call(bf16[768,384]{1,0:T(8,128)(2,1)S(1)} %constant_dynamic-update-slice_fusion.own_ref.t_ref, bf16[768,384]{1,0:T(8,128)(2,1)S(1)} %collective-permute-done.3.other_ref.t_ref, bf16[336,2560]{1,0:T(8,128)(2,1)S(1)} %get-tuple-element.18.v_ref), custom_call_target="tpu_custom_call" | custom-call | flops 20000000000 | tf_op jit(solution)/shard_map/pallas_call | solution.py:320
  42.6 6.8 %collective-permute-done.5.c_ref = bf16[1008,128]{1,0:T(8,128)(2,1)S(1)} collective-permute-done((bf16[1008,128]{1,0:T(8,128)(2,1)S(1)}, bf16[1008,128]{1,0:T(8,128)(2,1)S(1)}, u32[]{:S(2)}, u32[]{:S(2)}) %collective-permute-start.5) | collective-permute-done | bytes 258080 | tf_op jit(solution)/shard_map/ppermute | solution.py:266
  49.4 0.0 collective-permute-done.6.d_ref
  49.4 0.0 collective-permute-done.4.b_ref
  49.4 1.6 %shard_map.61 = bf16[1600,384]{1,0:T(8,128)(2,1)} custom-call(s32[8,128]{1,0:T(8,128)S(1)} %get-tuple-element.16.meta_ref, bf16[1008,128]{1,0:T(8,128)(2,1)S(1)} %get-tuple-element.19.a_ref, bf16[1008,128]{1,0:T(8,128)(2,1)S(1)} %collective-permute-done.4.b_ref, bf16[1008,128]{1,0:T(8,128)(2,1)S(1)} %collective-permute-done.5.c_ref, ...), custom_call_target="tpu_custom_call" | custom-call | bytes 2600000 | tf_op jit(solution)/shard_map/pallas_call | solution.py:323
  (4 shorter events, 0.1 us)
Async XLA Ops:
  18.7 8.8 %collective-permute-start = (bf16[192,384]{1,0:T(8,128)(2,1)S(1)}, bf16[192,384]{1,0:T(8,128)(2,1)S(1)}, u32[]{:S(2)}, u32[]{:S(2)}) collective-permute-start(bf16[192,384]{1,0:T(8,128)(2,1)S(1)} %bitcast.3), channel_id=1, source_target_pairs={{0,64},{64,128},{128,192},{192,0},{1,65},{65,129},{129,193},{193,1... | collective-permute-start | bytes 442376 | tf_op jit(solution)/shard_map/ppermute | solution.py:266
  20.0 7.7 %collective-permute-start.2 = (bf16[192,384]{1,0:T(8,128)(2,1)S(1)}, bf16[192,384]{1,0:T(8,128)(2,1)S(1)}, u32[]{:S(2)}, u32[]{:S(2)}) collective-permute-start(bf16[192,384]{1,0:T(8,128)(2,1)S(1)} %bitcast.4), channel_id=1, source_target_pairs={{0,192},{64,0},{128,64},{192,128},{1,193},{65,1},{129,65},{193,129... | collective-permute-start | bytes 442376 | tf_op jit(solution)/shard_map/ppermute | solution.py:266
  21.4 6.2 %collective-permute-start.1 = (bf16[192,384]{1,0:T(8,128)(2,1)S(1)}, bf16[192,384]{1,0:T(8,128)(2,1)S(1)}, u32[]{:S(2)}, u32[]{:S(2)}) collective-permute-start(bf16[192,384]{1,0:T(8,128)(2,1)S(1)} %bitcast.5), channel_id=1, source_target_pairs={{0,128},{64,192},{128,0},{192,64},{1,129},{65,193},{129,1},{193,65... | collective-permute-start | bytes 442376 | tf_op jit(solution)/shard_map/ppermute | solution.py:266
  27.7 5.4 %collective-permute-start.3 = (bf16[768,384]{1,0:T(8,128)(2,1)S(1)}, bf16[768,384]{1,0:T(8,128)(2,1)S(1)}, u32[]{:S(2)}, u32[]{:S(2)}) collective-permute-start(bf16[768,384]{1,0:T(8,128)(2,1)S(1)} %constant_dynamic-update-slice_fusion.own_ref.t_ref), channel_id=1, source_target_pairs={{0,4},{4,0},{1,5},{5,1},{2,6},{6,2},{3,7},{7,3},{8,12},{12,8},{9,1... | collective-permute-start | bytes 1769480 | tf_op jit(solution)/shard_map/ppermute | solution.py:266
  33.9 15.5 %collective-permute-start.4 = (bf16[1008,128]{1,0:T(8,128)(2,1)S(1)}, bf16[1008,128]{1,0:T(8,128)(2,1)S(1)}, u32[]{:S(2)}, u32[]{:S(2)}) collective-permute-start(bf16[1008,128]{1,0:T(8,128)(2,1)S(1)} %shard_map.59.refs_0_), channel_id=1, source_target_pairs={{0,2},{1,3},{2,0},{3,1},{4,6},{5,7},{6,4},{7,5},{8,10},{9,11},{10,... | collective-permute-start | bytes 774152 | tf_op jit(solution)/shard_map/ppermute | solution.py:266
  38.5 10.9 %collective-permute-start.5 = (bf16[1008,128]{1,0:T(8,128)(2,1)S(1)}, bf16[1008,128]{1,0:T(8,128)(2,1)S(1)}, u32[]{:S(2)}, u32[]{:S(2)}) collective-permute-start(bf16[1008,128]{1,0:T(8,128)(2,1)S(1)} %get-tuple-element.23), channel_id=1, source_target_pairs={{0,1},{1,2},{2,3},{3,0},{4,5},{5,6},{6,7},{7,4},{8,9},{9,10},{10,1... | collective-permute-start | bytes 774152 | tf_op jit(solution)/shard_map/ppermute | solution.py:266
  39.0 10.4 %collective-permute-start.6 = (bf16[1008,128]{1,0:T(8,128)(2,1)S(1)}, bf16[1008,128]{1,0:T(8,128)(2,1)S(1)}, u32[]{:S(2)}, u32[]{:S(2)}) collective-permute-start(bf16[1008,128]{1,0:T(8,128)(2,1)S(1)} %get-tuple-element.24), channel_id=1, source_target_pairs={{0,3},{1,0},{2,1},{3,2},{4,7},{5,4},{6,5},{7,6},{8,11},{9,8},{10,9... | collective-permute-start | bytes 774152 | tf_op jit(solution)/shard_map/ppermute | solution.py:266

commit v6 on v5

--- a/solution.py
+++ b/solution.py
@@ -22,7 +22,8 @@
 TAIL = BMAX - MAIN
 DEPTH = 8 * BMAX
 WINDOW = 336
-MESSAGE = 3 * WINDOW
+HEIGHT = 320
+MESSAGE = 3 * HEIGHT
 SPAN = 512
 LAST = 1152
 META = BMAX - MAIN + 8
@@ -117,7 +118,9 @@
     sizes[...] = mine_ref[:16, MAIN:].astype(F32).astype(I32)
     virt = [sizes[0, META + g] * 16 + sizes[0, META + 8 + g] for g in range(8)]
     ra, hc = row_irrep(virt), col_irrep(virt)
-    starts = [block_start(offset_of(virt, jnp.bitwise_xor(ra, s))) for s in range(8)]
+    offsets = [offset_of(virt, jnp.bitwise_xor(ra, s)) for s in range(8)]
+    starts = [block_start(offset) for offset in offsets]
+    skips = [offset - start for offset, start in zip(offsets, starts)]
     firsts = [pl.multiple_of(jnp.minimum(start, VIRT - WINDOW), 16) for start in starts]
     copies = [
         pltpu.make_async_copy(v_hbm.at[pl.ds(firsts[s], WINDOW), :], windows.at[s, pl.ds(0, WINDOW), :], sems.at[s])
@@ -152,6 +155,8 @@
         def emit(value, turn):
             block = pltpu.roll(value.astype(F32), turn, 1)[:, :LANES]
             block = jnp.where(keep, block, 0.0)
+            head = jnp.where(row[:16] < skips[s], block[HEIGHT:], block[:16])
+            block = jnp.concatenate([head, block[16:HEIGHT]], axis=0)
             out_ref[:, s * MAIN:(s + 1) * MAIN] = block[:, :MAIN].astype(BF16)
             tail, place = block[:, MAIN:], slice(8 * MAIN + s // 2 * 128, 8 * MAIN + s // 2 * 128 + 128)
             if s % 2:
@@ -203,8 +208,8 @@
     multiply(v_ref, [portion_rows(t_ref, r) for r in steps], *scratch)
     total = scratch[-1]
     for i, out_ref in enumerate(outs):
-        out_ref[:WINDOW, :] = total[:, i * MAIN:i * MAIN + 128].astype(BF16)
-        out_ref[WINDOW:, :] = total[:, i * MAIN + 128:(i + 1) * MAIN].astype(BF16)
+        out_ref[:HEIGHT, :] = total[:, i * MAIN:i * MAIN + 128].astype(BF16)
+        out_ref[HEIGHT:, :] = total[:, i * MAIN + 128:(i + 1) * MAIN].astype(BF16)
 
 
 def other_kernel(steps, after, t_ref, v_ref, *refs):
@@ -213,22 +218,22 @@
     mine, outs, scratch = refs[:n], refs[n:2 * n], refs[2 * n:]
     multiply(v_ref, [portion_rows(t_ref, r) for r in steps], *scratch)
     total = scratch[-1]
-    lane = lax.broadcasted_iota(I32, (WINDOW, 128), 1)
+    lane = lax.broadcasted_iota(I32, (HEIGHT, 128), 1)
     for i, (mine_ref, out_ref) in enumerate(zip(mine, outs)):
-        out_ref[:WINDOW, :] = mine_ref[:WINDOW, :]
-        out_ref[WINDOW:2 * WINDOW, :] = total[:, i * MAIN:i * MAIN + 128].astype(BF16)
+        out_ref[:HEIGHT, :] = mine_ref[:HEIGHT, :]
+        out_ref[HEIGHT:2 * HEIGHT, :] = total[:, i * MAIN:i * MAIN + 128].astype(BF16)
         tail = pltpu.roll(total[:, i * MAIN + 128:(i + 1) * MAIN], 64, 1)
-        out_ref[2 * WINDOW:, :] = jnp.where(lane < 64, mine_ref[WINDOW:, :].astype(F32), tail).astype(BF16)
+        out_ref[2 * HEIGHT:, :] = jnp.where(lane < 64, mine_ref[HEIGHT:, :].astype(F32), tail).astype(BF16)
 
 
 def stay_kernel(own_ref, other_ref, v_ref, out_ref, sym_ref, *scratch):
     multiply(v_ref, [portion_rows(own_ref, 0), portion_rows(other_ref, 0)], *scratch)
     syms, total = scratch[-2:]
-    lane = lax.broadcasted_iota(I32, (WINDOW, 128), 1)
-    out_ref[:WINDOW, :] = total[:, :128].astype(BF16)
-    out_ref[WINDOW:2 * WINDOW, :] = total[:, MAIN:MAIN + 128].astype(BF16)
+    lane = lax.broadcasted_iota(I32, (HEIGHT, 128), 1)
+    out_ref[:HEIGHT, :] = total[:, :128].astype(BF16)
+    out_ref[HEIGHT:2 * HEIGHT, :] = total[:, MAIN:MAIN + 128].astype(BF16)
     tail = jnp.where(lane < 64, total[:, 128:MAIN], pltpu.roll(total[:, MAIN + 128:], 64, 1))
-    out_ref[2 * WINDOW:, :] = tail.astype(BF16)
+    out_ref[2 * HEIGHT:, :] = tail.astype(BF16)
     one = (lane[:16] == 0).astype(F32).astype(BF16)
     sym = lax.dot_general(one, syms[...], NT, preferred_element_type=F32)
     sym_ref[:, :128] = sym[:, :128].astype(BF16)
@@ -240,7 +245,7 @@
 def place_kernel(meta_ref, a_ref, b_ref, c_ref, d_ref, sym_ref, order_ref, out_ref, total, wide, sems):
     meta = [[meta_ref[group, i] for i in range(3)] for group in range(8)]
     for i in range(3):
-        rows = slice(i * WINDOW, (i + 1) * WINDOW)
+        rows = slice(i * HEIGHT, (i + 1) * HEIGHT)
         value = a_ref[rows, :].astype(F32) + b_ref[rows, :].astype(F32) + c_ref[rows, :].astype(F32)
         total[:, i * 128:(i + 1) * 128] = (value + d_ref[rows, :].astype(F32)).astype(BF16)
     row = lax.broadcasted_iota(I32, (16, 128), 0)
@@ -252,10 +257,11 @@
         for first, start, code in meta:
             start = pl.multiple_of(start, 16)
             mask = sym == code.astype(F32).astype(BF16)
-            kept = jnp.where(jnp.concatenate([mask] * (WINDOW // 16), axis=0), value, jnp.zeros((), BF16))
+            kept = jnp.where(jnp.concatenate([mask] * (HEIGHT // 16), axis=0), value, jnp.zeros((), BF16))
             head = wide[pl.ds(start, 16), lanes].astype(F32)
             wide[pl.ds(start, 16), lanes] = jnp.where(row < first - start, head, kept[:16].astype(F32)).astype(BF16)
-            wide[pl.ds(start + 16, WINDOW - 16), lanes] = kept[16:]
+            wide[pl.ds(start + 16, HEIGHT - 16), lanes] = kept[16:]
+            wide[pl.ds(start + HEIGHT, 16), lanes] = kept[:16]
         copies.append(pltpu.make_async_copy(wide.at[pl.ds(0, VIRT), lanes], out_ref.at[:, lanes], sems.at[i]))
         copies[i].start()
     for copy in copies:
@@ -290,20 +296,20 @@
     across = [shift(mine, "x", NX, k) for k in (2, 1, 3)]
     blocks, order, meta, mine = call(
         blocks_kernel, [VMEM, HBM],
-        (shape((WINDOW, DEPTH), BF16), shape((PORTION, PORTION), BF16), shape((8, 128), I32),
+        (shape((HEIGHT, DEPTH), BF16), shape((PORTION, PORTION), BF16), shape((8, 128), I32),
          shape((HALF, LANES), BF16)),
         [pltpu.VMEM((8, 2 * WINDOW, VIRT), BF16), pltpu.VMEM((WINDOW, SPAN), BF16),
          pltpu.VMEM((16, 128), I32), pltpu.SemaphoreType.DMA((8,))], moved=16000000, limit=48,
     )(mine, integrals)
     own = jnp.concatenate([mine, across[1], across[0], across[2]], axis=0)
     other = shift(own, "c", NC, 1)
-    tile, part = shape((MESSAGE, 128), BF16), shape((2 * WINDOW, 128), BF16)
+    tile, part = shape((MESSAGE, 128), BF16), shape((2 * HEIGHT, 128), BF16)
 
     def scratch(columns):
-        return [pltpu.VMEM((columns, DEPTH), BF16), pltpu.VMEM((columns, 128), BF16), pltpu.VMEM((WINDOW, columns), F32)]
+        return [pltpu.VMEM((columns, DEPTH), BF16), pltpu.VMEM((columns, 128), BF16), pltpu.VMEM((HEIGHT, columns), F32)]
 
     def cost(columns):
-        return dict(flops=2 * columns * WINDOW * DEPTH, moved=4000000)
+        return dict(flops=2 * columns * HEIGHT * DEPTH, moved=4000000)
 
     two, plus, minus = call(
         functools.partial(own_kernel, (2, 1, 3)), [VMEM] * 2, (part,) * 3, scratch(3 * MAIN), **cost(3 * MAIN)
@@ -322,7 +328,7 @@
     )(own, other, blocks)
     out = call(
         place_kernel, [VMEM] * 7, shape((VIRT, PORTION), BF16),
-        [pltpu.VMEM((WINDOW, PORTION), BF16), pltpu.VMEM((VIRT + WINDOW, PORTION), BF16), pltpu.SemaphoreType.DMA((3,))],
+        [pltpu.VMEM((HEIGHT, PORTION), BF16), pltpu.VMEM((VIRT + WINDOW, PORTION), BF16), pltpu.SemaphoreType.DMA((3,))],
         HBM, moved=2600000,
     )(meta, stay, *far, sym, order)
     return out.T

time: 51.4 us -> 50.6 us (0.984)
  waiting for transfers between devices: 6.82 us -> 6.27 us
    ppermute x7, waiting for transfers between devices: 6.82 us -> 6.27 us  [shift(): lax.ppermute(value, axis, [(i, (i + by) % size) for i in range(size)])]
where the time goes in v6:
time: 50.6 us; the launch traced here: 50.4 us
  blocking collectives  16.9 us (33%)
  starting transfers between devices  13.7 us (27%)
  Pallas kernels  13.2 us (26%)
  waiting for transfers between devices  6.27 us (12%)
    all_to_all x1, blocking collectives, shards(): mine = lax.all_to_all(packed, 'z', 0, 0, tiled=True)  16.9 us
    ppermute x7, starting transfers between devices, shift(): lax.ppermute(value, axis, [(i, (i + by) % size) for i in range(size)])  13.7 us
    ppermute x7, waiting for transfers between devices, shift(): lax.ppermute(value, axis, [(i, (i + by) % size) for i in range(size)])  6.27 us
    pallas_call x1, Pallas kernels, shards(): call(blocks_kernel, [VMEM, HBM], (shape((HEIGHT, DEPTH), BF16), shape((PO...  4.61 us
    pallas_call x2, Pallas kernels, shards(): call(functools.partial(other_kernel, steps, len(terms)), [VMEM] * len(ope...  2.19 us
    pallas_call x1, Pallas kernels, shards(): call(pack_kernel, [HBM] * 4, shape((HALF, LANES), BF16), [pltpu.SMEM((8,)...  1.78 us
    pallas_call x1, Pallas kernels, shards(): call(functools.partial(own_kernel, (2, 1, 3)), [VMEM] * 2, (part,) * 3, s...  1.75 us
    pallas_call x1, Pallas kernels, shards(): call(place_kernel, [VMEM] * 7, shape((VIRT, PORTION), BF16), [pltpu.VMEM(...  1.54 us
  transfers between devices with their start and end apart: 7, of which 1 were waited for; matrix products, arithmetic and copies ran while one was open for 0% of the time, Pallas kernels for 18%

profile of v6, /device:TPU:1, one launch (start us, length us, event | category | flops | bytes accessed | tf_op | source)
XLA Modules:
  0.0 50.4 jit_solution(3258492070579271398)
XLA Ops:
  0.0 1.8 %shard_map.55 = bf16[192,384]{1,0:T(8,128)(2,1)} custom-call(s32[8]{0:T(128)} %virt_hbm.1, s32[8]{0:T(128)} %occ_hbm.1, s32[1536]{0:T(1024)} %ids_hbm.1, bf16[24,1600]{1,0:T(8,128)(2,1)} %t_hbm.1), custom_call_target="tpu_custom_call" | custom-call | bytes 300000 | tf_op jit(solution)/shard_map/pallas_call | solution.py:289
  1.8 16.9 %all_to_all.11 = bf16[8,24,384]{2,1,0:T(8,128)(2,1)S(1)} all-to-all(bf16[8,24,384]{2,1,0:T(8,128)(2,1)} %bitcast.7), channel_id=1, replica_groups=mesh['x'=4,'z'=8,'c'=2,'y'=4] {'z'}, dimensions={0} | all-to-all | bytes 294912 | tf_op jit(solution)/shard_map/all_to_all | solution.py:295
  18.7 1.2 %collective-permute-start = (bf16[192,384]{1,0:T(8,128)(2,1)S(1)}, bf16[192,384]{1,0:T(8,128)(2,1)S(1)}, u32[]{:S(2)}, u32[]{:S(2)}) collective-permute-start(bf16[192,384]{1,0:T(8,128)(2,1)S(1)} %bitcast.3), channel_id=1, source_target_pairs={{0,64},{64,128},{128,192},{192,0},{1,65},{65,129},{129,193},{193,1... | collective-permute-start | bytes 442376 | tf_op jit(solution)/shard_map/ppermute | solution.py:272
  20.0 1.5 %collective-permute-start.2 = (bf16[192,384]{1,0:T(8,128)(2,1)S(1)}, bf16[192,384]{1,0:T(8,128)(2,1)S(1)}, u32[]{:S(2)}, u32[]{:S(2)}) collective-permute-start(bf16[192,384]{1,0:T(8,128)(2,1)S(1)} %bitcast.4), channel_id=1, source_target_pairs={{0,192},{64,0},{128,64},{192,128},{1,193},{65,1},{129,65},{193,129... | collective-permute-start | bytes 442376 | tf_op jit(solution)/shard_map/ppermute | solution.py:272
  21.4 1.5 %collective-permute-start.1 = (bf16[192,384]{1,0:T(8,128)(2,1)S(1)}, bf16[192,384]{1,0:T(8,128)(2,1)S(1)}, u32[]{:S(2)}, u32[]{:S(2)}) collective-permute-start(bf16[192,384]{1,0:T(8,128)(2,1)S(1)} %bitcast.5), channel_id=1, source_target_pairs={{0,128},{64,192},{128,0},{192,64},{1,129},{65,193},{129,1},{193,65... | collective-permute-start | bytes 442376 | tf_op jit(solution)/shard_map/ppermute | solution.py:272
  22.9 4.6 %shard_map.56 = (bf16[320,2560]{1,0:T(8,128)(2,1)S(1)}, bf16[384,384]{1,0:T(8,128)(2,1)S(1)}, s32[8,128]{1,0:T(8,128)S(1)}, bf16[192,384]{1,0:T(8,128)(2,1)S(1)}) custom-call(bf16[192,384]{1,0:T(8,128)(2,1)S(1)} %bitcast.6, bf16[1600,1600]{1,0:T(8,128)(2,1)} %v_hbm.1), custom_call_target="tpu_custom_call" | custom-call | bytes 16000000 | tf_op jit(solution)/shard_map/pallas_call | solution.py:297
  27.6 0.0 collective-permute-done
  27.6 0.0 collective-permute-done.1
  27.7 0.0 collective-permute-done.2
  27.7 3.5 %collective-permute-start.3 = (bf16[768,384]{1,0:T(8,128)(2,1)S(1)}, bf16[768,384]{1,0:T(8,128)(2,1)S(1)}, u32[]{:S(2)}, u32[]{:S(2)}) collective-permute-start(bf16[768,384]{1,0:T(8,128)(2,1)S(1)} %constant_dynamic-update-slice_fusion.own_ref.t_ref), channel_id=1, source_target_pairs={{0,4},{4,0},{1,5},{5,1},{2,6},{6,2},{3,7},{7,3},{8,12},{12,8},{9,1... | collective-permute-start | bytes 1769480 | tf_op jit(solution)/shard_map/ppermute | solution.py:272
  31.2 1.8 %shard_map.58 = (bf16[640,128]{1,0:T(8,128)(2,1)S(1)}, bf16[640,128]{1,0:T(8,128)(2,1)S(1)}, bf16[640,128]{1,0:T(8,128)(2,1)S(1)}) custom-call(bf16[768,384]{1,0:T(8,128)(2,1)S(1)} %constant_dynamic-update-slice_fusion.own_ref.t_ref, bf16[320,2560]{1,0:T(8,128)(2,1)S(1)} %get-tuple-element.18.v_ref), custom_call_target="tpu_custom_call" | custom-call | flops 1258291200 | bytes 4000000 | tf_op jit(solution)/shard_map/pallas_call | solution.py:314
  33.0 0.0 collective-permute-done.3.other_ref.t_ref
  33.0 0.8 %shard_map.59.refs_0_ = bf16[960,128]{1,0:T(8,128)(2,1)S(1)} custom-call(bf16[768,384]{1,0:T(8,128)(2,1)S(1)} %collective-permute-done.3.other_ref.t_ref, bf16[320,2560]{1,0:T(8,128)(2,1)S(1)} %get-tuple-element.18.v_ref, bf16[640,128]{1,0:T(8,128)(2,1)S(1)} %get-tuple-element.20.refs_0_), custom_call_target="tpu_custom_call" | custom-call | flops 419430400 | bytes 4000000 | tf_op jit(solution)/shard_map/pallas_call | solution.py:321
  33.9 3.2 %collective-permute-start.4 = (bf16[960,128]{1,0:T(8,128)(2,1)S(1)}, bf16[960,128]{1,0:T(8,128)(2,1)S(1)}, u32[]{:S(2)}, u32[]{:S(2)}) collective-permute-start(bf16[960,128]{1,0:T(8,128)(2,1)S(1)} %shard_map.59.refs_0_), channel_id=1, source_target_pairs={{0,2},{1,3},{2,0},{3,1},{4,6},{5,7},{6,4},{7,5},{8,10},{9,11},{10,... | collective-permute-start | bytes 737288 | tf_op jit(solution)/shard_map/ppermute | solution.py:272
  37.0 1.3 %shard_map.60 = (bf16[960,128]{1,0:T(8,128)(2,1)S(1)}, bf16[960,128]{1,0:T(8,128)(2,1)S(1)}) custom-call(bf16[768,384]{1,0:T(8,128)(2,1)S(1)} %collective-permute-done.3.other_ref.t_ref, bf16[320,2560]{1,0:T(8,128)(2,1)S(1)} %get-tuple-element.18.v_ref, bf16[960,128]{1,0:T(8,128)(2,1)S(1)} %shard_map.59.refs_0_, ...), custom_call_target="tpu_custom_call" | custom-call | flops 838860800 | bytes 4000000 | tf_op jit(solution)/shard_map/pallas_call | solution.py:321
  38.4 0.5 collective-permute-start.5
  38.9 2.3 %collective-permute-start.6 = (bf16[960,128]{1,0:T(8,128)(2,1)S(1)}, bf16[960,128]{1,0:T(8,128)(2,1)S(1)}, u32[]{:S(2)}, u32[]{:S(2)}) collective-permute-start(bf16[960,128]{1,0:T(8,128)(2,1)S(1)} %get-tuple-element.24), channel_id=1, source_target_pairs={{0,3},{1,0},{2,1},{3,2},{4,7},{5,4},{6,5},{7,6},{8,11},{9,8},{10,9... | collective-permute-start | bytes 737288 | tf_op jit(solution)/shard_map/ppermute | solution.py:272
  41.1 1.3 %shard_map.57 = (bf16[960,128]{1,0:T(8,128)(2,1)S(1)}, bf16[16,384]{1,0:T(8,128)(2,1)S(1)}) custom-call(bf16[768,384]{1,0:T(8,128)(2,1)S(1)} %constant_dynamic-update-slice_fusion.own_ref.t_ref, bf16[768,384]{1,0:T(8,128)(2,1)S(1)} %collective-permute-done.3.other_ref.t_ref, bf16[320,2560]{1,0:T(8,128)(2,1)S(1)} %get-tuple-element.18.v_ref), custom_call_target="tpu_custom_call" | custom-call | flops 20000000000 | tf_op jit(solution)/shard_map/pallas_call | solution.py:326
  42.4 6.3 %collective-permute-done.5.c_ref = bf16[960,128]{1,0:T(8,128)(2,1)S(1)} collective-permute-done((bf16[960,128]{1,0:T(8,128)(2,1)S(1)}, bf16[960,128]{1,0:T(8,128)(2,1)S(1)}, u32[]{:S(2)}, u32[]{:S(2)}) %collective-permute-start.5) | collective-permute-done | bytes 245792 | tf_op jit(solution)/shard_map/ppermute | solution.py:272
  48.7 0.0 collective-permute-done.6.d_ref
  48.7 0.0 collective-permute-done.4.b_ref
  48.7 1.5 %shard_map.61 = bf16[1600,384]{1,0:T(8,128)(2,1)} custom-call(s32[8,128]{1,0:T(8,128)S(1)} %get-tuple-element.16.meta_ref, bf16[960,128]{1,0:T(8,128)(2,1)S(1)} %get-tuple-element.19.a_ref, bf16[960,128]{1,0:T(8,128)(2,1)S(1)} %collective-permute-done.4.b_ref, bf16[960,128]{1,0:T(8,128)(2,1)S(1)} %collective-permute-done.5.c_ref, ...), custom_call_target="tpu_custom_call" | custom-call | bytes 2600000 | tf_op jit(solution)/shard_map/pallas_call | solution.py:329
  (4 shorter events, 0.1 us)
Async XLA Ops:
  18.7 8.9 %collective-permute-start = (bf16[192,384]{1,0:T(8,128)(2,1)S(1)}, bf16[192,384]{1,0:T(8,128)(2,1)S(1)}, u32[]{:S(2)}, u32[]{:S(2)}) collective-permute-start(bf16[192,384]{1,0:T(8,128)(2,1)S(1)} %bitcast.3), channel_id=1, source_target_pairs={{0,64},{64,128},{128,192},{192,0},{1,65},{65,129},{129,193},{193,1... | collective-permute-start | bytes 442376 | tf_op jit(solution)/shard_map/ppermute | solution.py:272
  20.0 7.7 %collective-permute-start.2 = (bf16[192,384]{1,0:T(8,128)(2,1)S(1)}, bf16[192,384]{1,0:T(8,128)(2,1)S(1)}, u32[]{:S(2)}, u32[]{:S(2)}) collective-permute-start(bf16[192,384]{1,0:T(8,128)(2,1)S(1)} %bitcast.4), channel_id=1, source_target_pairs={{0,192},{64,0},{128,64},{192,128},{1,193},{65,1},{129,65},{193,129... | collective-permute-start | bytes 442376 | tf_op jit(solution)/shard_map/ppermute | solution.py:272
  21.4 6.2 %collective-permute-start.1 = (bf16[192,384]{1,0:T(8,128)(2,1)S(1)}, bf16[192,384]{1,0:T(8,128)(2,1)S(1)}, u32[]{:S(2)}, u32[]{:S(2)}) collective-permute-start(bf16[192,384]{1,0:T(8,128)(2,1)S(1)} %bitcast.5), channel_id=1, source_target_pairs={{0,128},{64,192},{128,0},{192,64},{1,129},{65,193},{129,1},{193,65... | collective-permute-start | bytes 442376 | tf_op jit(solution)/shard_map/ppermute | solution.py:272
  27.7 5.3 %collective-permute-start.3 = (bf16[768,384]{1,0:T(8,128)(2,1)S(1)}, bf16[768,384]{1,0:T(8,128)(2,1)S(1)}, u32[]{:S(2)}, u32[]{:S(2)}) collective-permute-start(bf16[768,384]{1,0:T(8,128)(2,1)S(1)} %constant_dynamic-update-slice_fusion.own_ref.t_ref), channel_id=1, source_target_pairs={{0,4},{4,0},{1,5},{5,1},{2,6},{6,2},{3,7},{7,3},{8,12},{12,8},{9,1... | collective-permute-start | bytes 1769480 | tf_op jit(solution)/shard_map/ppermute | solution.py:272
  33.9 14.8 %collective-permute-start.4 = (bf16[960,128]{1,0:T(8,128)(2,1)S(1)}, bf16[960,128]{1,0:T(8,128)(2,1)S(1)}, u32[]{:S(2)}, u32[]{:S(2)}) collective-permute-start(bf16[960,128]{1,0:T(8,128)(2,1)S(1)} %shard_map.59.refs_0_), channel_id=1, source_target_pairs={{0,2},{1,3},{2,0},{3,1},{4,6},{5,7},{6,4},{7,5},{8,10},{9,11},{10,... | collective-permute-start | bytes 737288 | tf_op jit(solution)/shard_map/ppermute | solution.py:272
  38.4 10.3 %collective-permute-start.5 = (bf16[960,128]{1,0:T(8,128)(2,1)S(1)}, bf16[960,128]{1,0:T(8,128)(2,1)S(1)}, u32[]{:S(2)}, u32[]{:S(2)}) collective-permute-start(bf16[960,128]{1,0:T(8,128)(2,1)S(1)} %get-tuple-element.23), channel_id=1, source_target_pairs={{0,1},{1,2},{2,3},{3,0},{4,5},{5,6},{6,7},{7,4},{8,9},{9,10},{10,1... | collective-permute-start | bytes 737288 | tf_op jit(solution)/shard_map/ppermute | solution.py:272
  38.9 9.8 %collective-permute-start.6 = (bf16[960,128]{1,0:T(8,128)(2,1)S(1)}, bf16[960,128]{1,0:T(8,128)(2,1)S(1)}, u32[]{:S(2)}, u32[]{:S(2)}) collective-permute-start(bf16[960,128]{1,0:T(8,128)(2,1)S(1)} %get-tuple-element.24), channel_id=1, source_target_pairs={{0,3},{1,0},{2,1},{3,2},{4,7},{5,4},{6,5},{7,6},{8,11},{9,8},{10,9... | collective-permute-start | bytes 737288 | tf_op jit(solution)/shard_map/ppermute | solution.py:272

commit v7 on v6

--- a/solution.py
+++ b/solution.py
@@ -26,7 +26,9 @@
 MESSAGE = 3 * HEIGHT
 SPAN = 512
 LAST = 1152
-META = BMAX - MAIN + 8
+PACK = 64
+SLOT = NZ * PACK
+META = 112
 F32, BF16, I32 = jnp.float32, jnp.bfloat16, jnp.int32
 SMEM = pl.BlockSpec(memory_space=pltpu.SMEM)
 VMEM = pl.BlockSpec(memory_space=pltpu.VMEM)
@@ -95,11 +97,7 @@
     for r in range(ROWS):
         ids = jnp.where(row == r, ids_ref[base + r], ids)
     sym = pair_sym(ids, occ)
-    meta = jnp.where(lane < META, sym, 0)
-    for g in range(8):
-        meta = jnp.where(lane == META + g, lax.shift_right_logical(virt[g], 4), meta)
-        meta = jnp.where(lane == META + 8 + g, jnp.bitwise_and(virt[g], 15), meta)
-    parts = [jnp.zeros((ROWS, 128), F32)] * 2 + [jnp.where(lane >= BMAX - MAIN, meta, 0).astype(F32)]
+    parts = [jnp.zeros((ROWS, 128), F32)] * 3
     copies[3].wait()
     wide[:, :VIRT] = t_ref[...].astype(F32)
     for s in range(8):
@@ -110,13 +108,22 @@
         for i in range(3):
             keep = (sym == s) & (lane < size - i * 128)
             parts[i] = jnp.where(keep, span[:, i * 128:(i + 1) * 128], parts[i])
-    packed = jnp.concatenate(parts, axis=1)
+    lane, tail = lane[:8], parts[2]
+    spare = jnp.zeros((8, 128), I32)
+    for i in range(3):
+        spare = jnp.where((lane >= 64 + 16 * i) & (lane < 80 + 16 * i), sym[8 * i:8 * i + 8], spare)
+    for g in range(8):
+        spare = jnp.where(lane == META + g, lax.shift_right_logical(virt[g], 4), spare)
+        spare = jnp.where(lane == META + 8 + g, jnp.bitwise_and(virt[g], 15), spare)
+    first = jnp.where(lane < TAIL, tail[:8], pltpu.roll(tail[16:], TAIL, 1))
+    second = jnp.where(lane < TAIL, tail[8:16], spare.astype(F32))
+    packed = jnp.concatenate([parts[0], parts[1], first, second], axis=0)
     out_ref[...] = jnp.concatenate([packed] * NZ, axis=0).astype(BF16)
 
 
 def blocks_kernel(mine_ref, v_hbm, out_ref, order_ref, meta_ref, copy_ref, windows, span, sizes, sems):
-    sizes[...] = mine_ref[:16, MAIN:].astype(F32).astype(I32)
-    virt = [sizes[0, META + g] * 16 + sizes[0, META + 8 + g] for g in range(8)]
+    sizes[...] = mine_ref[PACK - 16:PACK, :].astype(F32).astype(I32)
+    virt = [sizes[8, META + g] * 16 + sizes[8, META + 8 + g] for g in range(8)]
     ra, hc = row_irrep(virt), col_irrep(virt)
     offsets = [offset_of(virt, jnp.bitwise_xor(ra, s)) for s in range(8)]
     starts = [block_start(offset) for offset in offsets]
@@ -180,7 +187,7 @@
 
 def portion_rows(t_ref, r):
     slot = lax.rem(lax.axis_index("x") - lax.axis_index("y") - r + 2 * NX, NX)
-    return t_ref[pl.ds(pl.multiple_of(slot * HALF, HALF), HALF), :]
+    return t_ref[pl.ds(pl.multiple_of(slot * SLOT, SLOT), SLOT), :]
 
 
 def multiply(v_ref, parts, stack, syms, total):
@@ -188,11 +195,17 @@
     zero = jnp.zeros((), BF16)
     for i, part in enumerate(parts):
         rows = slice(i * MAIN, i * MAIN + HALF)
-        sym = jnp.broadcast_to(part[:, BMAX:BMAX + 1].astype(F32), (HALF, MAIN)).astype(BF16)
+        part = part.astype(F32)
+        blocks = [part[z * PACK:(z + 1) * PACK] for z in range(NZ)]
+        halves = [jnp.concatenate([b[h * ROWS:(h + 1) * ROWS] for b in blocks], axis=0).astype(BF16) for h in range(2)]
+        columns = [b[56:, 64 + 16 * k:65 + 16 * k] for b in blocks for k in range(3)]
+        sym = jnp.concatenate([jnp.broadcast_to(c, (8, 128)) for c in columns], axis=0).astype(BF16)
         for s in range(8):
-            stack[rows, s * MAIN:(s + 1) * MAIN] = jnp.where(sym == jnp.asarray(s, BF16), part[:, :MAIN], zero)
-        sym = sym[:, :128]
-        tail = jnp.where(lane < TAIL, part[:, MAIN:].astype(F32), 0.0)
+            keep = sym == jnp.asarray(s, BF16)
+            for h in range(2):
+                stack[rows, s * MAIN + h * 128:s * MAIN + h * 128 + 128] = jnp.where(keep, halves[h], zero)
+        tail = jnp.concatenate([t for b in blocks for t in (b[48:], pltpu.roll(b[48:56], TAIL, 1))], axis=0)
+        tail = jnp.where(lane < TAIL, tail, 0.0)
         turned = pltpu.roll(tail, TAIL, 1).astype(BF16)
         tail = tail.astype(BF16)
         for s in range(0, 8, 2):
@@ -287,7 +300,7 @@
 def shards(virt_sizes, occ_sizes, pair_ids, amplitudes, integrals):
     shape = jax.ShapeDtypeStruct
     packed = call(
-        pack_kernel, [HBM] * 4, shape((HALF, LANES), BF16),
+        pack_kernel, [HBM] * 4, shape((SLOT, 128), BF16),
         [pltpu.SMEM((8,), I32), pltpu.SMEM((8,), I32), pltpu.SMEM((PAIRS,), I32), pltpu.VMEM((ROWS, VIRT), BF16),
          pltpu.VMEM((ROWS, 1536 + SPAN + 128), F32), pltpu.SemaphoreType.DMA((4,))],
         moved=300000, limit=64,
@@ -297,7 +310,7 @@
     blocks, order, meta, mine = call(
         blocks_kernel, [VMEM, HBM],
         (shape((HEIGHT, DEPTH), BF16), shape((PORTION, PORTION), BF16), shape((8, 128), I32),
-         shape((HALF, LANES), BF16)),
+         shape((SLOT, 128), BF16)),
         [pltpu.VMEM((8, 2 * WINDOW, VIRT), BF16), pltpu.VMEM((WINDOW, SPAN), BF16),
          pltpu.VMEM((16, 128), I32), pltpu.SemaphoreType.DMA((8,))], moved=16000000, limit=48,
     )(mine, integrals)

time: 50.6 us -> 50.2 us (level)
  no operation moved by 1% of the time
where the time goes in v7:
time: 50.2 us; the launch traced here: 50 us
  blocking collectives  16.8 us (33%)
  Pallas kernels  13.3 us (26%)
  starting transfers between devices  13.3 us (26%)
  waiting for transfers between devices  6.22 us (12%)
    all_to_all x1, blocking collectives, shards(): mine = lax.all_to_all(packed, 'z', 0, 0, tiled=True)  16.8 us
    ppermute x7, starting transfers between devices, shift(): lax.ppermute(value, axis, [(i, (i + by) % size) for i in range(size)])  13.3 us
    ppermute x7, waiting for transfers between devices, shift(): lax.ppermute(value, axis, [(i, (i + by) % size) for i in range(size)])  6.22 us
    pallas_call x1, Pallas kernels, shards(): call(blocks_kernel, [VMEM, HBM], (shape((HEIGHT, DEPTH), BF16), shape((PO...  4.61 us
    pallas_call x2, Pallas kernels, shards(): call(functools.partial(other_kernel, steps, len(terms)), [VMEM] * len(ope...  2.24 us
    pallas_call x1, Pallas kernels, shards(): call(pack_kernel, [HBM] * 4, shape((SLOT, 128), BF16), [pltpu.SMEM((8,),...  1.83 us
    pallas_call x1, Pallas kernels, shards(): call(functools.partial(own_kernel, (2, 1, 3)), [VMEM] * 2, (part,) * 3, s...  1.74 us
    pallas_call x1, Pallas kernels, shards(): call(place_kernel, [VMEM] * 7, shape((VIRT, PORTION), BF16), [pltpu.VMEM(...  1.54 us
  transfers between devices with their start and end apart: 7, of which 1 were waited for; matrix products, arithmetic and copies ran while one was open for 0% of the time, Pallas kernels for 18%

profile of v7, /device:TPU:1, one launch (start us, length us, event | category | flops | bytes accessed | tf_op | source)
XLA Modules:
  0.0 50.0 jit_solution(8242014867938257494)
XLA Ops:
  0.0 1.8 %shard_map.55 = bf16[512,128]{1,0:T(8,128)(2,1)} custom-call(s32[8]{0:T(128)} %virt_hbm.1, s32[8]{0:T(128)} %occ_hbm.1, s32[1536]{0:T(1024)} %ids_hbm.1, bf16[24,1600]{1,0:T(8,128)(2,1)} %t_hbm.1), custom_call_target="tpu_custom_call" | custom-call | bytes 300000 | tf_op jit(solution)/shard_map/pallas_call | solution.py:302
  1.8 16.8 %all_to_all.11 = bf16[8,64,128]{2,1,0:T(8,128)(2,1)S(1)} all-to-all(bf16[8,64,128]{2,1,0:T(8,128)(2,1)} %bitcast.7), channel_id=1, replica_groups=mesh['x'=4,'z'=8,'c'=2,'y'=4] {'z'}, dimensions={0} | all-to-all | bytes 262144 | tf_op jit(solution)/shard_map/all_to_all | solution.py:308
  18.6 1.2 %collective-permute-start = (bf16[512,128]{1,0:T(8,128)(2,1)S(1)}, bf16[512,128]{1,0:T(8,128)(2,1)S(1)}, u32[]{:S(2)}, u32[]{:S(2)}) collective-permute-start(bf16[512,128]{1,0:T(8,128)(2,1)S(1)} %bitcast.3), channel_id=1, source_target_pairs={{0,64},{64,128},{128,192},{192,0},{1,65},{65,129},{129,193},{193,1... | collective-permute-start | bytes 393224 | tf_op jit(solution)/shard_map/ppermute | solution.py:285
  19.8 1.5 %collective-permute-start.2 = (bf16[512,128]{1,0:T(8,128)(2,1)S(1)}, bf16[512,128]{1,0:T(8,128)(2,1)S(1)}, u32[]{:S(2)}, u32[]{:S(2)}) collective-permute-start(bf16[512,128]{1,0:T(8,128)(2,1)S(1)} %bitcast.4), channel_id=1, source_target_pairs={{0,192},{64,0},{128,64},{192,128},{1,193},{65,1},{129,65},{193,129... | collective-permute-start | bytes 393224 | tf_op jit(solution)/shard_map/ppermute | solution.py:285
  21.3 1.5 %collective-permute-start.1 = (bf16[512,128]{1,0:T(8,128)(2,1)S(1)}, bf16[512,128]{1,0:T(8,128)(2,1)S(1)}, u32[]{:S(2)}, u32[]{:S(2)}) collective-permute-start(bf16[512,128]{1,0:T(8,128)(2,1)S(1)} %bitcast.5), channel_id=1, source_target_pairs={{0,128},{64,192},{128,0},{192,64},{1,129},{65,193},{129,1},{193,65... | collective-permute-start | bytes 393224 | tf_op jit(solution)/shard_map/ppermute | solution.py:285
  22.8 4.6 %shard_map.56 = (bf16[320,2560]{1,0:T(8,128)(2,1)S(1)}, bf16[384,384]{1,0:T(8,128)(2,1)S(1)}, s32[8,128]{1,0:T(8,128)S(1)}, bf16[512,128]{1,0:T(8,128)(2,1)S(1)}) custom-call(bf16[512,128]{1,0:T(8,128)(2,1)S(1)} %bitcast.6, bf16[1600,1600]{1,0:T(8,128)(2,1)} %v_hbm.1), custom_call_target="tpu_custom_call" | custom-call | bytes 16000000 | tf_op jit(solution)/shard_map/pallas_call | solution.py:310
  27.5 0.0 collective-permute-done
  27.5 0.0 collective-permute-done.1
  27.6 0.0 collective-permute-done.2
  27.6 3.2 %collective-permute-start.3 = (bf16[2048,128]{1,0:T(8,128)(2,1)S(1)}, bf16[2048,128]{1,0:T(8,128)(2,1)S(1)}, u32[]{:S(2)}, u32[]{:S(2)}) collective-permute-start(bf16[2048,128]{1,0:T(8,128)(2,1)S(1)} %constant_dynamic-update-slice_fusion.own_ref.t_ref), channel_id=1, source_target_pairs={{0,4},{4,0},{1,5},{5,1},{2,6},{6,2},{3,7},{7,3},{8,12},{12,8},{9,1... | collective-permute-start | bytes 1572872 | tf_op jit(solution)/shard_map/ppermute | solution.py:285
  30.8 1.7 %shard_map.58 = (bf16[640,128]{1,0:T(8,128)(2,1)S(1)}, bf16[640,128]{1,0:T(8,128)(2,1)S(1)}, bf16[640,128]{1,0:T(8,128)(2,1)S(1)}) custom-call(bf16[2048,128]{1,0:T(8,128)(2,1)S(1)} %constant_dynamic-update-slice_fusion.own_ref.t_ref, bf16[320,2560]{1,0:T(8,128)(2,1)S(1)} %get-tuple-element.18.v_ref), custom_call_target="tpu_custom_call" | custom-call | flops 1258291200 | bytes 4000000 | tf_op jit(solution)/shard_map/pallas_call | solution.py:327
  32.6 0.0 collective-permute-done.3.other_ref.t_ref
  32.6 0.8 %shard_map.59.refs_0_ = bf16[960,128]{1,0:T(8,128)(2,1)S(1)} custom-call(bf16[2048,128]{1,0:T(8,128)(2,1)S(1)} %collective-permute-done.3.other_ref.t_ref, bf16[320,2560]{1,0:T(8,128)(2,1)S(1)} %get-tuple-element.18.v_ref, bf16[640,128]{1,0:T(8,128)(2,1)S(1)} %get-tuple-element.20.refs_0_), custom_call_target="tpu_custom_call" | custom-call | flops 419430400 | bytes 4000000 | tf_op jit(solution)/shard_map/pallas_call | solution.py:334
  33.4 3.2 %collective-permute-start.4 = (bf16[960,128]{1,0:T(8,128)(2,1)S(1)}, bf16[960,128]{1,0:T(8,128)(2,1)S(1)}, u32[]{:S(2)}, u32[]{:S(2)}) collective-permute-start(bf16[960,128]{1,0:T(8,128)(2,1)S(1)} %shard_map.59.refs_0_), channel_id=1, source_target_pairs={{0,2},{1,3},{2,0},{3,1},{4,6},{5,7},{6,4},{7,5},{8,10},{9,11},{10,... | collective-permute-start | bytes 737288 | tf_op jit(solution)/shard_map/ppermute | solution.py:285
  36.6 1.4 %shard_map.60 = (bf16[960,128]{1,0:T(8,128)(2,1)S(1)}, bf16[960,128]{1,0:T(8,128)(2,1)S(1)}) custom-call(bf16[2048,128]{1,0:T(8,128)(2,1)S(1)} %collective-permute-done.3.other_ref.t_ref, bf16[320,2560]{1,0:T(8,128)(2,1)S(1)} %get-tuple-element.18.v_ref, bf16[960,128]{1,0:T(8,128)(2,1)S(1)} %shard_map.59.refs_0_, ...), custom_call_target="tpu_custom_call" | custom-call | flops 838860800 | bytes 4000000 | tf_op jit(solution)/shard_map/pallas_call | solution.py:334
  38.0 0.5 collective-permute-start.5
  38.5 2.3 %collective-permute-start.6 = (bf16[960,128]{1,0:T(8,128)(2,1)S(1)}, bf16[960,128]{1,0:T(8,128)(2,1)S(1)}, u32[]{:S(2)}, u32[]{:S(2)}) collective-permute-start(bf16[960,128]{1,0:T(8,128)(2,1)S(1)} %get-tuple-element.24), channel_id=1, source_target_pairs={{0,3},{1,0},{2,1},{3,2},{4,7},{5,4},{6,5},{7,6},{8,11},{9,8},{10,9... | collective-permute-start | bytes 737288 | tf_op jit(solution)/shard_map/ppermute | solution.py:285
  40.7 1.3 %shard_map.57 = (bf16[960,128]{1,0:T(8,128)(2,1)S(1)}, bf16[16,384]{1,0:T(8,128)(2,1)S(1)}) custom-call(bf16[2048,128]{1,0:T(8,128)(2,1)S(1)} %constant_dynamic-update-slice_fusion.own_ref.t_ref, bf16[2048,128]{1,0:T(8,128)(2,1)S(1)} %collective-permute-done.3.other_ref.t_ref, bf16[320,2560]{1,0:T(8,128)(2,1)S(1)} %get-tuple-element.18.v_ref), custom_call_target="tpu_custom_call" | custom-call | flops 20000000000 | tf_op jit(solution)/shard_map/pallas_call | solution.py:339
  42.1 6.2 %collective-permute-done.5.c_ref = bf16[960,128]{1,0:T(8,128)(2,1)S(1)} collective-permute-done((bf16[960,128]{1,0:T(8,128)(2,1)S(1)}, bf16[960,128]{1,0:T(8,128)(2,1)S(1)}, u32[]{:S(2)}, u32[]{:S(2)}) %collective-permute-start.5) | collective-permute-done | bytes 245792 | tf_op jit(solution)/shard_map/ppermute | solution.py:285
  48.3 0.0 collective-permute-done.6.d_ref
  48.3 0.0 collective-permute-done.4.b_ref
  48.3 1.5 %shard_map.61 = bf16[1600,384]{1,0:T(8,128)(2,1)} custom-call(s32[8,128]{1,0:T(8,128)S(1)} %get-tuple-element.16.meta_ref, bf16[960,128]{1,0:T(8,128)(2,1)S(1)} %get-tuple-element.19.a_ref, bf16[960,128]{1,0:T(8,128)(2,1)S(1)} %collective-permute-done.4.b_ref, bf16[960,128]{1,0:T(8,128)(2,1)S(1)} %collective-permute-done.5.c_ref, ...), custom_call_target="tpu_custom_call" | custom-call | bytes 2600000 | tf_op jit(solution)/shard_map/pallas_call | solution.py:342
  (4 shorter events, 0.1 us)
Async XLA Ops:
  18.6 8.8 %collective-permute-start = (bf16[512,128]{1,0:T(8,128)(2,1)S(1)}, bf16[512,128]{1,0:T(8,128)(2,1)S(1)}, u32[]{:S(2)}, u32[]{:S(2)}) collective-permute-start(bf16[512,128]{1,0:T(8,128)(2,1)S(1)} %bitcast.3), channel_id=1, source_target_pairs={{0,64},{64,128},{128,192},{192,0},{1,65},{65,129},{129,193},{193,1... | collective-permute-start | bytes 393224 | tf_op jit(solution)/shard_map/ppermute | solution.py:285
  19.8 7.7 %collective-permute-start.2 = (bf16[512,128]{1,0:T(8,128)(2,1)S(1)}, bf16[512,128]{1,0:T(8,128)(2,1)S(1)}, u32[]{:S(2)}, u32[]{:S(2)}) collective-permute-start(bf16[512,128]{1,0:T(8,128)(2,1)S(1)} %bitcast.4), channel_id=1, source_target_pairs={{0,192},{64,0},{128,64},{192,128},{1,193},{65,1},{129,65},{193,129... | collective-permute-start | bytes 393224 | tf_op jit(solution)/shard_map/ppermute | solution.py:285
  21.3 6.2 %collective-permute-start.1 = (bf16[512,128]{1,0:T(8,128)(2,1)S(1)}, bf16[512,128]{1,0:T(8,128)(2,1)S(1)}, u32[]{:S(2)}, u32[]{:S(2)}) collective-permute-start(bf16[512,128]{1,0:T(8,128)(2,1)S(1)} %bitcast.5), channel_id=1, source_target_pairs={{0,128},{64,192},{128,0},{192,64},{1,129},{65,193},{129,1},{193,65... | collective-permute-start | bytes 393224 | tf_op jit(solution)/shard_map/ppermute | solution.py:285
  27.6 5.0 %collective-permute-start.3 = (bf16[2048,128]{1,0:T(8,128)(2,1)S(1)}, bf16[2048,128]{1,0:T(8,128)(2,1)S(1)}, u32[]{:S(2)}, u32[]{:S(2)}) collective-permute-start(bf16[2048,128]{1,0:T(8,128)(2,1)S(1)} %constant_dynamic-update-slice_fusion.own_ref.t_ref), channel_id=1, source_target_pairs={{0,4},{4,0},{1,5},{5,1},{2,6},{6,2},{3,7},{7,3},{8,12},{12,8},{9,1... | collective-permute-start | bytes 1572872 | tf_op jit(solution)/shard_map/ppermute | solution.py:285
  33.4 14.9 %collective-permute-start.4 = (bf16[960,128]{1,0:T(8,128)(2,1)S(1)}, bf16[960,128]{1,0:T(8,128)(2,1)S(1)}, u32[]{:S(2)}, u32[]{:S(2)}) collective-permute-start(bf16[960,128]{1,0:T(8,128)(2,1)S(1)} %shard_map.59.refs_0_), channel_id=1, source_target_pairs={{0,2},{1,3},{2,0},{3,1},{4,6},{5,7},{6,4},{7,5},{8,10},{9,11},{10,... | collective-permute-start | bytes 737288 | tf_op jit(solution)/shard_map/ppermute | solution.py:285
  38.0 10.3 %collective-permute-start.5 = (bf16[960,128]{1,0:T(8,128)(2,1)S(1)}, bf16[960,128]{1,0:T(8,128)(2,1)S(1)}, u32[]{:S(2)}, u32[]{:S(2)}) collective-permute-start(bf16[960,128]{1,0:T(8,128)(2,1)S(1)} %get-tuple-element.23), channel_id=1, source_target_pairs={{0,1},{1,2},{2,3},{3,0},{4,5},{5,6},{6,7},{7,4},{8,9},{9,10},{10,1... | collective-permute-start | bytes 737288 | tf_op jit(solution)/shard_map/ppermute | solution.py:285
  38.5 9.8 %collective-permute-start.6 = (bf16[960,128]{1,0:T(8,128)(2,1)S(1)}, bf16[960,128]{1,0:T(8,128)(2,1)S(1)}, u32[]{:S(2)}, u32[]{:S(2)}) collective-permute-start(bf16[960,128]{1,0:T(8,128)(2,1)S(1)} %get-tuple-element.24), channel_id=1, source_target_pairs={{0,3},{1,0},{2,1},{3,2},{4,7},{5,4},{6,5},{7,6},{8,11},{9,8},{10,9... | collective-permute-start | bytes 737288 | tf_op jit(solution)/shard_map/ppermute | solution.py:285

commit v8 on v7

--- a/solution.py
+++ b/solution.py
@@ -129,12 +129,18 @@
     starts = [block_start(offset) for offset in offsets]
     skips = [offset - start for offset, start in zip(offsets, starts)]
     firsts = [pl.multiple_of(jnp.minimum(start, VIRT - WINDOW), 16) for start in starts]
-    copies = [
-        pltpu.make_async_copy(v_hbm.at[pl.ds(firsts[s], WINDOW), :], windows.at[s, pl.ds(0, WINDOW), :], sems.at[s])
-        for s in range(8)
-    ]
-    for copy in copies:
-        copy.start()
+    spans = [offset_of(virt, jnp.bitwise_xor(hc, s)) for s in range(8)]
+
+    def fetch(s, whole):
+        lanes, place = pl.ds(pl.multiple_of(lax.div(spans[s], 128) * 128, 128), SPAN), pl.ds(0, SPAN)
+        if whole:
+            lanes = place = slice(None)
+        source = v_hbm.at[pl.ds(firsts[s], WINDOW), lanes]
+        return pltpu.make_async_copy(source, windows.at[s, pl.ds(0, WINDOW), place], sems.at[s])
+
+    for s in range(8):
+        pl.when(spans[s] < LAST)(lambda: fetch(s, False).start())
+        pl.when(spans[s] >= LAST)(lambda: fetch(s, True).start())
     copy_ref[...] = mine_ref[...]
     row, lane = lax.broadcasted_iota(I32, (8, 128), 0), lax.broadcasted_iota(I32, (8, 128), 1)
     meta = jnp.zeros((8, 128), I32)
@@ -155,7 +161,7 @@
     row = lax.broadcasted_iota(I32, (WINDOW, LANES), 0)
     for s in range(8):
         group = jnp.bitwise_xor(hc, s)
-        offset, size = offset_of(virt, group), size_of(virt, group)
+        offset, size = spans[s], size_of(virt, group)
         rows = pl.ds(pl.multiple_of(starts[s] - firsts[s], 16), WINDOW)
         keep = (lane < size) & (row < VIRT - starts[s])
 
@@ -170,15 +176,14 @@
                 tail = out_ref[:, place].astype(F32) + pltpu.roll(tail, TAIL, 1)
             out_ref[:, place] = tail.astype(BF16)
 
-        copies[s].wait()
-
         @pl.when(offset < LAST)
         def _():
-            start = pl.multiple_of(lax.div(offset, 128) * 128, 128)
-            emit(windows[s, rows, pl.ds(start, SPAN)], lax.rem(SPAN - lax.rem(offset, 128), SPAN))
+            fetch(s, False).wait()
+            emit(windows[s, rows, :SPAN], lax.rem(SPAN - lax.rem(offset, 128), SPAN))
 
         @pl.when(offset >= LAST)
         def _():
+            fetch(s, True).wait()
             span[:, :384] = windows[s, rows, LAST:1536]
             span[:, 384:448] = windows[s, rows, 1536:1600]
             span[:, 448:] = jnp.zeros((WINDOW, 64), BF16)

time: 50.2 us -> 50.2 us (level)
  transfers between devices with their start and end apart: 7 -> 7, of which waited for: 1 -> 2; matrix products, arithmetic and copies ran while one was open for 0% -> 0% of each run, Pallas kernels for 18% -> 18%
where the time goes in v8:
time: 50.2 us; the launch traced here: 49.9 us
  blocking collectives  16.8 us (33%)
  starting transfers between devices  13.5 us (27%)
  Pallas kernels  13 us (26%)
  waiting for transfers between devices  6.34 us (13%)
    all_to_all x1, blocking collectives, shards(): mine = lax.all_to_all(packed, 'z', 0, 0, tiled=True)  16.8 us
    ppermute x7, starting transfers between devices, shift(): lax.ppermute(value, axis, [(i, (i + by) % size) for i in range(size)])  13.5 us
    ppermute x7, waiting for transfers between devices, shift(): lax.ppermute(value, axis, [(i, (i + by) % size) for i in range(size)])  6.34 us
    pallas_call x1, Pallas kernels, shards(): call(blocks_kernel, [VMEM, HBM], (shape((HEIGHT, DEPTH), BF16), shape((PO...  4.28 us
    pallas_call x2, Pallas kernels, shards(): call(functools.partial(other_kernel, steps, len(terms)), [VMEM] * len(ope...  2.23 us
    pallas_call x1, Pallas kernels, shards(): call(pack_kernel, [HBM] * 4, shape((SLOT, 128), BF16), [pltpu.SMEM((8,),...  1.83 us
    pallas_call x1, Pallas kernels, shards(): call(functools.partial(own_kernel, (2, 1, 3)), [VMEM] * 2, (part,) * 3, s...  1.74 us
    pallas_call x1, Pallas kernels, shards(): call(place_kernel, [VMEM] * 7, shape((VIRT, PORTION), BF16), [pltpu.VMEM(...  1.55 us
  transfers between devices with their start and end apart: 7, of which 2 were waited for; matrix products, arithmetic and copies ran while one was open for 0% of the time, Pallas kernels for 18%

profile of v8, /device:TPU:1, one launch (start us, length us, event | category | flops | bytes accessed | tf_op | source)
XLA Modules:
  0.0 49.9 jit_solution(4307275019582157843)
XLA Ops:
  0.0 1.8 %shard_map.55 = bf16[512,128]{1,0:T(8,128)(2,1)} custom-call(s32[8]{0:T(128)} %virt_hbm.1, s32[8]{0:T(128)} %occ_hbm.1, s32[1536]{0:T(1024)} %ids_hbm.1, bf16[24,1600]{1,0:T(8,128)(2,1)} %t_hbm.1), custom_call_target="tpu_custom_call" | custom-call | bytes 300000 | tf_op jit(solution)/shard_map/pallas_call | solution.py:307
  1.8 16.8 %all_to_all.11 = bf16[8,64,128]{2,1,0:T(8,128)(2,1)S(1)} all-to-all(bf16[8,64,128]{2,1,0:T(8,128)(2,1)} %bitcast.7), channel_id=1, replica_groups=mesh['x'=4,'z'=8,'c'=2,'y'=4] {'z'}, dimensions={0} | all-to-all | bytes 262144 | tf_op jit(solution)/shard_map/all_to_all | solution.py:313
  18.6 1.2 %collective-permute-start = (bf16[512,128]{1,0:T(8,128)(2,1)S(1)}, bf16[512,128]{1,0:T(8,128)(2,1)S(1)}, u32[]{:S(2)}, u32[]{:S(2)}) collective-permute-start(bf16[512,128]{1,0:T(8,128)(2,1)S(1)} %bitcast.3), channel_id=1, source_target_pairs={{0,64},{64,128},{128,192},{192,0},{1,65},{65,129},{129,193},{193,1... | collective-permute-start | bytes 393224 | tf_op jit(solution)/shard_map/ppermute | solution.py:290
  19.8 1.5 %collective-permute-start.2 = (bf16[512,128]{1,0:T(8,128)(2,1)S(1)}, bf16[512,128]{1,0:T(8,128)(2,1)S(1)}, u32[]{:S(2)}, u32[]{:S(2)}) collective-permute-start(bf16[512,128]{1,0:T(8,128)(2,1)S(1)} %bitcast.4), channel_id=1, source_target_pairs={{0,192},{64,0},{128,64},{192,128},{1,193},{65,1},{129,65},{193,129... | collective-permute-start | bytes 393224 | tf_op jit(solution)/shard_map/ppermute | solution.py:290
  21.3 1.5 %collective-permute-start.1 = (bf16[512,128]{1,0:T(8,128)(2,1)S(1)}, bf16[512,128]{1,0:T(8,128)(2,1)S(1)}, u32[]{:S(2)}, u32[]{:S(2)}) collective-permute-start(bf16[512,128]{1,0:T(8,128)(2,1)S(1)} %bitcast.5), channel_id=1, source_target_pairs={{0,128},{64,192},{128,0},{192,64},{1,129},{65,193},{129,1},{193,65... | collective-permute-start | bytes 393224 | tf_op jit(solution)/shard_map/ppermute | solution.py:290
  22.8 4.3 %shard_map.56 = (bf16[320,2560]{1,0:T(8,128)(2,1)S(1)}, bf16[384,384]{1,0:T(8,128)(2,1)S(1)}, s32[8,128]{1,0:T(8,128)S(1)}, bf16[512,128]{1,0:T(8,128)(2,1)S(1)}) custom-call(bf16[512,128]{1,0:T(8,128)(2,1)S(1)} %bitcast.6, bf16[1600,1600]{1,0:T(8,128)(2,1)} %v_hbm.1), custom_call_target="tpu_custom_call" | custom-call | bytes 16000000 | tf_op jit(solution)/shard_map/pallas_call | solution.py:315
  27.2 0.0 collective-permute-done
  27.2 0.1 collective-permute-done.1
  27.3 0.0 collective-permute-done.2
  27.4 3.4 %collective-permute-start.3 = (bf16[2048,128]{1,0:T(8,128)(2,1)S(1)}, bf16[2048,128]{1,0:T(8,128)(2,1)S(1)}, u32[]{:S(2)}, u32[]{:S(2)}) collective-permute-start(bf16[2048,128]{1,0:T(8,128)(2,1)S(1)} %constant_dynamic-update-slice_fusion.own_ref.t_ref), channel_id=1, source_target_pairs={{0,4},{4,0},{1,5},{5,1},{2,6},{6,2},{3,7},{7,3},{8,12},{12,8},{9,1... | collective-permute-start | bytes 1572872 | tf_op jit(solution)/shard_map/ppermute | solution.py:290
  30.8 1.7 %shard_map.58 = (bf16[640,128]{1,0:T(8,128)(2,1)S(1)}, bf16[640,128]{1,0:T(8,128)(2,1)S(1)}, bf16[640,128]{1,0:T(8,128)(2,1)S(1)}) custom-call(bf16[2048,128]{1,0:T(8,128)(2,1)S(1)} %constant_dynamic-update-slice_fusion.own_ref.t_ref, bf16[320,2560]{1,0:T(8,128)(2,1)S(1)} %get-tuple-element.18.v_ref), custom_call_target="tpu_custom_call" | custom-call | flops 1258291200 | bytes 4000000 | tf_op jit(solution)/shard_map/pallas_call | solution.py:332
  32.5 0.0 collective-permute-done.3.other_ref.t_ref
  32.5 0.8 %shard_map.59.refs_0_ = bf16[960,128]{1,0:T(8,128)(2,1)S(1)} custom-call(bf16[2048,128]{1,0:T(8,128)(2,1)S(1)} %collective-permute-done.3.other_ref.t_ref, bf16[320,2560]{1,0:T(8,128)(2,1)S(1)} %get-tuple-element.18.v_ref, bf16[640,128]{1,0:T(8,128)(2,1)S(1)} %get-tuple-element.20.refs_0_), custom_call_target="tpu_custom_call" | custom-call | flops 419430400 | bytes 4000000 | tf_op jit(solution)/shard_map/pallas_call | solution.py:339
  33.4 3.2 %collective-permute-start.4 = (bf16[960,128]{1,0:T(8,128)(2,1)S(1)}, bf16[960,128]{1,0:T(8,128)(2,1)S(1)}, u32[]{:S(2)}, u32[]{:S(2)}) collective-permute-start(bf16[960,128]{1,0:T(8,128)(2,1)S(1)} %shard_map.59.refs_0_), channel_id=1, source_target_pairs={{0,2},{1,3},{2,0},{3,1},{4,6},{5,7},{6,4},{7,5},{8,10},{9,11},{10,... | collective-permute-start | bytes 737288 | tf_op jit(solution)/shard_map/ppermute | solution.py:290
  36.6 1.4 %shard_map.60 = (bf16[960,128]{1,0:T(8,128)(2,1)S(1)}, bf16[960,128]{1,0:T(8,128)(2,1)S(1)}) custom-call(bf16[2048,128]{1,0:T(8,128)(2,1)S(1)} %collective-permute-done.3.other_ref.t_ref, bf16[320,2560]{1,0:T(8,128)(2,1)S(1)} %get-tuple-element.18.v_ref, bf16[960,128]{1,0:T(8,128)(2,1)S(1)} %shard_map.59.refs_0_, ...), custom_call_target="tpu_custom_call" | custom-call | flops 838860800 | bytes 4000000 | tf_op jit(solution)/shard_map/pallas_call | solution.py:339
  38.0 0.5 collective-permute-start.5
  38.4 2.3 %collective-permute-start.6 = (bf16[960,128]{1,0:T(8,128)(2,1)S(1)}, bf16[960,128]{1,0:T(8,128)(2,1)S(1)}, u32[]{:S(2)}, u32[]{:S(2)}) collective-permute-start(bf16[960,128]{1,0:T(8,128)(2,1)S(1)} %get-tuple-element.24), channel_id=1, source_target_pairs={{0,3},{1,0},{2,1},{3,2},{4,7},{5,4},{6,5},{7,6},{8,11},{9,8},{10,9... | collective-permute-start | bytes 737288 | tf_op jit(solution)/shard_map/ppermute | solution.py:290
  40.7 1.3 %shard_map.57 = (bf16[960,128]{1,0:T(8,128)(2,1)S(1)}, bf16[16,384]{1,0:T(8,128)(2,1)S(1)}) custom-call(bf16[2048,128]{1,0:T(8,128)(2,1)S(1)} %constant_dynamic-update-slice_fusion.own_ref.t_ref, bf16[2048,128]{1,0:T(8,128)(2,1)S(1)} %collective-permute-done.3.other_ref.t_ref, bf16[320,2560]{1,0:T(8,128)(2,1)S(1)} %get-tuple-element.18.v_ref), custom_call_target="tpu_custom_call" | custom-call | flops 20000000000 | tf_op jit(solution)/shard_map/pallas_call | solution.py:344
  42.0 6.2 %collective-permute-done.5.c_ref = bf16[960,128]{1,0:T(8,128)(2,1)S(1)} collective-permute-done((bf16[960,128]{1,0:T(8,128)(2,1)S(1)}, bf16[960,128]{1,0:T(8,128)(2,1)S(1)}, u32[]{:S(2)}, u32[]{:S(2)}) %collective-permute-start.5) | collective-permute-done | bytes 245792 | tf_op jit(solution)/shard_map/ppermute | solution.py:290
  48.2 0.0 collective-permute-done.6.d_ref
  48.2 0.0 collective-permute-done.4.b_ref
  48.2 1.5 %shard_map.61 = bf16[1600,384]{1,0:T(8,128)(2,1)} custom-call(s32[8,128]{1,0:T(8,128)S(1)} %get-tuple-element.16.meta_ref, bf16[960,128]{1,0:T(8,128)(2,1)S(1)} %get-tuple-element.19.a_ref, bf16[960,128]{1,0:T(8,128)(2,1)S(1)} %collective-permute-done.4.b_ref, bf16[960,128]{1,0:T(8,128)(2,1)S(1)} %collective-permute-done.5.c_ref, ...), custom_call_target="tpu_custom_call" | custom-call | bytes 2600000 | tf_op jit(solution)/shard_map/pallas_call | solution.py:347
  (4 shorter events, 0.1 us)
Async XLA Ops:
  18.6 8.5 %collective-permute-start = (bf16[512,128]{1,0:T(8,128)(2,1)S(1)}, bf16[512,128]{1,0:T(8,128)(2,1)S(1)}, u32[]{:S(2)}, u32[]{:S(2)}) collective-permute-start(bf16[512,128]{1,0:T(8,128)(2,1)S(1)} %bitcast.3), channel_id=1, source_target_pairs={{0,64},{64,128},{128,192},{192,0},{1,65},{65,129},{129,193},{193,1... | collective-permute-start | bytes 393224 | tf_op jit(solution)/shard_map/ppermute | solution.py:290
  19.8 7.5 %collective-permute-start.2 = (bf16[512,128]{1,0:T(8,128)(2,1)S(1)}, bf16[512,128]{1,0:T(8,128)(2,1)S(1)}, u32[]{:S(2)}, u32[]{:S(2)}) collective-permute-start(bf16[512,128]{1,0:T(8,128)(2,1)S(1)} %bitcast.4), channel_id=1, source_target_pairs={{0,192},{64,0},{128,64},{192,128},{1,193},{65,1},{129,65},{193,129... | collective-permute-start | bytes 393224 | tf_op jit(solution)/shard_map/ppermute | solution.py:290
  21.3 6.0 %collective-permute-start.1 = (bf16[512,128]{1,0:T(8,128)(2,1)S(1)}, bf16[512,128]{1,0:T(8,128)(2,1)S(1)}, u32[]{:S(2)}, u32[]{:S(2)}) collective-permute-start(bf16[512,128]{1,0:T(8,128)(2,1)S(1)} %bitcast.5), channel_id=1, source_target_pairs={{0,128},{64,192},{128,0},{192,64},{1,129},{65,193},{129,1},{193,65... | collective-permute-start | bytes 393224 | tf_op jit(solution)/shard_map/ppermute | solution.py:290
  27.4 5.1 %collective-permute-start.3 = (bf16[2048,128]{1,0:T(8,128)(2,1)S(1)}, bf16[2048,128]{1,0:T(8,128)(2,1)S(1)}, u32[]{:S(2)}, u32[]{:S(2)}) collective-permute-start(bf16[2048,128]{1,0:T(8,128)(2,1)S(1)} %constant_dynamic-update-slice_fusion.own_ref.t_ref), channel_id=1, source_target_pairs={{0,4},{4,0},{1,5},{5,1},{2,6},{6,2},{3,7},{7,3},{8,12},{12,8},{9,1... | collective-permute-start | bytes 1572872 | tf_op jit(solution)/shard_map/ppermute | solution.py:290
  33.4 14.9 %collective-permute-start.4 = (bf16[960,128]{1,0:T(8,128)(2,1)S(1)}, bf16[960,128]{1,0:T(8,128)(2,1)S(1)}, u32[]{:S(2)}, u32[]{:S(2)}) collective-permute-start(bf16[960,128]{1,0:T(8,128)(2,1)S(1)} %shard_map.59.refs_0_), channel_id=1, source_target_pairs={{0,2},{1,3},{2,0},{3,1},{4,6},{5,7},{6,4},{7,5},{8,10},{9,11},{10,... | collective-permute-start | bytes 737288 | tf_op jit(solution)/shard_map/ppermute | solution.py:290
  38.0 10.3 %collective-permute-start.5 = (bf16[960,128]{1,0:T(8,128)(2,1)S(1)}, bf16[960,128]{1,0:T(8,128)(2,1)S(1)}, u32[]{:S(2)}, u32[]{:S(2)}) collective-permute-start(bf16[960,128]{1,0:T(8,128)(2,1)S(1)} %get-tuple-element.23), channel_id=1, source_target_pairs={{0,1},{1,2},{2,3},{3,0},{4,5},{5,6},{6,7},{7,4},{8,9},{9,10},{10,1... | collective-permute-start | bytes 737288 | tf_op jit(solution)/shard_map/ppermute | solution.py:290
  38.4 9.8 %collective-permute-start.6 = (bf16[960,128]{1,0:T(8,128)(2,1)S(1)}, bf16[960,128]{1,0:T(8,128)(2,1)S(1)}, u32[]{:S(2)}, u32[]{:S(2)}) collective-permute-start(bf16[960,128]{1,0:T(8,128)(2,1)S(1)} %get-tuple-element.24), channel_id=1, source_target_pairs={{0,3},{1,0},{2,1},{3,2},{4,7},{5,4},{6,5},{7,6},{8,11},{9,8},{10,9... | collective-permute-start | bytes 737288 | tf_op jit(solution)/shard_map/ppermute | solution.py:290
